TPU v7x, 128 devices: a whole 4x4x4 slice. The times are simulated.
128 devices in a mesh: rows: 16 (over y_lo, x, core), cols: 8 (over z, y_hi).
Axes of the slice: x: 4, y: 4 (y_hi: 2, y_lo: 2; y = y_hi * 2 + y_lo), z: 4, core: 2. Of those that a mesh axis runs over, the one named last changes fastest.
Arguments:
- image: bfloat16 [256, 512, 384], P('rows', 'cols'), may hold values from -14 to 14
- mb_expand: bfloat16 [384, 1536], replicated, may hold values from -0.3125 to 0.3125
- mb_taps: bfloat16 [9, 1536], replicated, may hold values from -3.5 to 3.5
- mb_reduce: bfloat16 [1536, 96], replicated, may hold values from -2.5 to 2.5
- mb_restore: bfloat16 [96, 1536], replicated, may hold values from -3.5 to 3.5
- mb_project: bfloat16 [1536, 384], replicated, may hold values from -0.15625 to 0.15625
- block_qkv: bfloat16 [384, 1152], replicated, may hold values from -2 to 2
- block_out: bfloat16 [384, 384], replicated, may hold values from -0.3125 to 0.3125
- first_up: bfloat16 [384, 1536], replicated, may hold values from -0.3125 to 0.3125
- first_down: bfloat16 [1536, 384], replicated, may hold values from -0.15625 to 0.15625
- grid_qkv: bfloat16 [384, 1152], replicated, may hold values from -2 to 2
- grid_out: bfloat16 [384, 384], replicated, may hold values from -0.3125 to 0.3125
- second_up: bfloat16 [384, 1536], replicated, may hold values from -0.3125 to 0.3125
- second_down: bfloat16 [1536, 384], replicated, may hold values from -0.15625 to 0.15625
- down_expand: bfloat16 [384, 1536], replicated, may hold values from -0.3125 to 0.3125
- down_taps: bfloat16 [9, 1536], replicated, may hold values from -3.5 to 3.5
- down_reduce: bfloat16 [1536, 96], replicated, may hold values from -2.5 to 2.5
- down_restore: bfloat16 [96, 1536], replicated, may hold values from -3.5 to 3.5
- down_project: bfloat16 [1536, 768], replicated, may hold values from -0.15625 to 0.15625
- down_shortcut: bfloat16 [384, 768], replicated, may hold values from -0.15625 to 0.15625
Outputs:
- section_out: bfloat16 [256, 512, 384], P('rows', 'cols')
- downsampled: bfloat16 [128, 256, 768], P('rows', 'cols')
All inputs are finite; a program needn't handle non-finite values.
Results may differ from a plain program's by a relative error of at most 0.014.
Values may be sent and summed in bfloat16 or wider, within the bound.
No kernel may reach another device: no remote copies, remote signals or barrier semaphores. Data moves between devices by JAX's collectives and lax.ppermute only.
A program may use at most 128 MiB of HBM per device.

v0:
```python
import math

import jax
import jax.numpy as jnp
from jax import lax
from jax.sharding import PartitionSpec as P

HEADS = 12
WIN = 8


epsilon = 1e-05


def padded_2(x, sides, width):
    for axis, dim in sides:
        size, length = (lax.axis_size(axis), x.shape[dim])
        up = [(i, (i + 1) % size) for i in range(size - 1)]
        down = [(j, i) for i, j in up]
        last = lax.slice_in_dim(x, length - width, length, axis=dim)
        first = lax.slice_in_dim(x, 0, width, axis=dim)
        before = lax.ppermute(last, axis, up)
        after = lax.ppermute(first, axis, down)
        x = jnp.concatenate([before, x, after], axis=dim)
    return x


def from_behind(x, axis, by):
    length = lax.axis_size(axis)
    pairs = [(i, i + by) for i in range(length) if 0 <= i + by < length]
    return lax.ppermute(x, axis, pairs)


def layer_norm(values):
    values = values.astype(jnp.float32)
    average = jnp.mean(values, axis=-1, keepdims=True)
    centred = values - average
    spread = jnp.mean(centred * centred, axis=-1, keepdims=True)
    return centred * lax.rsqrt(spread + epsilon)


def expand_cells(cells_in, weight):
    channels = cells_in.shape[-1]
    normed = layer_norm(cells_in.reshape(-1, channels)).astype(jnp.bfloat16)
    hidden = jax.nn.gelu(
        jnp.dot(normed, weight, preferred_element_type=jnp.float32), approximate=True
    )
    return hidden.astype(jnp.bfloat16).reshape(cells_in.shape[:-1] + (weight.shape[1],))


def depthwise(padded, kernel, out_rows, out_cols, stride):
    summed = jnp.zeros((out_rows, out_cols, padded.shape[-1]), jnp.float32)
    for row_tap in range(3):
        for col_tap in range(3):
            window = padded[
                row_tap : row_tap + stride * (out_rows - 1) + 1 : stride,
                col_tap : col_tap + stride * (out_cols - 1) + 1 : stride,
            ]
            summed = summed + window.astype(jnp.float32) * kernel[3 * row_tap + col_tap].astype(
                jnp.float32
            )
    return jax.nn.gelu(summed, approximate=True)


def excite(channel_sums, cell_count, shrink_weight, expand_weight):
    average = (channel_sums / cell_count)[None, :]
    squeezed = jax.nn.silu(
        jnp.dot(average, shrink_weight.astype(jnp.float32), precision=lax.Precision.HIGHEST)
    )
    return jax.nn.sigmoid(
        jnp.dot(squeezed, expand_weight.astype(jnp.float32), precision=lax.Precision.HIGHEST)
    )[0]


def attend(groups, qkv_weight, out_weight, head_count):
    group_count, group_size, channels = groups.shape
    head_width = channels // head_count
    normed = layer_norm(groups.reshape(-1, channels)).astype(jnp.bfloat16)
    projected = jnp.dot(normed, qkv_weight, preferred_element_type=jnp.float32).astype(jnp.bfloat16)
    projected = projected.reshape(group_count, group_size, 3, head_count, head_width)
    queries = projected[:, :, 0]
    key_rows = projected[:, :, 1]
    value_rows = projected[:, :, 2]
    scores = jnp.einsum(
        "gqhd,gkhd->ghqk", queries, key_rows, preferred_element_type=jnp.float32
    ) / math.sqrt(head_width)
    row_max = jnp.max(scores, axis=-1, keepdims=True)
    weights = jnp.exp(scores - row_max)
    shares = (weights / jnp.sum(weights, axis=-1, keepdims=True)).astype(jnp.bfloat16)
    blended = jnp.einsum(
        "ghqk,gkhd->gqhd", shares, value_rows, preferred_element_type=jnp.float32
    ).astype(jnp.bfloat16)
    blended = blended.reshape(-1, channels)
    result = groups.reshape(-1, channels).astype(jnp.float32) + jnp.dot(
        blended, out_weight, preferred_element_type=jnp.float32
    )
    return result.astype(jnp.bfloat16).reshape(groups.shape)


def feed_cells(cells_in, up_weight, down_weight):
    channels = cells_in.shape[-1]
    rows_flat = cells_in.reshape(-1, channels)
    normed = layer_norm(rows_flat).astype(jnp.bfloat16)
    hidden = jax.nn.gelu(
        jnp.dot(normed, up_weight, preferred_element_type=jnp.float32), approximate=True
    ).astype(jnp.bfloat16)
    result = rows_flat.astype(jnp.float32) + jnp.dot(
        hidden, down_weight, preferred_element_type=jnp.float32
    )
    return result.astype(jnp.bfloat16).reshape(cells_in.shape)


def into_groups(cells_in, row_count, col_count):
    tile_rows, tile_cols, channels = cells_in.shape
    pieces = cells_in.reshape(
        tile_rows // row_count, row_count, tile_cols // col_count, col_count, channels
    )
    pieces = pieces.transpose(0, 2, 1, 3, 4).reshape(
        tile_rows // row_count, tile_cols // col_count, row_count * col_count, channels
    )
    arrived = lax.all_to_all(pieces, ("rows", "cols"), split_axis=2, concat_axis=2, tiled=True)
    arrived = arrived.reshape(
        tile_rows // row_count, tile_cols // col_count, row_count, col_count, channels
    )
    return arrived.transpose(2, 0, 3, 1, 4).reshape(tile_rows, tile_cols, channels)


def from_groups(cells_in, row_count, col_count):
    tile_rows, tile_cols, channels = cells_in.shape
    pieces = cells_in.reshape(
        row_count, tile_rows // row_count, col_count, tile_cols // col_count, channels
    )
    pieces = pieces.transpose(1, 3, 0, 2, 4).reshape(
        tile_rows // row_count, tile_cols // col_count, row_count * col_count, channels
    )
    arrived = lax.all_to_all(pieces, ("rows", "cols"), split_axis=2, concat_axis=2, tiled=True)
    arrived = arrived.reshape(
        tile_rows // row_count, tile_cols // col_count, row_count, col_count, channels
    )
    return arrived.transpose(0, 2, 1, 3, 4).reshape(tile_rows, tile_cols, channels)


def local(
    image,
    mb_expand,
    mb_taps,
    mb_reduce,
    mb_restore,
    mb_project,
    block_qkv,
    block_out,
    first_up,
    first_down,
    grid_qkv,
    grid_out,
    second_up,
    second_down,
    down_expand,
    down_taps,
    down_reduce,
    down_restore,
    down_project,
    down_shortcut,
):
    rows_here, cols_here, channels = image.shape
    row_count = lax.axis_size("rows")
    col_count = lax.axis_size("cols")
    all_cells = rows_here * cols_here * row_count * col_count
    hidden = expand_cells(image, mb_expand)
    padded = padded_2(hidden, (("rows", 0), ("cols", 1)), 1)
    activated = depthwise(padded, mb_taps, rows_here, cols_here, 1)
    conv_sums = lax.psum(jnp.sum(activated, axis=(0, 1)), ("rows", "cols"))
    gate_vec = excite(conv_sums, all_cells, mb_reduce, mb_restore)
    excited = (activated * gate_vec).astype(jnp.bfloat16).reshape(-1, activated.shape[-1])
    after_conv = image.reshape(-1, channels).astype(jnp.float32) + jnp.dot(
        excited, mb_project, preferred_element_type=jnp.float32
    )
    after_conv = after_conv.astype(jnp.bfloat16).reshape(rows_here, cols_here, channels)
    blocks = after_conv.reshape(rows_here // WIN, WIN, cols_here // WIN, WIN, channels).transpose(
        0, 2, 1, 3, 4
    )
    blocks = attend(blocks.reshape(-1, WIN * WIN, channels), block_qkv, block_out, HEADS)
    block_mixed = blocks.reshape(rows_here // WIN, cols_here // WIN, WIN, WIN, channels).transpose(
        0, 2, 1, 3, 4
    )
    first_mixed = feed_cells(
        block_mixed.reshape(rows_here, cols_here, channels), first_up, first_down
    )
    grouped = into_groups(first_mixed, row_count, col_count)
    grid_sets = grouped.reshape(WIN, rows_here // WIN, WIN, cols_here // WIN, channels).transpose(
        1, 3, 0, 2, 4
    )
    grid_sets = attend(grid_sets.reshape(-1, WIN * WIN, channels), grid_qkv, grid_out, HEADS)
    grid_mixed = grid_sets.reshape(
        rows_here // WIN, cols_here // WIN, WIN, WIN, channels
    ).transpose(2, 0, 3, 1, 4)
    grid_mixed = grid_mixed.reshape(rows_here, cols_here, channels)
    section_out = feed_cells(from_groups(grid_mixed, row_count, col_count), second_up, second_down)
    upper_rim = from_behind(section_out[rows_here - 1 :], "rows", 1)
    extended = jnp.concatenate([upper_rim, section_out], axis=0)
    left_rim = from_behind(extended[:, cols_here - 1 :], "cols", 1)
    framed = jnp.concatenate([left_rim, extended], axis=1)
    down_hidden = expand_cells(framed, down_expand)
    down_act = depthwise(down_hidden, down_taps, rows_here // 2, cols_here // 2, 2)
    down_sums = lax.psum(jnp.sum(down_act, axis=(0, 1)), ("rows", "cols"))
    down_gate = excite(down_sums, all_cells // 4, down_reduce, down_restore)
    down_scaled = (down_act * down_gate).astype(jnp.bfloat16).reshape(-1, down_act.shape[-1])
    pooled = jnp.mean(
        section_out.astype(jnp.float32).reshape(rows_here // 2, 2, cols_here // 2, 2, channels),
        axis=(1, 3),
    )
    pooled = pooled.astype(jnp.bfloat16).reshape(-1, channels)
    branch = jnp.dot(down_scaled, down_project, preferred_element_type=jnp.float32)
    shortcut = jnp.dot(pooled, down_shortcut, preferred_element_type=jnp.float32)
    downsampled = (
        (branch + shortcut)
        .astype(jnp.bfloat16)
        .reshape(rows_here // 2, cols_here // 2, down_project.shape[1])
    )
    return (section_out, downsampled)


def solution(mesh):
    in_specs = (
        P("rows", "cols", None),
        P(),
        P(),
        P(),
        P(),
        P(),
        P(),
        P(),
        P(),
        P(),
        P(),
        P(),
        P(),
        P(),
        P(),
        P(),
        P(),
        P(),
        P(),
        P(),
    )
    out_specs = (P("rows", "cols", None), P("rows", "cols", None))
    return jax.shard_map(local, mesh=mesh, in_specs=in_specs, out_specs=out_specs, check_vma=False)
```

profile of v0, /device:TPU:1, one launch (start us, length us, event | category | flops | bytes accessed | tf_op | source)
XLA Modules:
  0.0 472.6 jit_solution(2250442716261454927)
XLA Ops:
  0.7 1.5 convert_reduce_fusion
  2.2 1.6 fusion.77
  4.2 4.2 fusion.17
  8.5 4.5 collective-permute-start
  13.0 1.9 collective-permute-start.1
  15.6 4.4 collective-permute-done.1
  20.2 4.8 %collective-permute-start.2 = (bf16[18,1,1536]{2,1,0:T(2,128)(2,1)S(1)}, bf16[18,1,1536]{2,1,0:T(2,128)(2,1)S(1)}, u32[]{:S(2)}, u32[]{:S(2)}) collective-permute-start(bf16[18,1,1536]{2,1,0:T(2,128)(2,1)S(1)} %get-tuple-element.32), channel_id=1, source_target_pairs={{0,1},{1,2},{2,3},{3,4},{4,5},{5,6},{6,7},{8,9},{9,10},{10,11},{11... | collective-permute-start | bytes 165896 | tf_op jit(solution)/shard_map/ppermute | solution.py:22
  26.7 5.3 %collective-permute-done.3 = bf16[18,1,1536]{2,1,0:T(2,128)(2,1)S(1)} collective-permute-done((bf16[18,1,1536]{2,1,0:T(2,128)(2,1)S(1)}, bf16[18,1,1536]{2,1,0:T(2,128)(2,1)S(1)}, u32[]{:S(2)}, u32[]{:S(2)}) %collective-permute-start.3) | collective-permute-done | bytes 55328 | tf_op jit(solution)/shard_map/ppermute | solution.py:23
  32.0 2.2 maximum_maximum_fusion
  34.2 10.5 %fusion.112 = (f32[1536]{0:T(1024)S(1)}, f32[16,64,1536]{2,1,0:T(8,128)}) fusion(f32[1536]{0:T(1024)S(1)} %get-tuple-element.18, bf16[18,65,1536]{2,1,0:T(8,128)(2,1)S(1)} %get-tuple-element.31, f32[1536]{0:T(1024)S(1)} %get-tuple-element.19, bf16[1,64,1536]{2,1,0:T(8,128)(2,1)S(1)} %collective-permute-done.1, bf16[16,64,1536]{2,1,0:T(8,128)(2,1)S(1)} %bitcast.200, ...), kind=kLoop, calls=%fused_computation.205 | loop fusion | flops 58194432 | bytes 28766208 | tf_op jit(solution)/shard_map/reduce_sum | solution.py:172
  44.6 68.0 %psum.14 = f32[1536]{0:T(1024)S(1)} all-reduce(f32[1536]{0:T(1024)S(1)} %get-tuple-element.22), channel_id=1, replica_groups=mesh['rows'=16,'cols'=8] {'rows','cols'}, use_global_device_ids=true, to_apply=%region_3.0 | all-reduce | flops 1536 | bytes 12288 | tf_op jit(solution)/shard_map/psum | solution.py:172
  114.2 3.7 multiply_convert_fusion
  118.0 1.8 fusion.80
  121.9 2.8 copy.89
  124.8 1.8 fusion.74
  126.6 2.9 convolution_convert_fusion.1
  129.5 4.3 copy.92
  133.8 7.3 %reshape.447 = bf16[16,64,3,12,32]{1,0,4,3,2:T(8,128)(2,1)} reshape(bf16[1024,1152]{0,1:T(8,128)(2,1)} %copy.92) | data formatting | bytes 4718592 | tf_op jit(solution)/shard_map/reshape | solution.py:80
  141.0 3.2 fusion.115
  144.2 1.4 fusion.63
  145.6 9.3 %fusion.116 = (f32[16,12,64]{2,1,0:T(8,128)S(1)}, f32[16,12,64,64]{2,3,1,0:T(8,128)S(1)}) fusion(f32[16,12,64,64]{2,3,1,0:T(8,128)S(1)} %fusion.63), kind=kOutput, calls=%fused_computation.208 | output fusion | flops 3145791 | bytes 6340608 | tf_op jit(solution)/shard_map/sub | solution.py:88
  156.1 2.2 copy.97
  158.3 2.7 reshape.448
  161.1 2.1 fusion.75
  165.4 2.7 copy.98
  168.2 2.6 fusion.71
  170.8 5.9 %fusion.72 = bf16[1024,384]{1,0:T(8,128)(2,1)S(1)} fusion(f32[2,8,8,8,384]{4,3,2,1,0:T(8,128)} %copy.98, bf16[1536,384]{1,0:T(8,128)(2,1)} %param.29, bf16[1024,384]{1,0:T(8,128)(2,1)} %fusion.71, bf16[384,1536]{1,0:T(8,128)(2,1)} %param.28), kind=kOutput, calls=%fused_computation.103 | convolution fusion | flops 2430861312 | bytes 5505024 | tf_op jit(solution)/shard_map/dot_general | solution.py:107
  177.2 20.6 %all_to_all.10 = bf16[1,8,128,384]{3,1,0,2:T(8,128)(2,1)S(1)} all-to-all(bf16[1,8,128,384]{3,1,0,2:T(8,128)(2,1)S(1)} %copy.102), channel_id=1, replica_groups=mesh['rows'=16,'cols'=8] {'rows','cols'}, dimensions={2} | all-to-all | bytes 1572864 | tf_op jit(solution)/shard_map/all_to_all | solution.py:121
  199.2 1.5 copy.103
  200.7 1.6 reduce_sum.161
  202.5 1.9 multiply_reduce_fusion.4
  204.7 1.7 fusion.68
  206.5 2.9 convolution_convert_fusion
  209.4 4.3 copy.109
  213.6 7.3 %reshape.451 = bf16[16,64,3,12,32]{1,0,4,3,2:T(8,128)(2,1)} reshape(bf16[1024,1152]{0,1:T(8,128)(2,1)} %copy.109) | data formatting | bytes 4718592 | tf_op jit(solution)/shard_map/reshape | solution.py:80
  220.9 3.2 fusion.114
  225.5 9.2 %fusion.117 = (f32[16,12,64]{2,1,0:T(8,128)S(1)}, f32[16,12,64,64]{2,3,1,0:T(8,128)S(1)}) fusion(f32[16,12,64,64]{2,3,1,0:T(8,128)S(1)} %fusion.62), kind=kOutput, calls=%fused_computation.209 | output fusion | flops 3145791 | bytes 6340608 | tf_op jit(solution)/shard_map/sub | solution.py:88
  235.8 2.2 copy.114
  238.0 2.7 reshape.452
  240.8 2.1 fusion.69
  243.4 20.7 %all_to_all.11 = bf16[1,8,128,384]{3,1,0,2:T(8,128)(2,1)S(1)} all-to-all(bf16[1,8,128,384]{3,1,0,2:T(8,128)(2,1)S(1)} %bitcast.214), channel_id=1, replica_groups=mesh['rows'=16,'cols'=8] {'rows','cols'}, dimensions={2} | all-to-all | bytes 1572864 | tf_op jit(solution)/shard_map/all_to_all | solution.py:136
  266.8 2.6 fusion.65
  269.4 5.9 %fusion.66 = bf16[1024,384]{1,0:T(8,128)(2,1)S(1)} fusion(f32[1,16,8,8,384]{4,3,2,1,0:T(8,128)} %copy.118, bf16[1536,384]{1,0:T(8,128)(2,1)} %param.33, bf16[1024,384]{1,0:T(8,128)(2,1)} %fusion.65, bf16[384,1536]{1,0:T(8,128)(2,1)} %param.32), kind=kOutput, calls=%fused_computation.92 | convolution fusion | flops 2430861312 | bytes 5505024 | tf_op jit(solution)/shard_map/dot_general | solution.py:107
  276.0 3.5 collective-permute-start.4
  280.3 1.9 reshape.482
  282.2 2.6 reduce_sum.169
  285.5 3.3 collective-permute-start.5
  291.6 1.6 multiply_reduce_fusion.2
  293.3 2.3 maximum_convert_fusion
  295.6 3.1 reshape.472
  298.6 6.5 %fusion.9 = bf16[1105,1536]{1,0:T(8,128)(2,1)} fusion(bf16[384,1536]{1,0:T(8,128)(2,1)} %param.34, f32[1105,384]{1,0:T(8,128)} %reshape.472, f32[1105]{0:T(1024)S(1)} %rsqrt.77, f32[1105]{0:T(1024)S(1)} %div.131), kind=kOutput, calls=%fused_computation.14 | convolution fusion | flops 1320059520 | bytes 6280328 | tf_op jit(solution)/shard_map/dot_general | solution.py:46
  305.1 3.8 reshape.455
  309.0 8.1 %slice.190 = bf16[8,32,1536]{2,1,0:T(8,128)(2,1)S(1)} slice(bf16[17,65,1536]{2,1,0:T(8,128)(2,1)} %reshape.455), slice={[0:15:2], [0:63:2], [0:1536:1]} | slice | bytes 1572864 | tf_op jit(solution)/shard_map/slice | solution.py:55
  317.1 9.6 %slice.192 = bf16[8,32,1536]{2,1,0:T(8,128)(2,1)} slice(bf16[17,65,1536]{2,1,0:T(8,128)(2,1)} %reshape.455), slice={[0:15:2], [1:64:2], [0:1536:1]} | slice | bytes 1572864 | tf_op jit(solution)/shard_map/slice | solution.py:55
  326.7 9.9 %slice.194 = bf16[8,32,1536]{2,1,0:T(8,128)(2,1)} slice(bf16[17,65,1536]{2,1,0:T(8,128)(2,1)} %reshape.455), slice={[0:15:2], [2:65:2], [0:1536:1]} | slice | bytes 1572864 | tf_op jit(solution)/shard_map/slice | solution.py:55
  336.6 9.6 %slice.196 = bf16[8,32,1536]{2,1,0:T(8,128)(2,1)} slice(bf16[17,65,1536]{2,1,0:T(8,128)(2,1)} %reshape.455), slice={[1:16:2], [0:63:2], [0:1536:1]} | slice | bytes 1572864 | tf_op jit(solution)/shard_map/slice | solution.py:55
  346.2 9.6 %slice.198 = bf16[8,32,1536]{2,1,0:T(8,128)(2,1)} slice(bf16[17,65,1536]{2,1,0:T(8,128)(2,1)} %reshape.455), slice={[1:16:2], [1:64:2], [0:1536:1]} | slice | bytes 1572864 | tf_op jit(solution)/shard_map/slice | solution.py:55
  355.8 9.9 %slice.200 = bf16[8,32,1536]{2,1,0:T(8,128)(2,1)} slice(bf16[17,65,1536]{2,1,0:T(8,128)(2,1)} %reshape.455), slice={[1:16:2], [2:65:2], [0:1536:1]} | slice | bytes 1572864 | tf_op jit(solution)/shard_map/slice | solution.py:55
  365.7 9.6 %slice.202 = bf16[8,32,1536]{2,1,0:T(8,128)(2,1)} slice(bf16[17,65,1536]{2,1,0:T(8,128)(2,1)} %reshape.455), slice={[2:17:2], [0:63:2], [0:1536:1]} | slice | bytes 1572864 | tf_op jit(solution)/shard_map/slice | solution.py:55
  375.3 9.6 %slice.204 = bf16[8,32,1536]{2,1,0:T(8,128)(2,1)} slice(bf16[17,65,1536]{2,1,0:T(8,128)(2,1)} %reshape.455), slice={[2:17:2], [1:64:2], [0:1536:1]} | slice | bytes 1572864 | tf_op jit(solution)/shard_map/slice | solution.py:55
  384.9 9.8 %slice.206 = bf16[8,32,1536]{2,1,0:T(8,128)(2,1)} slice(bf16[17,65,1536]{2,1,0:T(8,128)(2,1)} %reshape.455), slice={[2:17:2], [2:65:2], [0:1536:1]} | slice | bytes 1572864 | tf_op jit(solution)/shard_map/slice | solution.py:55
  394.8 5.8 %fusion.110 = (f32[1536]{0:T(1024)S(1)}, f32[8,32,1536]{2,1,0:T(8,128)}) fusion(f32[1536]{0:T(1024)S(1)} %copy-done.18, bf16[8,32,1536]{2,1,0:T(8,128)(2,1)} %slice.206, f32[1536]{0:T(1024)S(1)} %copy-done.19, bf16[8,32,1536]{2,1,0:T(8,128)(2,1)} %slice.204, f32[1536]{0:T(1024)S(1)} %get-tuple-element.3, bf16[8,32,1536]{2,1,0:T(8,128)(2,1)} %slice.202, ...), kind=kLoop, calls=%fused_computation.204 | loop fusion | flops 13761024 | bytes 8712192 | tf_op jit(solution)/shard_map/reduce_sum | solution.py:205
  400.7 66.3 %psum.15 = f32[1536]{0:T(1024)S(1)} all-reduce(f32[1536]{0:T(1024)S(1)} %get-tuple-element.20), channel_id=1, replica_groups=mesh['rows'=16,'cols'=8] {'rows','cols'}, use_global_device_ids=true, to_apply=%region_19.20 | all-reduce | flops 1536 | bytes 12288 | tf_op jit(solution)/shard_map/psum | solution.py:205
  468.5 1.5 multiply_convert_fusion.2
  (127 shorter events, 27.3 us)
Async XLA Ops:
  0.6 469.4 %copy-start = (bf16[1536,768]{1,0:T(8,128)(2,1)S(1)}, bf16[1536,768]{1,0:T(8,128)(2,1)}, u32[]{:S(2)}) copy-start(bf16[1536,768]{1,0:T(8,128)(2,1)} %param.38) | copy-start | bytes 7077892
  0.6 3.2 copy-start.3
  8.5 7.1 %collective-permute-start = (bf16[1,64,1536]{2,1,0:T(8,128)(2,1)S(1)}, bf16[1,64,1536]{2,1,0:T(8,128)(2,1)S(1)}, u32[]{:S(2)}, u32[]{:S(2)}) collective-permute-start(bf16[1,64,1536]{2,1,0:T(8,128)(2,1)S(1)} %get-tuple-element.34), channel_id=1, source_target_pairs={{0,8},{8,16},{16,24},{24,32},{32,40},{40,48},{48,56},{56,64},{64,7... | collective-permute-start | bytes 589832 | tf_op jit(solution)/shard_map/ppermute | solution.py:22
  13.0 7.0 %collective-permute-start.1 = (bf16[1,64,1536]{2,1,0:T(8,128)(2,1)S(1)}, bf16[1,64,1536]{2,1,0:T(8,128)(2,1)S(1)}, u32[]{:S(2)}, u32[]{:S(2)}) collective-permute-start(bf16[1,64,1536]{2,1,0:T(8,128)(2,1)S(1)} %get-tuple-element.35), channel_id=1, source_target_pairs={{8,0},{16,8},{24,16},{32,24},{40,32},{48,40},{56,48},{64,56},{72,6... | collective-permute-start | bytes 589832 | tf_op jit(solution)/shard_map/ppermute | solution.py:23
  20.0 6.3 %copy-start.11 = (bf16[9,1536]{1,0:T(8,128)(2,1)S(1)}, bf16[9,1536]{1,0:T(8,128)(2,1)}, u32[]{:S(2)}) copy-start(bf16[9,1536]{1,0:T(8,128)(2,1)} %param.22) | copy-start | bytes 82948
  20.2 6.6 %collective-permute-start.2 = (bf16[18,1,1536]{2,1,0:T(2,128)(2,1)S(1)}, bf16[18,1,1536]{2,1,0:T(2,128)(2,1)S(1)}, u32[]{:S(2)}, u32[]{:S(2)}) collective-permute-start(bf16[18,1,1536]{2,1,0:T(2,128)(2,1)S(1)} %get-tuple-element.32), channel_id=1, source_target_pairs={{0,1},{1,2},{2,3},{3,4},{4,5},{5,6},{6,7},{8,9},{9,10},{10,11},{11... | collective-permute-start | bytes 165896 | tf_op jit(solution)/shard_map/ppermute | solution.py:22
  25.0 7.0 %collective-permute-start.3 = (bf16[18,1,1536]{2,1,0:T(2,128)(2,1)S(1)}, bf16[18,1,1536]{2,1,0:T(2,128)(2,1)S(1)}, u32[]{:S(2)}, u32[]{:S(2)}) collective-permute-start(bf16[18,1,1536]{2,1,0:T(2,128)(2,1)S(1)} %get-tuple-element.33), channel_id=1, source_target_pairs={{1,0},{2,1},{3,2},{4,3},{5,4},{6,5},{7,6},{9,8},{10,9},{11,10},{12... | collective-permute-start | bytes 165896 | tf_op jit(solution)/shard_map/ppermute | solution.py:23
  34.2 79.8 %copy-start.6 = (bf16[96,1536]{1,0:T(8,128)(2,1)S(1)}, bf16[96,1536]{1,0:T(8,128)(2,1)}, u32[]{:S(2)}) copy-start(bf16[96,1536]{1,0:T(8,128)(2,1)} %param.24) | copy-start | bytes 884740
  114.2 3.7 copy-start.20
  124.7 1.9 copy-start.21
  158.3 2.8 copy-start.8
  198.0 1.2 copy-start.1
  202.5 4.0 copy-start.22
  238.0 2.8 copy-start.9
  269.4 10.1 %copy-start.12 = (bf16[9,1536]{1,0:T(8,128)(2,1)S(1)}, bf16[9,1536]{1,0:T(8,128)(2,1)}, u32[]{:S(2)}) copy-start(bf16[9,1536]{1,0:T(8,128)(2,1)} %param.35) | copy-start | bytes 82948
  275.3 18.0 %copy-start.2 = (bf16[1024,384]{1,0:T(8,128)(2,1)}, bf16[1024,384]{1,0:T(8,128)(2,1)S(1)}, u32[]{:S(2)}) copy-start(bf16[1024,384]{1,0:T(8,128)(2,1)S(1)} %fusion.66) | copy-start | bytes 2359300
  276.0 8.8 %collective-permute-start.4 = (bf16[1,64,384]{2,1,0:T(8,128)(2,1)}, bf16[1,64,384]{2,1,0:T(8,128)(2,1)}, u32[]{:S(2)}, u32[]{:S(2)}) collective-permute-start(bf16[1,64,384]{2,1,0:T(8,128)(2,1)} %slice_bitcast_fusion.2), channel_id=1, source_target_pairs={{0,8},{8,16},{16,24},{24,32},{32,40},{40,48},{48,56},{56,64},{64,7... | collective-permute-start | bytes 147464 | tf_op jit(solution)/shard_map/ppermute | solution.py:31
  285.5 4.2 collective-permute-start.5
  289.7 0.6 copy-start.10
  375.3 19.5 %copy-start.13 = (f32[1536]{0:T(1024)S(1)}, f32[1536]{0:T(1024)}, u32[]{:S(2)}) copy-start(f32[1536]{0:T(1024)} %get-tuple-element.4) | copy-start | bytes 18436
  375.3 19.5 %copy-start.14 = (f32[1536]{0:T(1024)S(1)}, f32[1536]{0:T(1024)}, u32[]{:S(2)}) copy-start(f32[1536]{0:T(1024)} %get-tuple-element.5) | copy-start | bytes 18436
  375.3 19.5 %copy-start.15 = (f32[1536]{0:T(1024)S(1)}, f32[1536]{0:T(1024)}, u32[]{:S(2)}) copy-start(f32[1536]{0:T(1024)} %get-tuple-element.6) | copy-start | bytes 18436
  375.3 19.5 %copy-start.16 = (f32[1536]{0:T(1024)S(1)}, f32[1536]{0:T(1024)}, u32[]{:S(2)}) copy-start(f32[1536]{0:T(1024)} %get-tuple-element.7) | copy-start | bytes 18436
  375.3 19.5 %copy-start.17 = (f32[1536]{0:T(1024)S(1)}, f32[1536]{0:T(1024)}, u32[]{:S(2)}) copy-start(f32[1536]{0:T(1024)} %get-tuple-element.8) | copy-start | bytes 18436
  375.3 19.5 %copy-start.18 = (f32[1536]{0:T(1024)S(1)}, f32[1536]{0:T(1024)}, u32[]{:S(2)}) copy-start(f32[1536]{0:T(1024)} %get-tuple-element.9) | copy-start | bytes 18436
  375.3 19.5 %copy-start.19 = (f32[1536]{0:T(1024)S(1)}, f32[1536]{0:T(1024)}, u32[]{:S(2)}) copy-start(f32[1536]{0:T(1024)} %get-tuple-element.10) | copy-start | bytes 18436
  394.8 73.4 %copy-start.7 = (bf16[96,1536]{1,0:T(8,128)(2,1)S(1)}, bf16[96,1536]{1,0:T(8,128)(2,1)}, u32[]{:S(2)}) copy-start(bf16[96,1536]{1,0:T(8,128)(2,1)} %param.37) | copy-start | bytes 884740
  470.1 0.9 copy-start.4
  470.1 1.2 copy-start.5
where the time goes:
time: 480 us; the launch traced here: 473 us
  blocking collectives  176 us (37%)
  local copies, waits for them, and re-layouts  148 us (31%)
  other arithmetic  73.1 us (15%)
  matrix products  44.2 us (9%)
  starting transfers between devices  19.3 us (4%)
  waiting for transfers between devices  10.8 us (2%)
    slice x9, local copies, waits for them, and re-layouts, depthwise(): padded[row_tap:row_tap + stride * (out_rows - 1) + 1:stride, col_tap:col_...  85.7 us
    psum x1, blocking collectives, local(): conv_sums = lax.psum(jnp.sum(activated, axis=(0, 1)), ('rows', 'cols'))  68 us
    psum x1, blocking collectives, local(): down_sums = lax.psum(jnp.sum(down_act, axis=(0, 1)), ('rows', 'cols'))  66.3 us
    all_to_all x1, blocking collectives, from_groups(): lax.all_to_all(pieces, ('rows', 'cols'), split_axis=2, concat_axis=2, til...  20.7 us
    all_to_all x1, blocking collectives, into_groups(): lax.all_to_all(pieces, ('rows', 'cols'), split_axis=2, concat_axis=2, til...  20.6 us
    sub x2, other arithmetic, attend(): weights = jnp.exp(scores - row_max)  18.5 us
    reshape x2, local copies, waits for them, and re-layouts, attend(): projected.reshape(group_count, group_size, 3, head_count, head_width)  14.5 us
    dot_general x2, matrix products, feed_cells(): jnp.dot(hidden, down_weight, preferred_element_type=jnp.float32)  11.7 us
  transfers between devices with their start and end apart: 6, of which 5 were waited for; matrix products, arithmetic and copies ran while one was open for 1% of the time, Pallas kernels for 0%

commit v1 on v0

v1 whole, which is shorter than its diff:
```python
import math

import jax
import jax.numpy as jnp
import numpy as np
from jax import lax
from jax.experimental import pallas as pl
from jax.experimental.pallas import tpu as pltpu
from jax.sharding import Mesh
from jax.sharding import PartitionSpec as P

HEADS = 12
WIN = 8
CELLS = WIN * WIN
QUAD = 4

epsilon = 1e-05
F32 = jnp.float32
BF16 = jnp.bfloat16
ROWS = ("row_pair", "core")
ALL = ("row_pair", "core", "cols")
CLASS = ("row_pair", "cols")


def params(megabytes=48):
    return pltpu.CompilerParams(vmem_limit_bytes=megabytes << 20)


def cost(flops, moved):
    return pl.CostEstimate(flops=int(flops), bytes_accessed=int(moved), transcendentals=0)


def gelu(x):
    half = 0.5 * x
    inner = x * (0.7978845608028654 + 0.035677408136300125 * (x * x))
    return half + half * jnp.tanh(inner)


def layer_norm(x):
    average = jnp.mean(x, axis=-1, keepdims=True)
    centred = x - average
    spread = jnp.mean(centred * centred, axis=-1, keepdims=True)
    return centred * lax.rsqrt(spread + epsilon)


def dot(a, b):
    return jnp.dot(a, b, preferred_element_type=F32)


def panels(rows, channels):
    return pltpu.VMEM((channels // 128, rows, 128), F32)


def put(ref, x):
    for c in range(ref.shape[0]):
        ref[c] = x[:, c * 128 : (c + 1) * 128]


def put_strided(ref, x, start, count, stride):
    for c in range(ref.shape[0]):
        ref[c, pl.ds(start, count, stride=stride), :] = x[:, c * 128 : (c + 1) * 128]


def take(ref):
    return jnp.concatenate([ref[c] for c in range(ref.shape[0])], 1)


def take_strided(ref, start, count, stride):
    return jnp.concatenate(
        [ref[c, pl.ds(start, count, stride=stride), :] for c in range(ref.shape[0])], 1
    )


def expand_kernel(x_ref, w_ref, out_ref):
    normed = layer_norm(x_ref[...].astype(F32)).astype(BF16)
    for c in range(0, w_ref.shape[1], 512):
        out_ref[:, c : c + 512] = gelu(dot(normed, w_ref[:, c : c + 512])).astype(BF16)


def expand(x, weight, block=256):
    cells, channels = x.shape
    hidden = weight.shape[1]
    return pl.pallas_call(
        expand_kernel,
        grid=(cells // block,),
        in_specs=[
            pl.BlockSpec((block, channels), lambda i: (i, 0)),
            pl.BlockSpec((channels, hidden), lambda i: (0, 0)),
        ],
        out_specs=pl.BlockSpec((block, hidden), lambda i: (i, 0)),
        out_shape=jax.ShapeDtypeStruct((cells, hidden), BF16),
        compiler_params=params(),
        cost_estimate=cost(2 * cells * channels * hidden, 2 * cells * (channels + hidden)),
        name="expand",
    )(x, weight)


def conv_kernel(
    hid_ref, top_ref, bot_ref, left_ref, right_ref, w_ref, taps_ref, red_ref,
    act_ref, part_ref, normed, left, right, part,
):
    step = pl.program_id(0)
    rows, cols, chunk = hid_ref.shape

    @pl.when(step == 0)
    def _():
        for ref, start in ((top_ref, 0), (bot_ref, 80), (left_ref, 160), (right_ref, 176)):
            size = ref.shape[0]
            normed[start : start + size, :] = layer_norm(ref[...].astype(F32)).astype(BF16)
        part[...] = jnp.zeros_like(part)

    rim = gelu(dot(normed[...], w_ref[...])).astype(BF16).astype(F32)
    left[0:1, :] = rim[64:65]
    left[1:17, :] = rim[160:176]
    left[17:18, :] = rim[144:145]
    right[0:1, :] = rim[65:66]
    right[1:17, :] = rim[176:192]
    right[17:18, :] = rim[145:146]
    place = lax.broadcasted_iota(jnp.int32, (8, 128), 0)
    sums = []
    for lane in range(0, chunk, 128):
        lanes = slice(lane, lane + 128)
        taps = [taps_ref[t : t + 1, lanes].astype(F32) for t in range(9)]
        before = sum(taps[3 * a] * left[a : a + rows, lanes] for a in range(3))
        after = sum(taps[3 * a + 2] * right[a : a + rows, lanes] for a in range(3))
        total = jnp.zeros((8, 128), F32)

        def line(r):
            if r < 0:
                return rim[0:64, lanes]
            if r == rows:
                return rim[80:144, lanes]
            return hid_ref[r, :, lanes].astype(F32)

        window = [line(-1), line(0), None]
        for r in range(rows):
            window[2] = line(r + 1)
            one = [
                taps[b] * window[0] + taps[3 + b] * window[1] + taps[6 + b] * window[2]
                for b in range(3)
            ]
            down = pltpu.roll(one[0], 1, 0)
            up = pltpu.roll(one[2], cols - 1, 0)
            first = jnp.where(place == 0, before[r : r + 1], down[0:8])
            last = jnp.where(place == 7, after[r : r + 1], up[cols - 8 :])
            whole = (
                one[1]
                + jnp.concatenate([first, down[8:]], 0)
                + jnp.concatenate([up[: cols - 8], last], 0)
            )
            act = gelu(whole)
            act_ref[r, :, lanes] = act.astype(BF16)
            for s in range(0, cols, 8):
                total = total + act[s : s + 8]
            window = [window[1], window[2], None]
        sums.append(total)
    part[...] += jnp.dot(
        jnp.concatenate(sums, 1),
        red_ref[...].astype(F32),
        precision=lax.Precision.HIGHEST,
        preferred_element_type=F32,
    )

    @pl.when(step == pl.num_programs(0) - 1)
    def _():
        whole = jnp.sum(part[...], axis=0, keepdims=True)
        part_ref[...] = jnp.broadcast_to(whole, part_ref.shape)


def conv(hidden, top, bottom, left, right, weight, taps, reduce, copies, chunk=256):
    rows, cols, width = hidden.shape
    channels = weight.shape[0]
    squeezed = reduce.shape[1]
    whole = lambda a: pl.BlockSpec(a.shape, lambda c: (0, 0))
    return pl.pallas_call(
        conv_kernel,
        grid=(width // chunk,),
        in_specs=[
            pl.BlockSpec((rows, cols, chunk), lambda c: (0, 0, c)),
            whole(top),
            whole(bottom),
            whole(left),
            whole(right),
            pl.BlockSpec((channels, chunk), lambda c: (0, c)),
            pl.BlockSpec((9, chunk), lambda c: (0, c)),
            pl.BlockSpec((chunk, squeezed), lambda c: (c, 0)),
        ],
        out_specs=[
            pl.BlockSpec((rows, cols, chunk), lambda c: (0, 0, c)),
            pl.BlockSpec((copies, squeezed), lambda c: (0, 0)),
        ],
        out_shape=[
            jax.ShapeDtypeStruct((rows, cols, width), BF16),
            jax.ShapeDtypeStruct((copies, squeezed), F32),
        ],
        scratch_shapes=[
            pltpu.VMEM((192, channels), BF16),
            pltpu.VMEM((24, chunk), F32),
            pltpu.VMEM((24, chunk), F32),
            pltpu.VMEM((8, squeezed), F32),
        ],
        compiler_params=params(),
        name="conv",
    )(hidden, top, bottom, left, right, weight, taps, reduce)


def gate_of(parts_ref, restore_ref, cell_count):
    average = jnp.sum(parts_ref[...], axis=0, keepdims=True) / cell_count
    squeezed = average * jax.nn.sigmoid(average)
    squeezed = jnp.broadcast_to(squeezed, (8, squeezed.shape[1]))
    wide = jnp.dot(
        squeezed,
        restore_ref[...].astype(F32),
        precision=lax.Precision.HIGHEST,
        preferred_element_type=F32,
    )
    return jax.nn.sigmoid(wide)


def mix(x, qkv_ref, out_ref, up_ref, down_ref):
    cells, channels = x.shape
    width = channels // HEADS
    normed = layer_norm(x).astype(BF16)
    projected = dot(normed, qkv_ref[...])
    queries = (projected[:, :channels] * (1.0 / math.sqrt(width))).astype(BF16)
    keys = projected[:, channels : 2 * channels].astype(BF16)
    values = projected[:, 2 * channels :].astype(BF16)
    lane = lax.broadcasted_iota(jnp.int32, (1, 128), 1)
    masks = [((lane >= h * width) & (lane < (h + 1) * width)).astype(BF16) for h in range(QUAD)]
    groups = []
    for g in range(0, cells, CELLS):
        mine = slice(g, g + CELLS)
        quads = []
        for c in range(0, channels, 128):
            lanes = slice(c, c + 128)
            q, k, v = queries[mine, lanes], keys[mine, lanes], values[mine, lanes]
            stacked = jnp.concatenate([q * m for m in masks], 0)
            scores = lax.dot_general(
                k, stacked, (((1,), (1,)), ((), ())), preferred_element_type=F32
            )
            weights = jnp.exp(scores - jnp.max(scores, axis=0, keepdims=True))
            shares = weights * (1.0 / jnp.sum(weights, axis=0, keepdims=True))
            blended = lax.dot_general(
                shares.astype(BF16), v, (((0,), (0,)), ((), ())), preferred_element_type=F32
            )
            picked = blended[3 * CELLS :]
            for h in (2, 1, 0):
                picked = jnp.where(
                    lane < (h + 1) * width, blended[h * CELLS : (h + 1) * CELLS], picked
                )
            quads.append(picked)
        groups.append(jnp.concatenate(quads, 1).astype(BF16))
    x = x + dot(jnp.concatenate(groups, 0), out_ref[...])
    normed = layer_norm(x).astype(BF16)
    for c in range(0, up_ref.shape[1], 512):
        hidden = gelu(dot(normed, up_ref[:, c : c + 512])).astype(BF16)
        x = x + dot(hidden, down_ref[c : c + 512, :])
    return x


def block_kernel(
    img_ref, act_ref, parts_ref, restore_ref, project_ref, qkv_ref, out_ref, up_ref, down_ref,
    res_ref, gate, *, cell_count,
):
    @pl.when(pl.program_id(0) == 0)
    def _():
        gate[...] = gate_of(parts_ref, restore_ref, cell_count)

    rows, cols, channels = img_ref.shape
    scaled = act_ref[...].reshape(rows * cols, act_ref.shape[2]).astype(F32) * gate[0:1, :]
    x = img_ref[...].reshape(rows * cols, channels).astype(F32)
    x = x + dot(scaled.astype(BF16), project_ref[...])
    wide = cols // WIN
    pieces = [
        x[r * cols + g * WIN : r * cols + (g + 1) * WIN] for g in range(wide) for r in range(rows)
    ]
    y = mix(jnp.concatenate(pieces, 0), qkv_ref, out_ref, up_ref, down_ref)
    pieces = [
        y[g * CELLS + r * WIN : g * CELLS + (r + 1) * WIN] for r in range(rows) for g in range(wide)
    ]
    res_ref[...] = jnp.concatenate(pieces, 0).astype(BF16).reshape(rows, cols, channels)


def block_part(image, act, parts, restore, project, qkv, out, up, down, cell_count, wide=32):
    rows, cols, channels = image.shape
    hidden = act.shape[2]
    across = cols // wide
    place = lambda i: (i // across, i % across, 0)
    whole = lambda a: pl.BlockSpec(a.shape, lambda i: (0, 0))
    weights = (restore, project, qkv, out, up, down)

    def kernel(*refs):
        block_kernel(*refs, cell_count=cell_count)

    return pl.pallas_call(
        kernel,
        grid=((rows // WIN) * across,),
        in_specs=[
            pl.BlockSpec((WIN, wide, channels), place),
            pl.BlockSpec((WIN, wide, hidden), place),
            whole(parts),
            *[whole(w) for w in weights],
        ],
        out_specs=pl.BlockSpec((WIN, wide, channels), place),
        out_shape=jax.ShapeDtypeStruct(image.shape, BF16),
        scratch_shapes=[pltpu.VMEM((8, hidden), F32)],
        compiler_params=params(),
        name="block_part",
    )(image, act, parts, *weights)


def grid_kernel(x_ref, qkv_ref, out_ref, up_ref, down_ref, res_ref, before, after, *, groups):
    step = pl.program_id(0)
    members, held, channels = x_ref.shape

    @pl.when(step == 0)
    def _():
        put(before, x_ref[...].reshape(members * held, channels).astype(F32))

    x = jnp.concatenate(
        [take_strided(before, step * groups + g, members, held) for g in range(groups)], 0
    )
    y = mix(x, qkv_ref, out_ref, up_ref, down_ref)
    for g in range(groups):
        mine = y[g * CELLS : (g + 1) * CELLS]
        put_strided(after, mine, step * groups + g, members, held)

    @pl.when(step == pl.num_programs(0) - 1)
    def _():
        res_ref[...] = take(after).astype(BF16).reshape(members, held, channels)


def grid_part(x, qkv, out, up, down, groups=4):
    members, held, channels = x.shape
    weights = (qkv, out, up, down)

    def kernel(*refs):
        grid_kernel(*refs, groups=groups)

    return pl.pallas_call(
        kernel,
        grid=(held // groups,),
        in_specs=[
            pl.BlockSpec(x.shape, lambda i: (0, 0, 0)),
            *[pl.BlockSpec(w.shape, lambda i: (0, 0)) for w in weights],
        ],
        out_specs=pl.BlockSpec(x.shape, lambda i: (0, 0, 0)),
        out_shape=jax.ShapeDtypeStruct(x.shape, BF16),
        scratch_shapes=[
            panels(members * held, channels),
            panels(members * held, channels),
        ],
        compiler_params=params(),
        name="grid_part",
    )(x, *weights)


def down_expand_kernel(x_ref, w_ref, out_ref, cells):
    rows, cols, channels = x_ref.shape
    put(cells, x_ref[...].reshape(rows * cols, channels).astype(F32))
    half = rows * cols // 2
    x = jnp.concatenate([take_strided(cells, parity, half, 2) for parity in range(2)], 0)
    normed = layer_norm(x).astype(BF16)
    for c in range(0, w_ref.shape[1], 512):
        hidden = gelu(dot(normed, w_ref[:, c : c + 512])).astype(BF16)
        for parity in range(2):
            out_ref[:, parity, :, c : c + 512] = hidden[parity * half : (parity + 1) * half].reshape(
                rows, cols // 2, 512
            )


def down_expand_part(x, weight, block=4):
    rows, cols, channels = x.shape
    hidden = weight.shape[1]
    return pl.pallas_call(
        down_expand_kernel,
        grid=(rows // block,),
        in_specs=[
            pl.BlockSpec((block, cols, channels), lambda i: (i, 0, 0)),
            pl.BlockSpec((channels, hidden), lambda i: (0, 0)),
        ],
        out_specs=pl.BlockSpec((block, 2, cols // 2, hidden), lambda i: (i, 0, 0, 0)),
        out_shape=jax.ShapeDtypeStruct((rows, 2, cols // 2, hidden), BF16),
        scratch_shapes=[panels(block * cols, channels)],
        compiler_params=params(),
        cost_estimate=cost(2 * rows * cols * channels * hidden, 2 * rows * cols * hidden),
        name="down_expand",
    )(x, weight)


def down_conv_kernel(
    hid_ref, upper_ref, left_ref, corner_ref, w_ref, taps_ref, red_ref,
    act_ref, part_ref, cells, normed, left, part,
):
    step = pl.program_id(0)
    rows, _, cols, chunk = hid_ref.shape

    @pl.when(step == 0)
    def _():
        put(cells, layer_norm(upper_ref[...].astype(F32)))
        normed[0:32, :] = take_strided(cells, 0, 32, 2).astype(BF16)
        normed[32:64, :] = take_strided(cells, 1, 32, 2).astype(BF16)
        normed[64:80, :] = layer_norm(left_ref[...].astype(F32)).astype(BF16)
        corner = layer_norm(corner_ref[...].astype(F32))
        normed[80:96, :] = jnp.broadcast_to(corner, (16, corner.shape[1])).astype(BF16)
        part[...] = jnp.zeros_like(part)

    rim = gelu(dot(normed[...], w_ref[...])).astype(BF16).astype(F32)
    left[0:1, :] = rim[80:81]
    left[1:17, :] = rim[64:80]
    place = lax.broadcasted_iota(jnp.int32, (8, 128), 0)
    sums = []
    for lane in range(0, chunk, 128):
        lanes = slice(lane, lane + 128)
        taps = [taps_ref[t : t + 1, lanes].astype(F32) for t in range(9)]
        before = sum(taps[3 * a] * left[a : a + rows, lanes] for a in range(3))
        total = jnp.zeros((8, 128), F32)

        def line(r, parity):
            if r < 0:
                return rim[32 * parity : 32 * parity + 32, lanes]
            return hid_ref[r, parity, :, lanes].astype(F32)

        for p in range(rows // 2):
            even = [line(2 * p + a - 1, 0) for a in range(3)]
            odd = [line(2 * p + a - 1, 1) for a in range(3)]
            shifted = sum(taps[3 * a] * odd[a] for a in range(3))
            whole = sum(taps[3 * a + 1] * even[a] + taps[3 * a + 2] * odd[a] for a in range(3))
            shifted = pltpu.roll(shifted, 1, 0)
            first = jnp.where(place == 0, before[2 * p : 2 * p + 1], shifted[0:8])
            act = gelu(whole + jnp.concatenate([first, shifted[8:]], 0))
            act_ref[p, :, lanes] = act.astype(BF16)
            for s in range(0, cols, 8):
                total = total + act[s : s + 8]
        sums.append(total)
    part[...] += jnp.dot(
        jnp.concatenate(sums, 1),
        red_ref[...].astype(F32),
        precision=lax.Precision.HIGHEST,
        preferred_element_type=F32,
    )

    @pl.when(step == pl.num_programs(0) - 1)
    def _():
        whole = jnp.sum(part[...], axis=0, keepdims=True)
        part_ref[...] = jnp.broadcast_to(whole, part_ref.shape)


def down_conv(hidden, upper, left, corner, weight, taps, reduce, copies, chunk=256):
    rows, _, cols, width = hidden.shape
    channels = weight.shape[0]
    squeezed = reduce.shape[1]
    whole = lambda a: pl.BlockSpec(a.shape, lambda c: (0, 0))
    return pl.pallas_call(
        down_conv_kernel,
        grid=(width // chunk,),
        in_specs=[
            pl.BlockSpec((rows, 2, cols, chunk), lambda c: (0, 0, 0, c)),
            whole(upper),
            whole(left),
            whole(corner),
            pl.BlockSpec((channels, chunk), lambda c: (0, c)),
            pl.BlockSpec((9, chunk), lambda c: (0, c)),
            pl.BlockSpec((chunk, squeezed), lambda c: (c, 0)),
        ],
        out_specs=[
            pl.BlockSpec((rows // 2, cols, chunk), lambda c: (0, 0, c)),
            pl.BlockSpec((copies, squeezed), lambda c: (0, 0)),
        ],
        out_shape=[
            jax.ShapeDtypeStruct((rows // 2, cols, width), BF16),
            jax.ShapeDtypeStruct((copies, squeezed), F32),
        ],
        scratch_shapes=[
            panels(64, channels),
            pltpu.VMEM((96, channels), BF16),
            pltpu.VMEM((24, chunk), F32),
            pltpu.VMEM((8, squeezed), F32),
        ],
        compiler_params=params(),
        name="down_conv",
    )(hidden, upper, left, corner, weight, taps, reduce)


def down_out_kernel(
    act_ref, x_ref, parts_ref, restore_ref, project_ref, short_ref, res_ref, cells, *, cell_count
):
    gate = gate_of(parts_ref, restore_ref, cell_count)
    rows, cols, channels = x_ref.shape
    half = cols // 2
    x = x_ref[...].astype(F32).reshape(rows // 2, 2, cols, channels)
    put(cells, (x[:, 0] + x[:, 1]).reshape(rows // 2 * cols, channels))
    count = rows // 2 * half
    pooled = (take_strided(cells, 0, count, 2) + take_strided(cells, 1, count, 2)) * 0.25
    scaled = act_ref[...].reshape(count, act_ref.shape[2]).astype(F32) * gate[0:1, :]
    y = dot(scaled.astype(BF16), project_ref[...]) + dot(pooled.astype(BF16), short_ref[...])
    res_ref[...] = y.astype(BF16).reshape(rows // 2, half, y.shape[1])


def down_out(act, x, parts, restore, project, short, cell_count):
    rows, cols, channels = x.shape
    outs = project.shape[1]

    def kernel(*refs):
        down_out_kernel(*refs, cell_count=cell_count)

    return pl.pallas_call(
        kernel,
        out_shape=jax.ShapeDtypeStruct((rows // 2, cols // 2, outs), BF16),
        scratch_shapes=[panels(rows // 2 * cols, channels)],
        compiler_params=params(),
        name="down_out",
    )(act, x, parts, restore, project, short)


def shift(x, axes, by):
    size = lax.axis_size(axes)
    pairs = [(i, i + by) for i in range(size) if 0 <= i + by < size]
    return lax.ppermute(x, axes, pairs)


def shift_both(x, by_rows, by_cols):
    rows, cols = lax.axis_size(ROWS), lax.axis_size("cols")
    pairs = [
        (r * cols + c, (r + by_rows) * cols + c + by_cols)
        for r in range(rows)
        for c in range(cols)
        if 0 <= r + by_rows < rows and 0 <= c + by_cols < cols
    ]
    return lax.ppermute(x, ALL, pairs)


def sum_parts(part):
    other = lax.ppermute(part, "core", [(0, 1), (1, 0)])
    count, squeezed = part.shape
    both = (part + other).reshape(count, 1, squeezed)
    arrived = lax.all_to_all(both, CLASS, split_axis=0, concat_axis=0, tiled=True)
    return arrived.reshape(count, squeezed)


def local(
    image,
    mb_expand,
    mb_taps,
    mb_reduce,
    mb_restore,
    mb_project,
    block_qkv,
    block_out,
    first_up,
    first_down,
    grid_qkv,
    grid_out,
    second_up,
    second_down,
    down_expand,
    down_taps,
    down_reduce,
    down_restore,
    down_project,
    down_shortcut,
):
    rows, cols, channels = image.shape
    sharers = lax.axis_size(CLASS)
    all_cells = rows * cols * lax.axis_size(ALL)

    left = shift(image[:, cols - 1], "cols", 1)
    right = shift(image[:, 0], "cols", -1)
    hidden = expand(image.reshape(rows * cols, channels), mb_expand)
    pad = jnp.zeros((14, channels), image.dtype)
    last = jnp.concatenate([image[rows - 1], left[rows - 1 :], right[rows - 1 :], pad], 0)
    first = jnp.concatenate([image[0], left[:1], right[:1], pad], 0)
    top = shift(last, ROWS, 1)
    bottom = shift(first, ROWS, -1)
    act, part = conv(
        hidden.reshape(rows, cols, -1), top, bottom, left, right, mb_expand, mb_taps, mb_reduce,
        sharers,
    )
    parts = sum_parts(part)
    mixed = block_part(
        image, act, parts, mb_restore, mb_project, block_qkv, block_out, first_up, first_down,
        all_cells,
    )
    held = rows * cols // sharers
    grouped = lax.all_to_all(
        mixed.reshape(sharers, held, channels), CLASS, split_axis=0, concat_axis=0, tiled=True
    )
    grouped = grid_part(grouped, grid_qkv, grid_out, second_up, second_down)
    section = lax.all_to_all(grouped, CLASS, split_axis=0, concat_axis=0, tiled=True)
    section = section.reshape(rows, cols, channels)

    upper = shift(section[rows - 1], ROWS, 1)
    left = shift(section[:, cols - 1], "cols", 1)
    corner = shift_both(section[rows - 1, cols - 1 :], 1, 1)
    hidden = down_expand_part(section, down_expand)
    act, part = down_conv(
        hidden, upper, left, corner, down_expand, down_taps, down_reduce, sharers
    )
    parts = sum_parts(part)
    downsampled = down_out(
        act, section, parts, down_restore, down_project, down_shortcut, all_cells // 4
    )
    return (section, downsampled)


def solution(mesh):
    rows, cols = mesh.devices.shape
    fine = Mesh(np.asarray(mesh.devices).reshape(rows // 2, 2, cols), ALL)
    tile = P(ROWS, "cols", None)
    in_specs = (tile,) + (P(),) * 19
    return jax.shard_map(
        local, mesh=fine, in_specs=in_specs, out_specs=(tile, tile), check_vma=False
    )
```

time: 480 us -> 178 us (0.37); the launches traced: 473 us -> 177 us
  local copies, waits for them, and re-layouts: 148 us -> 8.84 us
  blocking collectives: 176 us -> 52.9 us
  other arithmetic: 73.1 us -> 0.1 us
  Pallas kernels: 0 us -> 64 us
  matrix products: 44.2 us -> 0 us
  starting transfers between devices: 19.3 us -> 32.9 us
  waiting for transfers between devices: 10.8 us -> 16.8 us
    psum x2 -> x0, blocking collectives: 134 us -> none  [the longest x1 68 us: local(): conv_sums = lax.psum(jnp.sum(activated, axis=(0, 1)), ('rows', 'cols'))]
    slice x13 -> x5, local copies, waits for them, and re-layouts: 92.8 us -> 1.13 us  [the longest x1 1.08 us: local(): left = shift(image[:, cols - 1], 'cols', 1)]
    pallas_call x0 -> x7, Pallas kernels: none -> 64 us  [the longest x1 20.5 us: block_part(): pl.pallas_call(kernel, grid=(rows // WIN * across,), in_specs=[pl.BlockSp...]
    dot_general x19 -> x0, matrix products: 44.2 us -> none  [the longest x2 11.7 us: feed_cells(): jnp.dot(hidden, down_weight, preferred_element_type=jnp.float32)]
    reduce_sum x15 -> x0, other arithmetic: 30.2 us -> none  [the longest x1 10.5 us: local(): conv_sums = lax.psum(jnp.sum(activated, axis=(0, 1)), ('rows', 'cols'))]
    convert_element_type x10 -> x0, local copies, waits for them, and re-layouts: 26.2 us -> none  [the longest x2 8.55 us: attend(): jnp.dot(normed, qkv_weight, preferred_element_type=jnp.float32)]
    reshape x6 -> x0, local copies, waits for them, and re-layouts: 24.3 us -> none  [the longest x2 14.5 us: attend(): projected.reshape(group_count, group_size, 3, head_count, head_width)]
    convert_element_type x15 -> x0, other arithmetic: 21.1 us -> none  [the longest x2 5.25 us: feed_cells(): normed = layer_norm(rows_flat).astype(jnp.bfloat16)]
  transfers between devices with their start and end apart: 6 -> 10, of which waited for: 5 -> 4; matrix products, arithmetic and copies ran while one was open for 1% -> 1% of each run, Pallas kernels for 0% -> 4%
where the time goes in v1:
time: 178 us; the launch traced here: 177 us
  Pallas kernels  64 us (36%)
  blocking collectives  52.9 us (30%)
  starting transfers between devices  32.9 us (18%)
  waiting for transfers between devices  16.8 us (9%)
  local copies, waits for them, and re-layouts  8.84 us (5%)
    all_to_all x2, blocking collectives, sum_parts(): lax.all_to_all(both, CLASS, split_axis=0, concat_axis=0, tiled=True)  34.7 us
    ppermute x6, starting transfers between devices, shift(): return lax.ppermute(x, axes, pairs)  23 us
    pallas_call x1, Pallas kernels, block_part(): pl.pallas_call(kernel, grid=(rows // WIN * across,), in_specs=[pl.BlockSp...  20.5 us
    all_to_all x1, blocking collectives, local(): lax.all_to_all(mixed.reshape(sharers, held, channels), CLASS, split_axis=...  18.2 us
    pallas_call x1, Pallas kernels, grid_part(): pl.pallas_call(kernel, grid=(held // groups,), in_specs=[pl.BlockSpec(x.s...  17.8 us
    all_to_all x1, waiting for transfers between devices, local(): lax.all_to_all(grouped, CLASS, split_axis=0, concat_axis=0, tiled=True)  12.2 us
    pallas_call x1, Pallas kernels, conv(): pl.pallas_call(conv_kernel, grid=(width // chunk,), in_specs=[pl.BlockSpe...  11.5 us
    unnamed x46, local copies, waits for them, and re-layouts  6.79 us
  transfers between devices with their start and end apart: 10, of which 4 were waited for; matrix products, arithmetic and copies ran while one was open for 1% of the time, Pallas kernels for 4%

profile of v1, /device:TPU:1, one launch (start us, length us, event | category | flops | bytes accessed | tf_op | source)
XLA Modules:
  0.0 176.6 jit_solution(4115710984170984562)
XLA Ops:
  0.6 0.0 copy-start.1
  0.6 1.1 fusion
  1.7 5.6 %collective-permute-start = (bf16[16,384]{1,0:T(8,128)(2,1)S(1)}, bf16[16,384]{1,0:T(8,128)(2,1)S(1)}, u32[]{:S(2)}, u32[]{:S(2)}) collective-permute-start(bf16[16,384]{1,0:T(8,128)(2,1)S(1)} %bitcast.41), channel_id=1, source_target_pairs={{0,1},{1,2},{2,3},{3,4},{4,5},{5,6},{6,7},{8,9},{9,10},{10,11},{11... | collective-permute-start | bytes 36872 | tf_op jit(solution)/shard_map/ppermute | solution.py:519
  7.4 1.3 collective-permute-start.1
  8.7 0.8 slice_bitcast_fusion
  9.5 1.2 copy.32.red_ref
  10.7 0.1 pad.7.clone
  10.8 0.0 collective-permute-done.left_ref
  10.8 2.5 %collective-permute-done.1.right_ref = bf16[16,384]{1,0:T(8,128)(2,1)S(1)} collective-permute-done((bf16[16,384]{1,0:T(8,128)(2,1)S(1)}, bf16[16,384]{1,0:T(8,128)(2,1)S(1)}, u32[]{:S(2)}, u32[]{:S(2)}) %collective-permute-start.1) | collective-permute-done | bytes 12320 | tf_op jit(solution)/shard_map/ppermute | solution.py:519
  13.4 0.1 maximum_maximum_fusion.1
  13.5 5.1 %collective-permute-start.2 = (bf16[80,384]{1,0:T(8,128)(2,1)S(1)}, bf16[80,384]{1,0:T(8,128)(2,1)S(1)}, u32[]{:S(2)}, u32[]{:S(2)}) collective-permute-start(bf16[80,384]{1,0:T(8,128)(2,1)S(1)} %get-tuple-element.19), channel_id=1, source_target_pairs={{0,8},{8,16},{16,24},{24,32},{32,40},{40,48},{48,56},{56,64},{64,7... | collective-permute-start | bytes 184328 | tf_op jit(solution)/shard_map/ppermute | solution.py:519
  18.6 1.9 %collective-permute-start.3 = (bf16[80,384]{1,0:T(8,128)(2,1)S(1)}, bf16[80,384]{1,0:T(8,128)(2,1)S(1)}, u32[]{:S(2)}, u32[]{:S(2)}) collective-permute-start(bf16[80,384]{1,0:T(8,128)(2,1)S(1)} %get-tuple-element.18), channel_id=1, source_target_pairs={{8,0},{16,8},{24,16},{32,24},{40,32},{48,40},{56,48},{64,56},{72,6... | collective-permute-start | bytes 184328 | tf_op jit(solution)/shard_map/ppermute | solution.py:519
  20.5 0.0 copy-done.1
  20.5 0.0 copy-start.3
  20.5 1.1 copy-done.3
  21.6 3.5 %expand.1 = bf16[1024,1536]{1,0:T(8,128)(2,1)S(1)} custom-call(bf16[1024,384]{1,0:T(8,128)(2,1)S(1)} %bitcast.34, bf16[384,1536]{1,0:T(8,128)(2,1)S(1)} %copy-done.1), custom_call_target="tpu_custom_call" | custom-call | flops 1207959552 | bytes 3932160 | tf_op jit(solution)/shard_map/expand/pallas_call | solution.py:83
  25.2 0.0 copy-start
  25.2 1.6 copy-done
  26.8 0.0 collective-permute-done.2.top_ref
  26.8 0.0 collective-permute-done.3.bot_ref
  26.8 0.0 copy-start.6
  26.9 0.0 copy-start.7
  26.9 0.0 copy-start.10
  26.9 0.0 copy-start.13
  26.9 0.0 copy-start.14
  26.9 11.5 %conv.1 = (bf16[16,64,1536]{2,1,0:T(8,128)(2,1)S(1)}, f32[64,96]{1,0:T(8,128)S(1)}) custom-call(bf16[16,64,1536]{2,1,0:T(8,128)(2,1)} %bitcast.33, bf16[80,384]{1,0:T(8,128)(2,1)S(1)} %collective-permute-done.2.top_ref, bf16[80,384]{1,0:T(8,128)(2,1)S(1)} %collective-permute-done.3.bot_ref, bf16[16,384]{1,0:T(8,128)(2,1)S(1)} %collective-permute-done.left_ref, ...), custom_call_target="tpu_custom_call" | custom-call | tf_op jit(solution)/shard_map/conv/pallas_call | solution.py:175
  38.4 0.0 copy-start.4
  38.4 1.6 copy-done.4
  40.0 0.0 collective-permute-start.4
  40.0 1.2 collective-permute-done.4
  41.2 19.3 %all_to_all.20 = f32[64,1,96]{2,1,0:T(1,128)S(1)} all-to-all(f32[64,1,96]{2,1,0:T(1,128)S(1)} %bitcast.38), channel_id=1, replica_groups=mesh['row_pair'=8,'core'=2,'cols'=8] {'row_pair','cols'}, dimensions={0} | all-to-all | bytes 49152 | tf_op jit(solution)/shard_map/all_to_all | solution.py:537
  60.5 0.0 copy-done.10
  60.5 0.0 copy-done.13
  60.5 0.0 copy-done.14
  60.5 0.0 copy-start.9
  60.6 0.0 copy-start.11
  60.6 20.5 %block_part.1 = bf16[16,64,384]{2,1,0:T(8,128)(2,1)S(1)} custom-call(bf16[16,64,384]{2,1,0:T(8,128)(2,1)S(1)} %copy-done.3, bf16[16,64,1536]{2,1,0:T(8,128)(2,1)} %copy-done.4, f32[64,96]{1,0:T(8,128)S(1)} %bitcast.36, bf16[96,1536]{1,0:T(8,128)(2,1)S(1)} %copy-done.13, bf16[1536,384]{1,0:T(8,128)(2,1)S(1)} %copy-done.6, bf16[384,1152]{1,0:T(8,128)(2,1)S(1)} %copy-done.10, ...), custom_call_target="tpu_custom_call" | custom-call | tf_op jit(solution)/shard_map/block_part/pallas_call | solution.py:295
  81.1 0.0 copy-start.8
  81.1 0.0 copy-start.15
  81.1 18.2 %all_to_all.21.refs_0_ = bf16[64,16,384]{2,1,0:T(8,128)(2,1)S(1)} all-to-all(bf16[64,16,384]{2,1,0:T(8,128)(2,1)S(1)} %bitcast.35), channel_id=1, replica_groups=mesh['row_pair'=8,'core'=2,'cols'=8] {'row_pair','cols'}, dimensions={0} | all-to-all | bytes 1572864 | tf_op jit(solution)/shard_map/all_to_all | solution.py:585
  99.3 0.0 copy-done.11
  99.3 17.8 %grid_part.1 = bf16[64,16,384]{2,1,0:T(8,128)(2,1)} custom-call(bf16[64,16,384]{2,1,0:T(8,128)(2,1)S(1)} %all_to_all.21.refs_0_, bf16[384,1152]{1,0:T(8,128)(2,1)S(1)} %copy-done.11, bf16[384,384]{1,0:T(8,128)(2,1)S(1)} %copy-done.15, bf16[384,1536]{1,0:T(8,128)(2,1)S(1)} %copy-done.8, bf16[1536,384]{1,0:T(8,128)(2,1)S(1)} %copy-done.9), custom_call_target="tpu_custom_call" | custom-call | tf_op jit(solution)/shard_map/grid_part/pallas_call | solution.py:340
  117.2 5.1 %all-to-all-start.2 = ((bf16[64,16,384]{2,1,0:T(8,128)(2,1)}), bf16[64,16,384]{2,1,0:T(8,128)(2,1)S(1)}, u32[]{:S(2)}, u32[]{:S(2)}) async-start(bf16[64,16,384]{2,1,0:T(8,128)(2,1)} %grid_part.1), calls=%async_computation.2 | async-start | bytes 1572864 | tf_op jit(solution)/shard_map/all_to_all | solution.py:589
  122.3 0.0 copy-done.19
  122.3 0.2 copy.34.red_ref
  122.6 12.2 %all-to-all-done.2 = bf16[64,16,384]{2,1,0:T(8,128)(2,1)S(1)} async-done(((bf16[64,16,384]{2,1,0:T(8,128)(2,1)}), bf16[64,16,384]{2,1,0:T(8,128)(2,1)S(1)}, u32[]{:S(2)}, u32[]{:S(2)}) %all-to-all-start.2) | async-done | bytes 786464 | tf_op jit(solution)/shard_map/all_to_all | solution.py:589
  134.8 6.3 %collective-permute-start.5 = (bf16[64,384]{1,0:T(8,128)(2,1)S(1)}, bf16[64,384]{1,0:T(8,128)(2,1)S(1)}, u32[]{:S(2)}, u32[]{:S(2)}) collective-permute-start(bf16[64,384]{1,0:T(8,128)(2,1)S(1)} %bitcast.40), channel_id=1, source_target_pairs={{0,8},{8,16},{16,24},{24,32},{32,40},{40,48},{48,56},{56,64},{64,7... | collective-permute-start | bytes 147464 | tf_op jit(solution)/shard_map/ppermute | solution.py:519
  141.1 0.0 copy-start.18
  141.1 2.7 %collective-permute-start.6 = (bf16[16,384]{1,0:T(8,128)(2,1)S(1)}, bf16[16,384]{1,0:T(8,128)(2,1)S(1)}, u32[]{:S(2)}, u32[]{:S(2)}) collective-permute-start(bf16[16,384]{1,0:T(8,128)(2,1)S(1)} %bitcast.43), channel_id=1, source_target_pairs={{0,1},{1,2},{2,3},{3,4},{4,5},{5,6},{6,7},{8,9},{9,10},{10,11},{11... | collective-permute-start | bytes 36872 | tf_op jit(solution)/shard_map/ppermute | solution.py:519
  143.9 4.4 %collective-permute-start.7 = (bf16[1,384]{1,0:T(2,128)(2,1)S(1)}, bf16[1,384]{1,0:T(2,128)(2,1)S(1)}, u32[]{:S(2)}, u32[]{:S(2)}) collective-permute-start(bf16[1,384]{1,0:T(2,128)(2,1)S(1)} %slice_bitcast_fusion.2), channel_id=1, source_target_pairs={{0,9},{1,10},{2,11},{3,12},{4,13},{5,14},{6,15},{8,17},{9,18},{10,... | collective-permute-start | bytes 2312 | tf_op jit(solution)/shard_map/ppermute | solution.py:530
  148.2 3.6 %down_expand.1.hid_ref = bf16[16,2,32,1536]{3,2,1,0:T(8,128)(2,1)S(1)} custom-call(bf16[16,64,384]{2,1,0:T(8,128)(2,1)S(1)} %bitcast.30, bf16[384,1536]{1,0:T(8,128)(2,1)S(1)} %copy-done.2), custom_call_target="tpu_custom_call" | custom-call | flops 1207959552 | bytes 3145728 | tf_op jit(solution)/shard_map/down_expand/pallas_call | solution.py:375
  151.9 0.0 copy-start.12
  151.9 0.0 copy-start.16
  151.9 0.0 collective-permute-done.7.corner_ref
  151.9 0.0 collective-permute-done.6.left_ref
  151.9 0.0 collective-permute-done.5.upper_ref
  151.9 0.0 copy-start.5
  151.9 5.1 %down_conv.1 = (bf16[8,32,1536]{2,1,0:T(8,128)(2,1)S(1)}, f32[64,96]{1,0:T(8,128)S(1)}) custom-call(bf16[16,2,32,1536]{3,2,1,0:T(8,128)(2,1)S(1)} %down_expand.1.hid_ref, bf16[64,384]{1,0:T(8,128)(2,1)S(1)} %collective-permute-done.5.upper_ref, bf16[16,384]{1,0:T(8,128)(2,1)S(1)} %collective-permute-done.6.left_ref, ...), custom_call_target="tpu_custom_call" | custom-call | tf_op jit(solution)/shard_map/down_conv/pallas_call | solution.py:454
  157.0 0.5 collective-permute-start.8
  157.5 0.9 collective-permute-done.8
  158.3 15.4 %all_to_all.22 = f32[64,1,96]{2,1,0:T(1,128)S(1)} all-to-all(f32[64,1,96]{2,1,0:T(1,128)S(1)} %bitcast.39), channel_id=1, replica_groups=mesh['row_pair'=8,'core'=2,'cols'=8] {'row_pair','cols'}, dimensions={0} | all-to-all | bytes 49152 | tf_op jit(solution)/shard_map/all_to_all | solution.py:537
  173.8 0.0 copy-done.16
  173.8 2.0 %down_out.1 = bf16[8,32,768]{2,1,0:T(8,128)(2,1)} custom-call(bf16[8,32,1536]{2,1,0:T(8,128)(2,1)S(1)} %get-tuple-element.8.refs_0_, bf16[16,64,384]{2,1,0:T(8,128)(2,1)S(1)} %bitcast.31, f32[64,96]{1,0:T(8,128)S(1)} %bitcast.37, bf16[96,1536]{1,0:T(8,128)(2,1)S(1)} %copy-done.16, bf16[1536,768]{1,0:T(8,128)(2,1)S(1)} %copy-done.5, ...), custom_call_target="tpu_custom_call" | custom-call | tf_op jit(solution)/shard_map/down_out/pallas_call | solution.py:507
  175.8 0.9 copy.46
  (24 shorter events, 0.1 us)
Async XLA Ops:
  0.6 19.9 %copy-start.1 = (bf16[384,1536]{1,0:T(8,128)(2,1)S(1)}, bf16[384,1536]{1,0:T(8,128)(2,1)}, u32[]{:S(2)}) copy-start(bf16[384,1536]{1,0:T(8,128)(2,1)} %w_ref.5) | copy-start | bytes 3538948
  1.7 9.1 %collective-permute-start = (bf16[16,384]{1,0:T(8,128)(2,1)S(1)}, bf16[16,384]{1,0:T(8,128)(2,1)S(1)}, u32[]{:S(2)}, u32[]{:S(2)}) collective-permute-start(bf16[16,384]{1,0:T(8,128)(2,1)S(1)} %bitcast.41), channel_id=1, source_target_pairs={{0,1},{1,2},{2,3},{3,4},{4,5},{5,6},{6,7},{8,9},{9,10},{10,11},{11... | collective-permute-start | bytes 36872 | tf_op jit(solution)/shard_map/ppermute | solution.py:519
  7.4 5.9 %collective-permute-start.1 = (bf16[16,384]{1,0:T(8,128)(2,1)S(1)}, bf16[16,384]{1,0:T(8,128)(2,1)S(1)}, u32[]{:S(2)}, u32[]{:S(2)}) collective-permute-start(bf16[16,384]{1,0:T(8,128)(2,1)S(1)} %bitcast.42), channel_id=1, source_target_pairs={{1,0},{2,1},{3,2},{4,3},{5,4},{6,5},{7,6},{9,8},{10,9},{11,10},{12... | collective-permute-start | bytes 36872 | tf_op jit(solution)/shard_map/ppermute | solution.py:519
  13.5 13.4 %collective-permute-start.2 = (bf16[80,384]{1,0:T(8,128)(2,1)S(1)}, bf16[80,384]{1,0:T(8,128)(2,1)S(1)}, u32[]{:S(2)}, u32[]{:S(2)}) collective-permute-start(bf16[80,384]{1,0:T(8,128)(2,1)S(1)} %get-tuple-element.19), channel_id=1, source_target_pairs={{0,8},{8,16},{16,24},{24,32},{32,40},{40,48},{48,56},{56,64},{64,7... | collective-permute-start | bytes 184328 | tf_op jit(solution)/shard_map/ppermute | solution.py:519
  18.6 8.3 %collective-permute-start.3 = (bf16[80,384]{1,0:T(8,128)(2,1)S(1)}, bf16[80,384]{1,0:T(8,128)(2,1)S(1)}, u32[]{:S(2)}, u32[]{:S(2)}) collective-permute-start(bf16[80,384]{1,0:T(8,128)(2,1)S(1)} %get-tuple-element.18), channel_id=1, source_target_pairs={{8,0},{16,8},{24,16},{32,24},{40,32},{48,40},{56,48},{64,56},{72,6... | collective-permute-start | bytes 184328 | tf_op jit(solution)/shard_map/ppermute | solution.py:519
  20.5 1.1 copy-start.3
  21.6 5.2 %copy-start.17 = (bf16[9,1536]{1,0:T(8,128)(2,1)S(1)}, bf16[9,1536]{1,0:T(8,128)(2,1)}, u32[]{:S(2)}) copy-start(bf16[9,1536]{1,0:T(8,128)(2,1)} %taps_ref.2) | copy-start | bytes 82948
  25.2 1.6 copy-start
  26.8 33.7 %copy-start.6 = (bf16[1536,384]{1,0:T(8,128)(2,1)S(1)}, bf16[1536,384]{1,0:T(8,128)(2,1)}, u32[]{:S(2)}) copy-start(bf16[1536,384]{1,0:T(8,128)(2,1)} %refs_4_.3) | copy-start | bytes 3538948
  26.9 33.7 %copy-start.7 = (bf16[384,1536]{1,0:T(8,128)(2,1)S(1)}, bf16[384,1536]{1,0:T(8,128)(2,1)}, u32[]{:S(2)}) copy-start(bf16[384,1536]{1,0:T(8,128)(2,1)} %refs_7_.1) | copy-start | bytes 3538948
  26.9 33.7 %copy-start.10 = (bf16[384,1152]{1,0:T(8,128)(2,1)S(1)}, bf16[384,1152]{1,0:T(8,128)(2,1)}, u32[]{:S(2)}) copy-start(bf16[384,1152]{1,0:T(8,128)(2,1)} %refs_5_.2) | copy-start | bytes 2654212
  26.9 33.6 %copy-start.13 = (bf16[96,1536]{1,0:T(8,128)(2,1)S(1)}, bf16[96,1536]{1,0:T(8,128)(2,1)}, u32[]{:S(2)}) copy-start(bf16[96,1536]{1,0:T(8,128)(2,1)} %refs_3_.3) | copy-start | bytes 884740
  26.9 33.6 %copy-start.14 = (bf16[384,384]{1,0:T(8,128)(2,1)S(1)}, bf16[384,384]{1,0:T(8,128)(2,1)}, u32[]{:S(2)}) copy-start(bf16[384,384]{1,0:T(8,128)(2,1)} %refs_6_.1) | copy-start | bytes 884740
  38.4 1.6 copy-start.4
  40.0 1.2 collective-permute-start.4
  60.5 38.8 %copy-start.9 = (bf16[1536,384]{1,0:T(8,128)(2,1)S(1)}, bf16[1536,384]{1,0:T(8,128)(2,1)}, u32[]{:S(2)}) copy-start(bf16[1536,384]{1,0:T(8,128)(2,1)} %refs_4_.4) | copy-start | bytes 3538948
  60.6 38.8 %copy-start.11 = (bf16[384,1152]{1,0:T(8,128)(2,1)S(1)}, bf16[384,1152]{1,0:T(8,128)(2,1)}, u32[]{:S(2)}) copy-start(bf16[384,1152]{1,0:T(8,128)(2,1)} %refs_1_.1) | copy-start | bytes 2654212
  81.1 18.2 %copy-start.8 = (bf16[384,1536]{1,0:T(8,128)(2,1)S(1)}, bf16[384,1536]{1,0:T(8,128)(2,1)}, u32[]{:S(2)}) copy-start(bf16[384,1536]{1,0:T(8,128)(2,1)} %refs_3_.4) | copy-start | bytes 3538948
  81.1 18.2 %copy-start.15 = (bf16[384,384]{1,0:T(8,128)(2,1)S(1)}, bf16[384,384]{1,0:T(8,128)(2,1)}, u32[]{:S(2)}) copy-start(bf16[384,384]{1,0:T(8,128)(2,1)} %refs_2_.1) | copy-start | bytes 884740
  117.2 5.2 %copy-start.19 = (bf16[1536,96]{0,1:T(8,128)(2,1)S(1)}, bf16[1536,96]{0,1:T(8,128)(2,1)}, u32[]{:S(2)}) copy-start(bf16[1536,96]{0,1:T(8,128)(2,1)} %param.36) | copy-start | bytes 884740
  117.2 31.1 %copy-start.2 = (bf16[384,1536]{1,0:T(8,128)(2,1)S(1)}, bf16[384,1536]{1,0:T(8,128)(2,1)}, u32[]{:S(2)}) copy-start(bf16[384,1536]{1,0:T(8,128)(2,1)} %w_ref.7) | copy-start | bytes 3538948
  117.2 17.6 %all-to-all-start.2 = ((bf16[64,16,384]{2,1,0:T(8,128)(2,1)}), bf16[64,16,384]{2,1,0:T(8,128)(2,1)S(1)}, u32[]{:S(2)}, u32[]{:S(2)}) async-start(bf16[64,16,384]{2,1,0:T(8,128)(2,1)} %grid_part.1), calls=%async_computation.2 | async-start | bytes 1572864 | tf_op jit(solution)/shard_map/all_to_all | solution.py:589
  134.8 17.1 %collective-permute-start.5 = (bf16[64,384]{1,0:T(8,128)(2,1)S(1)}, bf16[64,384]{1,0:T(8,128)(2,1)S(1)}, u32[]{:S(2)}, u32[]{:S(2)}) collective-permute-start(bf16[64,384]{1,0:T(8,128)(2,1)S(1)} %bitcast.40), channel_id=1, source_target_pairs={{0,8},{8,16},{16,24},{24,32},{32,40},{40,48},{48,56},{56,64},{64,7... | collective-permute-start | bytes 147464 | tf_op jit(solution)/shard_map/ppermute | solution.py:519
  141.1 10.8 %copy-start.18 = (bf16[9,1536]{1,0:T(8,128)(2,1)S(1)}, bf16[9,1536]{1,0:T(8,128)(2,1)}, u32[]{:S(2)}) copy-start(bf16[9,1536]{1,0:T(8,128)(2,1)} %taps_ref.3) | copy-start | bytes 82948
  141.1 10.8 %collective-permute-start.6 = (bf16[16,384]{1,0:T(8,128)(2,1)S(1)}, bf16[16,384]{1,0:T(8,128)(2,1)S(1)}, u32[]{:S(2)}, u32[]{:S(2)}) collective-permute-start(bf16[16,384]{1,0:T(8,128)(2,1)S(1)} %bitcast.43), channel_id=1, source_target_pairs={{0,1},{1,2},{2,3},{3,4},{4,5},{5,6},{6,7},{8,9},{9,10},{10,11},{11... | collective-permute-start | bytes 36872 | tf_op jit(solution)/shard_map/ppermute | solution.py:519
  143.9 8.0 %collective-permute-start.7 = (bf16[1,384]{1,0:T(2,128)(2,1)S(1)}, bf16[1,384]{1,0:T(2,128)(2,1)S(1)}, u32[]{:S(2)}, u32[]{:S(2)}) collective-permute-start(bf16[1,384]{1,0:T(2,128)(2,1)S(1)} %slice_bitcast_fusion.2), channel_id=1, source_target_pairs={{0,9},{1,10},{2,11},{3,12},{4,13},{5,14},{6,15},{8,17},{9,18},{10,... | collective-permute-start | bytes 2312 | tf_op jit(solution)/shard_map/ppermute | solution.py:530
  151.9 21.9 %copy-start.12 = (bf16[384,768]{1,0:T(8,128)(2,1)S(1)}, bf16[384,768]{1,0:T(8,128)(2,1)}, u32[]{:S(2)}) copy-start(bf16[384,768]{1,0:T(8,128)(2,1)} %refs_5_.3) | copy-start | bytes 1769476
  151.9 21.9 %copy-start.16 = (bf16[96,1536]{1,0:T(8,128)(2,1)S(1)}, bf16[96,1536]{1,0:T(8,128)(2,1)}, u32[]{:S(2)}) copy-start(bf16[96,1536]{1,0:T(8,128)(2,1)} %refs_3_.5) | copy-start | bytes 884740
  151.9 21.8 %copy-start.5 = (bf16[1536,768]{1,0:T(8,128)(2,1)S(1)}, bf16[1536,768]{1,0:T(8,128)(2,1)}, u32[]{:S(2)}) copy-start(bf16[1536,768]{1,0:T(8,128)(2,1)} %refs_4_.5) | copy-start | bytes 7077892
  157.0 1.3 collective-permute-start.8

commit v2 on v1

--- a/solution.py
+++ b/solution.py
@@ -22,7 +22,7 @@
 CLASS = ("row_pair", "cols")
 
 
-def params(megabytes=48):
+def params(megabytes):
     return pltpu.CompilerParams(vmem_limit_bytes=megabytes << 20)
 
 
@@ -45,6 +45,16 @@
 
 def dot(a, b):
     return jnp.dot(a, b, preferred_element_type=F32)
+
+
+def exact_dot(a, b, dims):
+    total = None
+    for _ in range(3):
+        term = a.astype(BF16)
+        a = a - term.astype(F32)
+        product = lax.dot_general(term, b, (dims, ((), ())), preferred_element_type=F32)
+        total = product if total is None else total + product
+    return total
 
 
 def panels(rows, channels):
@@ -89,35 +99,43 @@
         ],
         out_specs=pl.BlockSpec((block, hidden), lambda i: (i, 0)),
         out_shape=jax.ShapeDtypeStruct((cells, hidden), BF16),
-        compiler_params=params(),
+        compiler_params=params(16),
         cost_estimate=cost(2 * cells * channels * hidden, 2 * cells * (channels + hidden)),
         name="expand",
     )(x, weight)
 
 
+def rim_of(normed, w_ref, rim, slot):
+    rim[slot] = gelu(dot(normed[...], w_ref[...])).astype(BF16).astype(F32)
+
+
+def squeeze_sums(sums, red_ref, part_ref):
+    parts = exact_dot(sums[...], red_ref[...], ((1,), (1,)))
+    part_ref[...] = jnp.broadcast_to(jnp.sum(parts, axis=0, keepdims=True), part_ref.shape)
+
+
 def conv_kernel(
-    hid_ref, top_ref, bot_ref, left_ref, right_ref, w_ref, taps_ref, red_ref,
-    act_ref, part_ref, normed, left, right, part,
+    hid_ref, over_ref, pair_ref, left_ref, right_ref, first_ref, w_ref, taps_ref, red_ref,
+    act_ref, part_ref, normed, rim, left, right, sums,
 ):
     step = pl.program_id(0)
+    core = lax.axis_index("core")
     rows, cols, chunk = hid_ref.shape
+    slot = step % 2
 
     @pl.when(step == 0)
     def _():
-        for ref, start in ((top_ref, 0), (bot_ref, 80), (left_ref, 160), (right_ref, 176)):
+        for ref, start in ((over_ref, 0), (pair_ref, 80), (left_ref, 160), (right_ref, 176)):
             size = ref.shape[0]
             normed[start : start + size, :] = layer_norm(ref[...].astype(F32)).astype(BF16)
-        part[...] = jnp.zeros_like(part)
-
-    rim = gelu(dot(normed[...], w_ref[...])).astype(BF16).astype(F32)
-    left[0:1, :] = rim[64:65]
-    left[1:17, :] = rim[160:176]
-    left[17:18, :] = rim[144:145]
-    right[0:1, :] = rim[65:66]
-    right[1:17, :] = rim[176:192]
-    right[17:18, :] = rim[145:146]
+        rim_of(normed, first_ref, rim, 0)
+
+    top, bottom = core * 80, (1 - core) * 80
+    for ref, start, corner in ((left, 160, 64), (right, 176, 65)):
+        ref[0:1, :] = rim[slot, pl.ds(top + corner, 1), :]
+        ref[1:17, :] = rim[slot, start : start + 16, :]
+        ref[17:18, :] = rim[slot, pl.ds(bottom + corner, 1), :]
     place = lax.broadcasted_iota(jnp.int32, (8, 128), 0)
-    sums = []
     for lane in range(0, chunk, 128):
         lanes = slice(lane, lane + 128)
         taps = [taps_ref[t : t + 1, lanes].astype(F32) for t in range(9)]
@@ -127,9 +145,9 @@
 
         def line(r):
             if r < 0:
-                return rim[0:64, lanes]
+                return rim[slot, pl.ds(pl.multiple_of(top, 8), 64), lanes]
             if r == rows:
-                return rim[80:144, lanes]
+                return rim[slot, pl.ds(pl.multiple_of(bottom, 8), 64), lanes]
             return hid_ref[r, :, lanes].astype(F32)
 
         window = [line(-1), line(0), None]
@@ -153,37 +171,33 @@
             for s in range(0, cols, 8):
                 total = total + act[s : s + 8]
             window = [window[1], window[2], None]
-        sums.append(total)
-    part[...] += jnp.dot(
-        jnp.concatenate(sums, 1),
-        red_ref[...].astype(F32),
-        precision=lax.Precision.HIGHEST,
-        preferred_element_type=F32,
-    )
+        sums[:, pl.ds(pl.multiple_of(step * chunk + lane, 128), 128)] = total
+    rim_of(normed, w_ref, rim, 1 - slot)
 
     @pl.when(step == pl.num_programs(0) - 1)
     def _():
-        whole = jnp.sum(part[...], axis=0, keepdims=True)
-        part_ref[...] = jnp.broadcast_to(whole, part_ref.shape)
-
-
-def conv(hidden, top, bottom, left, right, weight, taps, reduce, copies, chunk=256):
+        squeeze_sums(sums, red_ref, part_ref)
+
+
+def conv(hidden, over, pair, left, right, weight, taps, reduce, copies, chunk=256):
     rows, cols, width = hidden.shape
     channels = weight.shape[0]
-    squeezed = reduce.shape[1]
+    squeezed = reduce.shape[0]
+    steps = width // chunk
     whole = lambda a: pl.BlockSpec(a.shape, lambda c: (0, 0))
     return pl.pallas_call(
         conv_kernel,
-        grid=(width // chunk,),
+        grid=(steps,),
         in_specs=[
             pl.BlockSpec((rows, cols, chunk), lambda c: (0, 0, c)),
-            whole(top),
-            whole(bottom),
+            whole(over),
+            whole(pair),
             whole(left),
             whole(right),
-            pl.BlockSpec((channels, chunk), lambda c: (0, c)),
+            pl.BlockSpec((channels, chunk), lambda c: (0, 0)),
+            pl.BlockSpec((channels, chunk), lambda c: (0, jnp.minimum(c + 1, steps - 1))),
             pl.BlockSpec((9, chunk), lambda c: (0, c)),
-            pl.BlockSpec((chunk, squeezed), lambda c: (c, 0)),
+            whole(reduce),
         ],
         out_specs=[
             pl.BlockSpec((rows, cols, chunk), lambda c: (0, 0, c)),
@@ -195,26 +209,21 @@
         ],
         scratch_shapes=[
             pltpu.VMEM((192, channels), BF16),
+            pltpu.VMEM((2, 192, chunk), F32),
             pltpu.VMEM((24, chunk), F32),
             pltpu.VMEM((24, chunk), F32),
-            pltpu.VMEM((8, squeezed), F32),
-        ],
-        compiler_params=params(),
+            pltpu.VMEM((8, width), F32),
+        ],
+        compiler_params=params(20),
         name="conv",
-    )(hidden, top, bottom, left, right, weight, taps, reduce)
+    )(hidden, over, pair, left, right, weight, weight, taps, reduce)
 
 
 def gate_of(parts_ref, restore_ref, cell_count):
     average = jnp.sum(parts_ref[...], axis=0, keepdims=True) / cell_count
     squeezed = average * jax.nn.sigmoid(average)
     squeezed = jnp.broadcast_to(squeezed, (8, squeezed.shape[1]))
-    wide = jnp.dot(
-        squeezed,
-        restore_ref[...].astype(F32),
-        precision=lax.Precision.HIGHEST,
-        preferred_element_type=F32,
-    )
-    return jax.nn.sigmoid(wide)
+    return jax.nn.sigmoid(exact_dot(squeezed, restore_ref[...], ((1,), (0,))))
 
 
 def mix(x, qkv_ref, out_ref, up_ref, down_ref):
@@ -281,7 +290,7 @@
     res_ref[...] = jnp.concatenate(pieces, 0).astype(BF16).reshape(rows, cols, channels)
 
 
-def block_part(image, act, parts, restore, project, qkv, out, up, down, cell_count, wide=32):
+def block_part(image, act, parts, restore, project, qkv, out, up, down, cell_count, wide=64):
     rows, cols, channels = image.shape
     hidden = act.shape[2]
     across = cols // wide
@@ -304,7 +313,7 @@
         out_specs=pl.BlockSpec((WIN, wide, channels), place),
         out_shape=jax.ShapeDtypeStruct(image.shape, BF16),
         scratch_shapes=[pltpu.VMEM((8, hidden), F32)],
-        compiler_params=params(),
+        compiler_params=params(40),
         name="block_part",
     )(image, act, parts, *weights)
 
@@ -330,7 +339,7 @@
         res_ref[...] = take(after).astype(BF16).reshape(members, held, channels)
 
 
-def grid_part(x, qkv, out, up, down, groups=4):
+def grid_part(x, qkv, out, up, down, groups=8):
     members, held, channels = x.shape
     weights = (qkv, out, up, down)
 
@@ -350,7 +359,7 @@
             panels(members * held, channels),
             panels(members * held, channels),
         ],
-        compiler_params=params(),
+        compiler_params=params(40),
         name="grid_part",
     )(x, *weights)
 
@@ -382,18 +391,19 @@
         out_specs=pl.BlockSpec((block, 2, cols // 2, hidden), lambda i: (i, 0, 0, 0)),
         out_shape=jax.ShapeDtypeStruct((rows, 2, cols // 2, hidden), BF16),
         scratch_shapes=[panels(block * cols, channels)],
-        compiler_params=params(),
+        compiler_params=params(16),
         cost_estimate=cost(2 * rows * cols * channels * hidden, 2 * rows * cols * hidden),
         name="down_expand",
     )(x, weight)
 
 
 def down_conv_kernel(
-    hid_ref, upper_ref, left_ref, corner_ref, w_ref, taps_ref, red_ref,
-    act_ref, part_ref, cells, normed, left, part,
+    hid_ref, upper_ref, left_ref, corner_ref, first_ref, w_ref, taps_ref, red_ref,
+    act_ref, part_ref, cells, normed, rim, left, sums,
 ):
     step = pl.program_id(0)
     rows, _, cols, chunk = hid_ref.shape
+    slot = step % 2
 
     @pl.when(step == 0)
     def _():
@@ -403,13 +413,11 @@
         normed[64:80, :] = layer_norm(left_ref[...].astype(F32)).astype(BF16)
         corner = layer_norm(corner_ref[...].astype(F32))
         normed[80:96, :] = jnp.broadcast_to(corner, (16, corner.shape[1])).astype(BF16)
-        part[...] = jnp.zeros_like(part)
-
-    rim = gelu(dot(normed[...], w_ref[...])).astype(BF16).astype(F32)
-    left[0:1, :] = rim[80:81]
-    left[1:17, :] = rim[64:80]
+        rim_of(normed, first_ref, rim, 0)
+
+    left[0:1, :] = rim[slot, 80:81, :]
+    left[1:17, :] = rim[slot, 64:80, :]
     place = lax.broadcasted_iota(jnp.int32, (8, 128), 0)
-    sums = []
     for lane in range(0, chunk, 128):
         lanes = slice(lane, lane + 128)
         taps = [taps_ref[t : t + 1, lanes].astype(F32) for t in range(9)]
@@ -418,7 +426,7 @@
 
         def line(r, parity):
             if r < 0:
-                return rim[32 * parity : 32 * parity + 32, lanes]
+                return rim[slot, 32 * parity : 32 * parity + 32, lanes]
             return hid_ref[r, parity, :, lanes].astype(F32)
 
         for p in range(rows // 2):
@@ -432,36 +440,32 @@
             act_ref[p, :, lanes] = act.astype(BF16)
             for s in range(0, cols, 8):
                 total = total + act[s : s + 8]
-        sums.append(total)
-    part[...] += jnp.dot(
-        jnp.concatenate(sums, 1),
-        red_ref[...].astype(F32),
-        precision=lax.Precision.HIGHEST,
-        preferred_element_type=F32,
-    )
+        sums[:, pl.ds(pl.multiple_of(step * chunk + lane, 128), 128)] = total
+    rim_of(normed, w_ref, rim, 1 - slot)
 
     @pl.when(step == pl.num_programs(0) - 1)
     def _():
-        whole = jnp.sum(part[...], axis=0, keepdims=True)
-        part_ref[...] = jnp.broadcast_to(whole, part_ref.shape)
+        squeeze_sums(sums, red_ref, part_ref)
 
 
 def down_conv(hidden, upper, left, corner, weight, taps, reduce, copies, chunk=256):
     rows, _, cols, width = hidden.shape
     channels = weight.shape[0]
-    squeezed = reduce.shape[1]
+    squeezed = reduce.shape[0]
+    steps = width // chunk
     whole = lambda a: pl.BlockSpec(a.shape, lambda c: (0, 0))
     return pl.pallas_call(
         down_conv_kernel,
-        grid=(width // chunk,),
+        grid=(steps,),
         in_specs=[
             pl.BlockSpec((rows, 2, cols, chunk), lambda c: (0, 0, 0, c)),
             whole(upper),
             whole(left),
             whole(corner),
-            pl.BlockSpec((channels, chunk), lambda c: (0, c)),
+            pl.BlockSpec((channels, chunk), lambda c: (0, 0)),
+            pl.BlockSpec((channels, chunk), lambda c: (0, jnp.minimum(c + 1, steps - 1))),
             pl.BlockSpec((9, chunk), lambda c: (0, c)),
-            pl.BlockSpec((chunk, squeezed), lambda c: (c, 0)),
+            whole(reduce),
         ],
         out_specs=[
             pl.BlockSpec((rows // 2, cols, chunk), lambda c: (0, 0, c)),
@@ -474,12 +478,13 @@
         scratch_shapes=[
             panels(64, channels),
             pltpu.VMEM((96, channels), BF16),
+            pltpu.VMEM((2, 96, chunk), F32),
             pltpu.VMEM((24, chunk), F32),
-            pltpu.VMEM((8, squeezed), F32),
-        ],
-        compiler_params=params(),
+            pltpu.VMEM((8, width), F32),
+        ],
+        compiler_params=params(16),
         name="down_conv",
-    )(hidden, upper, left, corner, weight, taps, reduce)
+    )(hidden, upper, left, corner, weight, weight, taps, reduce)
 
 
 def down_out_kernel(
@@ -508,7 +513,7 @@
         kernel,
         out_shape=jax.ShapeDtypeStruct((rows // 2, cols // 2, outs), BF16),
         scratch_shapes=[panels(rows // 2 * cols, channels)],
-        compiler_params=params(),
+        compiler_params=params(24),
         name="down_out",
     )(act, x, parts, restore, project, short)
 
@@ -531,11 +536,25 @@
 
 
 def sum_parts(part):
-    other = lax.ppermute(part, "core", [(0, 1), (1, 0)])
     count, squeezed = part.shape
-    both = (part + other).reshape(count, 1, squeezed)
-    arrived = lax.all_to_all(both, CLASS, split_axis=0, concat_axis=0, tiled=True)
+    part = part.reshape(count, 1, squeezed)
+    arrived = lax.all_to_all(part, ALL, split_axis=0, concat_axis=0, tiled=True)
     return arrived.reshape(count, squeezed)
+
+
+def row_rims(image, left, right):
+    rows, cols, channels = image.shape
+    size = lax.axis_size(ROWS)
+    pad = jnp.zeros((14, channels), image.dtype)
+    first = jnp.concatenate([image[0], left[:1], right[:1], pad], 0)
+    last = jnp.concatenate([image[rows - 1], left[rows - 1 :], right[rows - 1 :], pad], 0)
+    even = lax.axis_index("core") == 0
+    away = jnp.where(even, first, last)
+    near = jnp.where(even, last, first)
+    pairs = [(r, r - 1 if r % 2 == 0 else r + 1) for r in range(1, size - 1)]
+    over = lax.ppermute(away, ROWS, pairs)
+    pair = lax.ppermute(near, "core", [(0, 1), (1, 0)])
+    return over, pair
 
 
 def local(
@@ -567,14 +586,10 @@
     left = shift(image[:, cols - 1], "cols", 1)
     right = shift(image[:, 0], "cols", -1)
     hidden = expand(image.reshape(rows * cols, channels), mb_expand)
-    pad = jnp.zeros((14, channels), image.dtype)
-    last = jnp.concatenate([image[rows - 1], left[rows - 1 :], right[rows - 1 :], pad], 0)
-    first = jnp.concatenate([image[0], left[:1], right[:1], pad], 0)
-    top = shift(last, ROWS, 1)
-    bottom = shift(first, ROWS, -1)
+    over, pair = row_rims(image, left, right)
     act, part = conv(
-        hidden.reshape(rows, cols, -1), top, bottom, left, right, mb_expand, mb_taps, mb_reduce,
-        sharers,
+        hidden.reshape(rows, cols, -1), over, pair, left, right, mb_expand, mb_taps, mb_reduce.T,
+        lax.axis_size(ALL),
     )
     parts = sum_parts(part)
     mixed = block_part(
@@ -594,7 +609,7 @@
     corner = shift_both(section[rows - 1, cols - 1 :], 1, 1)
     hidden = down_expand_part(section, down_expand)
     act, part = down_conv(
-        hidden, upper, left, corner, down_expand, down_taps, down_reduce, sharers
+        hidden, upper, left, corner, down_expand, down_taps, down_reduce.T, lax.axis_size(ALL)
     )
     parts = sum_parts(part)
     downsampled = down_out(

time: 178 us -> 152 us (0.85)
  blocking collectives: 52.9 us -> 75.5 us
  Pallas kernels: 64 us -> 45.6 us
  waiting for transfers between devices: 16.8 us -> 0.02 us
  starting transfers between devices: 32.9 us -> 23.7 us
  local copies, waits for them, and re-layouts: 8.84 us -> 5.37 us
    all_to_all x2 -> x3, blocking collectives: 34.7 us -> 55.1 us  [the longest x2 36.1 us: sum_parts(): arrived = lax.all_to_all(part, ALL, split_axis=0, concat_axis=0, tiled=True)]
    all_to_all x1 -> x0, waiting for transfers between devices: 12.2 us -> none  [local(): lax.all_to_all(grouped, CLASS, split_axis=0, concat_axis=0, tiled=True)]
    ppermute x6 -> x4, starting transfers between devices: 23 us -> 14 us  [shift(): return lax.ppermute(x, axes, pairs)]
    pallas_call x1, Pallas kernels: 20.5 us -> 12.2 us  [block_part(): pl.pallas_call(kernel, grid=(rows // WIN * across,), in_specs=[pl.BlockSp...]
    pallas_call x1, Pallas kernels: 17.8 us -> 11.2 us  [grid_part(): pl.pallas_call(kernel, grid=(held // groups,), in_specs=[pl.BlockSpec(x.s...]
    all_to_all x1 -> x0, starting transfers between devices: 5.14 us -> none  [local(): lax.all_to_all(grouped, CLASS, split_axis=0, concat_axis=0, tiled=True)]
    ppermute x2, starting transfers between devices: 0.47 us -> 4.79 us  [the longest x1 3.1 us: row_rims(): over = lax.ppermute(away, ROWS, pairs)]
    pallas_call x2, Pallas kernels: 16.5 us -> 13.1 us  [the longest x1 9.26 us: conv(): pl.pallas_call(conv_kernel, grid=(steps,), in_specs=[pl.BlockSpec((rows,...]
  transfers between devices with their start and end apart: 10 -> 7, of which waited for: 4 -> 0; matrix products, arithmetic and copies ran while one was open for 1% -> 1% of each run, Pallas kernels for 4% -> 5%
where the time goes in v2:
time: 152 us; the launch traced here: 151 us
  blocking collectives  75.5 us (50%)
  Pallas kernels  45.6 us (30%)
  starting transfers between devices  23.7 us (16%)
  local copies, waits for them, and re-layouts  5.37 us (4%)
    all_to_all x2, blocking collectives, sum_parts(): arrived = lax.all_to_all(part, ALL, split_axis=0, concat_axis=0, tiled=True)  36.1 us
    all_to_all x1, blocking collectives, local(): lax.all_to_all(mixed.reshape(sharers, held, channels), CLASS, split_axis=...  20.3 us
    all_to_all x1, blocking collectives, local(): lax.all_to_all(grouped, CLASS, split_axis=0, concat_axis=0, tiled=True)  19 us
    ppermute x4, starting transfers between devices, shift(): return lax.ppermute(x, axes, pairs)  14 us
    pallas_call x1, Pallas kernels, block_part(): pl.pallas_call(kernel, grid=(rows // WIN * across,), in_specs=[pl.BlockSp...  12.2 us
    pallas_call x1, Pallas kernels, grid_part(): pl.pallas_call(kernel, grid=(held // groups,), in_specs=[pl.BlockSpec(x.s...  11.2 us
    pallas_call x1, Pallas kernels, conv(): pl.pallas_call(conv_kernel, grid=(steps,), in_specs=[pl.BlockSpec((rows,...  9.26 us
    ppermute x1, starting transfers between devices, shift_both(): return lax.ppermute(x, ALL, pairs)  4.99 us
  transfers between devices with their start and end apart: 7, of which 0 were waited for; matrix products, arithmetic and copies ran while one was open for 1% of the time, Pallas kernels for 5%

profile of v2, /device:TPU:1, one launch (start us, length us, event | category | flops | bytes accessed | tf_op | source)
XLA Modules:
  0.0 151.4 jit_solution(4117107384435033675)
XLA Ops:
  0.6 1.0 fusion
  1.6 1.3 collective-permute-start.1
  2.9 6.3 %collective-permute-start = (bf16[16,384]{1,0:T(8,128)(2,1)S(1)}, bf16[16,384]{1,0:T(8,128)(2,1)S(1)}, u32[]{:S(2)}, u32[]{:S(2)}) collective-permute-start(bf16[16,384]{1,0:T(8,128)(2,1)S(1)} %bitcast.46), channel_id=1, source_target_pairs={{0,1},{1,2},{2,3},{3,4},{4,5},{5,6},{6,7},{8,9},{9,10},{10,11},{11... | collective-permute-start | bytes 36872 | tf_op jit(solution)/shard_map/ppermute | solution.py:524
  9.2 0.8 slice_bitcast_fusion.1
  10.1 0.1 pad.7.clone
  10.2 0.0 collective-permute-done.1.right_ref
  10.2 0.0 collective-permute-done.left_ref
  10.2 0.1 broadcast_select_fusion
  10.3 1.7 %collective-permute-start.3 = (bf16[80,384]{1,0:T(8,128)(2,1)S(1)}, bf16[80,384]{1,0:T(8,128)(2,1)S(1)}, u32[]{:S(2)}, u32[]{:S(2)}) collective-permute-start(bf16[80,384]{1,0:T(8,128)(2,1)S(1)} %get-tuple-element.14), channel_id=1, source_target_pairs={{0,8},{8,0},{1,9},{9,1},{2,10},{10,2},{3,11},{11,3},{4,12},{12,4},... | collective-permute-start | bytes 184328 | tf_op jit(solution)/shard_map/ppermute | solution.py:556
  12.0 3.1 %collective-permute-start.2 = (bf16[80,384]{1,0:T(8,128)(2,1)S(1)}, bf16[80,384]{1,0:T(8,128)(2,1)S(1)}, u32[]{:S(2)}, u32[]{:S(2)}) collective-permute-start(bf16[80,384]{1,0:T(8,128)(2,1)S(1)} %get-tuple-element.15), channel_id=1, source_target_pairs={{8,16},{16,8},{24,32},{32,24},{40,48},{48,40},{56,64},{64,56},{72,... | collective-permute-start | bytes 184328 | tf_op jit(solution)/shard_map/ppermute | solution.py:555
  15.1 0.0 copy-start
  15.1 1.3 copy-done
  16.4 1.1 copy-done.3
  17.5 3.5 %expand.1 = bf16[1024,1536]{1,0:T(8,128)(2,1)S(1)} custom-call(bf16[1024,384]{1,0:T(8,128)(2,1)S(1)} %bitcast.36, bf16[384,1536]{1,0:T(8,128)(2,1)S(1)} %copy-done), custom_call_target="tpu_custom_call" | custom-call | flops 1207959552 | bytes 3932160 | tf_op jit(solution)/shard_map/expand/pallas_call | solution.py:93
  21.1 0.0 collective-permute-done.3.pair_ref
  21.1 0.0 collective-permute-done.2.over_ref
  21.1 0.0 copy-done.1
  21.1 0.0 copy-done.14
  21.1 0.0 copy-done.20
  21.1 0.0 copy-start.4
  21.1 0.0 copy-start.6
  21.1 0.0 copy-start.7
  21.2 0.0 copy-start.8
  21.2 0.0 copy-start.11
  21.2 0.0 copy-start.15
  21.2 0.0 copy-start.16
  21.2 9.3 %conv.1 = (bf16[16,64,1536]{2,1,0:T(8,128)(2,1)S(1)}, f32[128,96]{1,0:T(8,128)S(1)}) custom-call(bf16[16,64,1536]{2,1,0:T(8,128)(2,1)S(1)} %bitcast.35, bf16[80,384]{1,0:T(8,128)(2,1)S(1)} %collective-permute-done.2.over_ref, bf16[80,384]{1,0:T(8,128)(2,1)S(1)} %collective-permute-done.3.pair_ref, bf16[16,384]{1,0:T(8,128)(2,1)S(1)} %collective-permute-done.left_ref, ...), custom_call_target="tpu_custom_call" | custom-call | tf_op jit(solution)/shard_map/conv/pallas_call | solution.py:188
  30.5 21.0 %all_to_all.20 = f32[128,1,96]{2,1,0:T(1,128)S(1)} all-to-all(f32[128,1,96]{2,1,0:T(1,128)S(1)} %bitcast.42), channel_id=1, replica_groups=mesh['row_pair'=8,'core'=2,'cols'=8] {'row_pair','core','cols'}, dimensions={0} | all-to-all | bytes 98304 | tf_op jit(solution)/shard_map/all_to_all | solution.py:541
  51.4 0.0 copy-done.4
  51.4 0.0 copy-done.6
  51.4 0.0 copy-done.7
  51.4 0.0 copy-done.8
  51.5 0.0 copy-done.11
  51.5 0.0 copy-done.15
  51.5 0.0 copy-done.16
  51.5 0.0 copy-start.10
  51.5 0.0 copy-start.12
  51.5 12.2 %block_part.1 = bf16[16,64,384]{2,1,0:T(8,128)(2,1)S(1)} custom-call(bf16[16,64,384]{2,1,0:T(8,128)(2,1)S(1)} %copy-done.4, bf16[16,64,1536]{2,1,0:T(8,128)(2,1)S(1)} %get-tuple-element.6.refs_1_, f32[128,96]{1,0:T(8,128)S(1)} %bitcast.40, bf16[96,1536]{1,0:T(8,128)(2,1)S(1)} %copy-done.15, bf16[1536,384]{1,0:T(8,128)(2,1)S(1)} %copy-done.6, ...), custom_call_target="tpu_custom_call" | custom-call | tf_op jit(solution)/shard_map/block_part/pallas_call | solution.py:304
  63.7 0.0 copy-start.9
  63.8 0.0 copy-start.17
  63.8 20.3 %all_to_all.21.refs_0_ = bf16[64,16,384]{2,1,0:T(8,128)(2,1)S(1)} all-to-all(bf16[64,16,384]{2,1,0:T(8,128)(2,1)S(1)} %bitcast.37), channel_id=1, replica_groups=mesh['row_pair'=8,'core'=2,'cols'=8] {'row_pair','cols'}, dimensions={0} | all-to-all | bytes 1572864 | tf_op jit(solution)/shard_map/all_to_all | solution.py:600
  84.1 0.0 copy-done.10
  84.1 0.0 copy-done.12
  84.1 0.0 copy-done.9
  84.1 11.2 %grid_part.1 = bf16[64,16,384]{2,1,0:T(8,128)(2,1)S(1)} custom-call(bf16[64,16,384]{2,1,0:T(8,128)(2,1)S(1)} %all_to_all.21.refs_0_, bf16[384,1152]{1,0:T(8,128)(2,1)S(1)} %copy-done.12, bf16[384,384]{1,0:T(8,128)(2,1)S(1)} %copy-done.17, bf16[384,1536]{1,0:T(8,128)(2,1)S(1)} %copy-done.9, bf16[1536,384]{1,0:T(8,128)(2,1)S(1)} %copy-done.10), custom_call_target="tpu_custom_call" | custom-call | tf_op jit(solution)/shard_map/grid_part/pallas_call | solution.py:349
  95.3 0.0 copy-start.2
  95.3 19.0 %all_to_all.22 = bf16[64,16,384]{2,1,0:T(8,128)(2,1)S(1)} all-to-all(bf16[64,16,384]{2,1,0:T(8,128)(2,1)S(1)} %grid_part.1), channel_id=1, replica_groups=mesh['row_pair'=8,'core'=2,'cols'=8] {'row_pair','cols'}, dimensions={0} | all-to-all | bytes 1572864 | tf_op jit(solution)/shard_map/all_to_all | solution.py:604
  114.4 5.0 %collective-permute-start.6 = (bf16[1,384]{1,0:T(2,128)(2,1)S(1)}, bf16[1,384]{1,0:T(2,128)(2,1)S(1)}, u32[]{:S(2)}, u32[]{:S(2)}) collective-permute-start(bf16[1,384]{1,0:T(2,128)(2,1)S(1)} %slice_bitcast_fusion.2), channel_id=1, source_target_pairs={{0,9},{1,10},{2,11},{3,12},{4,13},{5,14},{6,15},{8,17},{9,18},{10,... | collective-permute-start | bytes 2312 | tf_op jit(solution)/shard_map/ppermute | solution.py:535
  119.4 4.3 %collective-permute-start.5 = (bf16[16,384]{1,0:T(8,128)(2,1)S(1)}, bf16[16,384]{1,0:T(8,128)(2,1)S(1)}, u32[]{:S(2)}, u32[]{:S(2)}) collective-permute-start(bf16[16,384]{1,0:T(8,128)(2,1)S(1)} %bitcast.47), channel_id=1, source_target_pairs={{0,1},{1,2},{2,3},{3,4},{4,5},{5,6},{6,7},{8,9},{9,10},{10,11},{11... | collective-permute-start | bytes 36872 | tf_op jit(solution)/shard_map/ppermute | solution.py:524
  123.8 0.0 copy-start.18
  123.8 0.0 copy-start.21
  123.8 2.1 %collective-permute-start.4 = (bf16[64,384]{1,0:T(8,128)(2,1)S(1)}, bf16[64,384]{1,0:T(8,128)(2,1)S(1)}, u32[]{:S(2)}, u32[]{:S(2)}) collective-permute-start(bf16[64,384]{1,0:T(8,128)(2,1)S(1)} %bitcast.44), channel_id=1, source_target_pairs={{0,8},{8,16},{16,24},{24,32},{32,40},{40,48},{48,56},{56,64},{64,7... | collective-permute-start | bytes 147464 | tf_op jit(solution)/shard_map/ppermute | solution.py:524
  125.9 3.6 %down_expand.1.hid_ref = bf16[16,2,32,1536]{3,2,1,0:T(8,128)(2,1)S(1)} custom-call(bf16[16,64,384]{2,1,0:T(8,128)(2,1)S(1)} %bitcast.32, bf16[384,1536]{1,0:T(8,128)(2,1)S(1)} %copy-done.2), custom_call_target="tpu_custom_call" | custom-call | flops 1207959552 | bytes 3145728 | tf_op jit(solution)/shard_map/down_expand/pallas_call | solution.py:384
  129.5 0.0 collective-permute-done.6.corner_ref
  129.5 0.0 collective-permute-done.5.left_ref
  129.5 0.0 collective-permute-done.4.upper_ref
  129.5 0.0 copy-start.5
  129.5 0.0 copy-start.13
  129.6 0.0 copy-start.19
  129.6 3.9 %down_conv.1 = (bf16[8,32,1536]{2,1,0:T(8,128)(2,1)S(1)}, f32[128,96]{1,0:T(8,128)S(1)}) custom-call(bf16[16,2,32,1536]{3,2,1,0:T(8,128)(2,1)S(1)} %down_expand.1.hid_ref, bf16[64,384]{1,0:T(8,128)(2,1)S(1)} %collective-permute-done.4.upper_ref, bf16[16,384]{1,0:T(8,128)(2,1)S(1)} %collective-permute-done.5.left_ref, ...), custom_call_target="tpu_custom_call" | custom-call | tf_op jit(solution)/shard_map/down_conv/pallas_call | solution.py:457
  133.5 15.2 %all_to_all.23 = f32[128,1,96]{2,1,0:T(1,128)S(1)} all-to-all(f32[128,1,96]{2,1,0:T(1,128)S(1)} %bitcast.43), channel_id=1, replica_groups=mesh['row_pair'=8,'core'=2,'cols'=8] {'row_pair','core','cols'}, dimensions={0} | all-to-all | bytes 98304 | tf_op jit(solution)/shard_map/all_to_all | solution.py:541
  148.6 0.0 copy-done.5
  148.6 1.9 %down_out.1 = bf16[8,32,768]{2,1,0:T(8,128)(2,1)} custom-call(bf16[8,32,1536]{2,1,0:T(8,128)(2,1)S(1)} %get-tuple-element.8.refs_0_, bf16[16,64,384]{2,1,0:T(8,128)(2,1)S(1)} %bitcast.33, f32[128,96]{1,0:T(8,128)S(1)} %bitcast.41, bf16[96,1536]{1,0:T(8,128)(2,1)S(1)} %copy-done.19, bf16[1536,768]{1,0:T(8,128)(2,1)S(1)} %copy-done.5, ...), custom_call_target="tpu_custom_call" | custom-call | tf_op jit(solution)/shard_map/down_out/pallas_call | solution.py:512
  150.5 0.9 copy.40
  (19 shorter events, 0.1 us)
Async XLA Ops:
  1.6 8.5 %collective-permute-start.1 = (bf16[16,384]{1,0:T(8,128)(2,1)S(1)}, bf16[16,384]{1,0:T(8,128)(2,1)S(1)}, u32[]{:S(2)}, u32[]{:S(2)}) collective-permute-start(bf16[16,384]{1,0:T(8,128)(2,1)S(1)} %bitcast.45), channel_id=1, source_target_pairs={{1,0},{2,1},{3,2},{4,3},{5,4},{6,5},{7,6},{9,8},{10,9},{11,10},{12... | collective-permute-start | bytes 36872 | tf_op jit(solution)/shard_map/ppermute | solution.py:524
  2.9 7.2 %collective-permute-start = (bf16[16,384]{1,0:T(8,128)(2,1)S(1)}, bf16[16,384]{1,0:T(8,128)(2,1)S(1)}, u32[]{:S(2)}, u32[]{:S(2)}) collective-permute-start(bf16[16,384]{1,0:T(8,128)(2,1)S(1)} %bitcast.46), channel_id=1, source_target_pairs={{0,1},{1,2},{2,3},{3,4},{4,5},{5,6},{6,7},{8,9},{9,10},{10,11},{11... | collective-permute-start | bytes 36872 | tf_op jit(solution)/shard_map/ppermute | solution.py:524
  10.3 10.8 %collective-permute-start.3 = (bf16[80,384]{1,0:T(8,128)(2,1)S(1)}, bf16[80,384]{1,0:T(8,128)(2,1)S(1)}, u32[]{:S(2)}, u32[]{:S(2)}) collective-permute-start(bf16[80,384]{1,0:T(8,128)(2,1)S(1)} %get-tuple-element.14), channel_id=1, source_target_pairs={{0,8},{8,0},{1,9},{9,1},{2,10},{10,2},{3,11},{11,3},{4,12},{12,4},... | collective-permute-start | bytes 184328 | tf_op jit(solution)/shard_map/ppermute | solution.py:556
  12.0 9.1 %collective-permute-start.2 = (bf16[80,384]{1,0:T(8,128)(2,1)S(1)}, bf16[80,384]{1,0:T(8,128)(2,1)S(1)}, u32[]{:S(2)}, u32[]{:S(2)}) collective-permute-start(bf16[80,384]{1,0:T(8,128)(2,1)S(1)} %get-tuple-element.15), channel_id=1, source_target_pairs={{8,16},{16,8},{24,32},{32,24},{40,48},{48,40},{56,64},{64,56},{72,... | collective-permute-start | bytes 184328 | tf_op jit(solution)/shard_map/ppermute | solution.py:555
  15.1 1.3 copy-start
  16.4 1.1 copy-start.3
  17.5 3.6 %copy-start.1 = (bf16[384,1536]{1,0:T(8,128)(2,1)S(1)}, bf16[384,1536]{1,0:T(8,128)(2,1)}, u32[]{:S(2)}) copy-start(bf16[384,1536]{1,0:T(8,128)(2,1)} %w_ref.5) | copy-start | bytes 3538948
  17.5 3.6 %copy-start.14 = (bf16[1536,96]{0,1:T(8,128)(2,1)S(1)}, bf16[1536,96]{0,1:T(8,128)(2,1)}, u32[]{:S(2)}) copy-start(bf16[1536,96]{0,1:T(8,128)(2,1)} %param.23) | copy-start | bytes 884740
  17.5 3.6 %copy-start.20 = (bf16[9,1536]{1,0:T(8,128)(2,1)S(1)}, bf16[9,1536]{1,0:T(8,128)(2,1)}, u32[]{:S(2)}) copy-start(bf16[9,1536]{1,0:T(8,128)(2,1)} %taps_ref.2) | copy-start | bytes 82948
  21.1 30.3 %copy-start.4 = (bf16[16,64,384]{2,1,0:T(8,128)(2,1)S(1)}, bf16[16,64,384]{2,1,0:T(8,128)(2,1)}, u32[]{:S(2)}) copy-start(bf16[16,64,384]{2,1,0:T(8,128)(2,1)} %refs_0_.1) | copy-start | bytes 2359300
  21.1 30.3 %copy-start.6 = (bf16[1536,384]{1,0:T(8,128)(2,1)S(1)}, bf16[1536,384]{1,0:T(8,128)(2,1)}, u32[]{:S(2)}) copy-start(bf16[1536,384]{1,0:T(8,128)(2,1)} %refs_4_.3) | copy-start | bytes 3538948
  21.1 30.3 %copy-start.7 = (bf16[384,1536]{1,0:T(8,128)(2,1)S(1)}, bf16[384,1536]{1,0:T(8,128)(2,1)}, u32[]{:S(2)}) copy-start(bf16[384,1536]{1,0:T(8,128)(2,1)} %refs_7_.1) | copy-start | bytes 3538948
  21.2 30.3 %copy-start.8 = (bf16[1536,384]{1,0:T(8,128)(2,1)S(1)}, bf16[1536,384]{1,0:T(8,128)(2,1)}, u32[]{:S(2)}) copy-start(bf16[1536,384]{1,0:T(8,128)(2,1)} %refs_8_.1) | copy-start | bytes 3538948
  21.2 30.3 %copy-start.11 = (bf16[384,1152]{1,0:T(8,128)(2,1)S(1)}, bf16[384,1152]{1,0:T(8,128)(2,1)}, u32[]{:S(2)}) copy-start(bf16[384,1152]{1,0:T(8,128)(2,1)} %refs_5_.2) | copy-start | bytes 2654212
  21.2 30.3 %copy-start.15 = (bf16[96,1536]{1,0:T(8,128)(2,1)S(1)}, bf16[96,1536]{1,0:T(8,128)(2,1)}, u32[]{:S(2)}) copy-start(bf16[96,1536]{1,0:T(8,128)(2,1)} %refs_3_.3) | copy-start | bytes 884740
  21.2 30.3 %copy-start.16 = (bf16[384,384]{1,0:T(8,128)(2,1)S(1)}, bf16[384,384]{1,0:T(8,128)(2,1)}, u32[]{:S(2)}) copy-start(bf16[384,384]{1,0:T(8,128)(2,1)} %refs_6_.1) | copy-start | bytes 884740
  51.5 32.6 %copy-start.10 = (bf16[1536,384]{1,0:T(8,128)(2,1)S(1)}, bf16[1536,384]{1,0:T(8,128)(2,1)}, u32[]{:S(2)}) copy-start(bf16[1536,384]{1,0:T(8,128)(2,1)} %refs_4_.4) | copy-start | bytes 3538948
  51.5 32.6 %copy-start.12 = (bf16[384,1152]{1,0:T(8,128)(2,1)S(1)}, bf16[384,1152]{1,0:T(8,128)(2,1)}, u32[]{:S(2)}) copy-start(bf16[384,1152]{1,0:T(8,128)(2,1)} %refs_1_.1) | copy-start | bytes 2654212
  63.7 20.4 %copy-start.9 = (bf16[384,1536]{1,0:T(8,128)(2,1)S(1)}, bf16[384,1536]{1,0:T(8,128)(2,1)}, u32[]{:S(2)}) copy-start(bf16[384,1536]{1,0:T(8,128)(2,1)} %refs_3_.4) | copy-start | bytes 3538948
  63.8 20.4 %copy-start.17 = (bf16[384,384]{1,0:T(8,128)(2,1)S(1)}, bf16[384,384]{1,0:T(8,128)(2,1)}, u32[]{:S(2)}) copy-start(bf16[384,384]{1,0:T(8,128)(2,1)} %refs_2_.1) | copy-start | bytes 884740
  95.3 30.5 %copy-start.2 = (bf16[384,1536]{1,0:T(8,128)(2,1)S(1)}, bf16[384,1536]{1,0:T(8,128)(2,1)}, u32[]{:S(2)}) copy-start(bf16[384,1536]{1,0:T(8,128)(2,1)} %w_ref.7) | copy-start | bytes 3538948
  114.4 15.1 %collective-permute-start.6 = (bf16[1,384]{1,0:T(2,128)(2,1)S(1)}, bf16[1,384]{1,0:T(2,128)(2,1)S(1)}, u32[]{:S(2)}, u32[]{:S(2)}) collective-permute-start(bf16[1,384]{1,0:T(2,128)(2,1)S(1)} %slice_bitcast_fusion.2), channel_id=1, source_target_pairs={{0,9},{1,10},{2,11},{3,12},{4,13},{5,14},{6,15},{8,17},{9,18},{10,... | collective-permute-start | bytes 2312 | tf_op jit(solution)/shard_map/ppermute | solution.py:535
  119.4 10.1 %collective-permute-start.5 = (bf16[16,384]{1,0:T(8,128)(2,1)S(1)}, bf16[16,384]{1,0:T(8,128)(2,1)S(1)}, u32[]{:S(2)}, u32[]{:S(2)}) collective-permute-start(bf16[16,384]{1,0:T(8,128)(2,1)S(1)} %bitcast.47), channel_id=1, source_target_pairs={{0,1},{1,2},{2,3},{3,4},{4,5},{5,6},{6,7},{8,9},{9,10},{10,11},{11... | collective-permute-start | bytes 36872 | tf_op jit(solution)/shard_map/ppermute | solution.py:524
  123.8 5.8 %copy-start.18 = (bf16[1536,96]{0,1:T(8,128)(2,1)S(1)}, bf16[1536,96]{0,1:T(8,128)(2,1)}, u32[]{:S(2)}) copy-start(bf16[1536,96]{0,1:T(8,128)(2,1)} %param.36) | copy-start | bytes 884740
  123.8 5.8 %copy-start.21 = (bf16[9,1536]{1,0:T(8,128)(2,1)S(1)}, bf16[9,1536]{1,0:T(8,128)(2,1)}, u32[]{:S(2)}) copy-start(bf16[9,1536]{1,0:T(8,128)(2,1)} %taps_ref.3) | copy-start | bytes 82948
  123.8 5.7 %collective-permute-start.4 = (bf16[64,384]{1,0:T(8,128)(2,1)S(1)}, bf16[64,384]{1,0:T(8,128)(2,1)S(1)}, u32[]{:S(2)}, u32[]{:S(2)}) collective-permute-start(bf16[64,384]{1,0:T(8,128)(2,1)S(1)} %bitcast.44), channel_id=1, source_target_pairs={{0,8},{8,16},{16,24},{24,32},{32,40},{40,48},{48,56},{56,64},{64,7... | collective-permute-start | bytes 147464 | tf_op jit(solution)/shard_map/ppermute | solution.py:524
  129.5 19.1 %copy-start.5 = (bf16[1536,768]{1,0:T(8,128)(2,1)S(1)}, bf16[1536,768]{1,0:T(8,128)(2,1)}, u32[]{:S(2)}) copy-start(bf16[1536,768]{1,0:T(8,128)(2,1)} %refs_4_.5) | copy-start | bytes 7077892
  129.5 19.1 %copy-start.13 = (bf16[384,768]{1,0:T(8,128)(2,1)S(1)}, bf16[384,768]{1,0:T(8,128)(2,1)}, u32[]{:S(2)}) copy-start(bf16[384,768]{1,0:T(8,128)(2,1)} %refs_5_.3) | copy-start | bytes 1769476
  129.6 19.1 %copy-start.19 = (bf16[96,1536]{1,0:T(8,128)(2,1)S(1)}, bf16[96,1536]{1,0:T(8,128)(2,1)}, u32[]{:S(2)}) copy-start(bf16[96,1536]{1,0:T(8,128)(2,1)} %refs_3_.5) | copy-start | bytes 884740

commit v3 on v2

--- a/solution.py
+++ b/solution.py
@@ -26,21 +26,28 @@
     return pltpu.CompilerParams(vmem_limit_bytes=megabytes << 20)
 
 
+def in_hbm(x):
+    return pltpu.with_memory_space_constraint(x, pltpu.HBM)
+
+
 def cost(flops, moved):
     return pl.CostEstimate(flops=int(flops), bytes_accessed=int(moved), transcendentals=0)
 
 
-def gelu(x):
-    half = 0.5 * x
-    inner = x * (0.7978845608028654 + 0.035677408136300125 * (x * x))
-    return half + half * jnp.tanh(inner)
-
-
-def layer_norm(x):
+def gelu_twice(h):
+    inner = h * (1.5957691216057308 + 0.285419265090401 * (h * h))
+    return h + h * jnp.tanh(inner)
+
+
+def layer_norm(x, scale=1.0):
     average = jnp.mean(x, axis=-1, keepdims=True)
     centred = x - average
     spread = jnp.mean(centred * centred, axis=-1, keepdims=True)
-    return centred * lax.rsqrt(spread + epsilon)
+    return centred * (scale * lax.rsqrt(spread + epsilon))
+
+
+def half_norm(x):
+    return layer_norm(x, 0.5)
 
 
 def dot(a, b):
@@ -82,31 +89,37 @@
 
 
 def expand_kernel(x_ref, w_ref, out_ref):
-    normed = layer_norm(x_ref[...].astype(F32)).astype(BF16)
+    rows, cols, channels = x_ref.shape
+    normed = half_norm(x_ref[...].reshape(rows * cols, channels).astype(F32)).astype(BF16)
     for c in range(0, w_ref.shape[1], 512):
-        out_ref[:, c : c + 512] = gelu(dot(normed, w_ref[:, c : c + 512])).astype(BF16)
-
-
-def expand(x, weight, block=256):
-    cells, channels = x.shape
+        hidden = gelu_twice(dot(normed, w_ref[:, c : c + 512])).astype(BF16)
+        out_ref[:, :, c : c + 512] = hidden.reshape(rows, cols, 512)
+
+
+def expand(image, weight, first, count, block=4):
+    _, cols, channels = image.shape
     hidden = weight.shape[1]
     return pl.pallas_call(
         expand_kernel,
-        grid=(cells // block,),
+        grid=(count // block,),
         in_specs=[
-            pl.BlockSpec((block, channels), lambda i: (i, 0)),
+            pl.BlockSpec((block, cols, channels), lambda i: (first // block + i, 0, 0)),
             pl.BlockSpec((channels, hidden), lambda i: (0, 0)),
         ],
-        out_specs=pl.BlockSpec((block, hidden), lambda i: (i, 0)),
-        out_shape=jax.ShapeDtypeStruct((cells, hidden), BF16),
+        out_specs=pl.BlockSpec((block, cols, hidden), lambda i: (i, 0, 0)),
+        out_shape=jax.ShapeDtypeStruct((count, cols, hidden), BF16),
         compiler_params=params(16),
-        cost_estimate=cost(2 * cells * channels * hidden, 2 * cells * (channels + hidden)),
+        cost_estimate=cost(2 * count * cols * channels * hidden, 2 * count * cols * hidden),
         name="expand",
-    )(x, weight)
+    )(in_hbm(image), in_hbm(weight))
+
+
+def flag(held):
+    return jnp.where(held, 1.0, 0.0).astype(F32)
 
 
 def rim_of(normed, w_ref, rim, slot):
-    rim[slot] = gelu(dot(normed[...], w_ref[...])).astype(BF16).astype(F32)
+    rim[slot] = gelu_twice(dot(normed[...], w_ref[...])).astype(BF16).astype(F32)
 
 
 def squeeze_sums(sums, red_ref, part_ref):
@@ -115,19 +128,29 @@
 
 
 def conv_kernel(
-    hid_ref, over_ref, pair_ref, left_ref, right_ref, first_ref, w_ref, taps_ref, red_ref,
-    act_ref, part_ref, normed, rim, left, right, sums,
+    upper_ref, lower_ref, over_ref, pair_ref, left_ref, right_ref, first_ref, w_ref, taps_ref,
+    red_ref, act_ref, part_ref, normed, rim, left, right, sums,
 ):
     step = pl.program_id(0)
     core = lax.axis_index("core")
-    rows, cols, chunk = hid_ref.shape
+    rows, cols, chunk = act_ref.shape
     slot = step % 2
 
     @pl.when(step == 0)
     def _():
-        for ref, start in ((over_ref, 0), (pair_ref, 80), (left_ref, 160), (right_ref, 176)):
+        row, col = lax.axis_index("row_pair"), lax.axis_index("cols")
+        has_over = flag(row + core > 0) * flag(row - (1 - core) < lax.axis_size("row_pair") - 1)
+        has_left, has_right = flag(col > 0), flag(col < lax.axis_size("cols") - 1)
+        cell = lax.broadcasted_iota(jnp.int32, (80, 1), 0)
+        corners = jnp.where(cell == cols, has_left, jnp.where(cell == cols + 1, has_right, 1.0))
+        for ref, start, held in (
+            (over_ref, 0, corners * has_over),
+            (pair_ref, 80, corners),
+            (left_ref, 160, has_left),
+            (right_ref, 176, has_right),
+        ):
             size = ref.shape[0]
-            normed[start : start + size, :] = layer_norm(ref[...].astype(F32)).astype(BF16)
+            normed[start : start + size, :] = (half_norm(ref[...].astype(F32)) * held).astype(BF16)
         rim_of(normed, first_ref, rim, 0)
 
     top, bottom = core * 80, (1 - core) * 80
@@ -138,25 +161,27 @@
     place = lax.broadcasted_iota(jnp.int32, (8, 128), 0)
     for lane in range(0, chunk, 128):
         lanes = slice(lane, lane + 128)
-        taps = [taps_ref[t : t + 1, lanes].astype(F32) for t in range(9)]
+        taps = [0.5 * taps_ref[t : t + 1, lanes].astype(F32) for t in range(9)]
+        short = [tap.astype(BF16) for tap in taps]
         before = sum(taps[3 * a] * left[a : a + rows, lanes] for a in range(3))
         after = sum(taps[3 * a + 2] * right[a : a + rows, lanes] for a in range(3))
         total = jnp.zeros((8, 128), F32)
 
         def line(r):
             if r < 0:
-                return rim[slot, pl.ds(pl.multiple_of(top, 8), 64), lanes]
+                return rim[slot, pl.ds(pl.multiple_of(top, 8), 64), lanes].astype(BF16)
             if r == rows:
-                return rim[slot, pl.ds(pl.multiple_of(bottom, 8), 64), lanes]
-            return hid_ref[r, :, lanes].astype(F32)
+                return rim[slot, pl.ds(pl.multiple_of(bottom, 8), 64), lanes].astype(BF16)
+            return upper_ref[r, :, lanes] if r < rows // 2 else lower_ref[r - rows // 2, :, lanes]
 
         window = [line(-1), line(0), None]
         for r in range(rows):
             window[2] = line(r + 1)
             one = [
-                taps[b] * window[0] + taps[3 + b] * window[1] + taps[6 + b] * window[2]
+                short[b] * window[0] + short[3 + b] * window[1] + short[6 + b] * window[2]
                 for b in range(3)
             ]
+            one = [line_sum.astype(F32) for line_sum in one]
             down = pltpu.roll(one[0], 1, 0)
             up = pltpu.roll(one[2], cols - 1, 0)
             first = jnp.where(place == 0, before[r : r + 1], down[0:8])
@@ -166,7 +191,7 @@
                 + jnp.concatenate([first, down[8:]], 0)
                 + jnp.concatenate([up[: cols - 8], last], 0)
             )
-            act = gelu(whole)
+            act = gelu_twice(whole)
             act_ref[r, :, lanes] = act.astype(BF16)
             for s in range(0, cols, 8):
                 total = total + act[s : s + 8]
@@ -179,8 +204,9 @@
         squeeze_sums(sums, red_ref, part_ref)
 
 
-def conv(hidden, over, pair, left, right, weight, taps, reduce, copies, chunk=256):
-    rows, cols, width = hidden.shape
+def conv(upper, lower, over, pair, left, right, weight, taps, reduce, copies, chunk=256):
+    rows, cols, width = upper.shape
+    rows = 2 * rows
     channels = weight.shape[0]
     squeezed = reduce.shape[0]
     steps = width // chunk
@@ -189,7 +215,8 @@
         conv_kernel,
         grid=(steps,),
         in_specs=[
-            pl.BlockSpec((rows, cols, chunk), lambda c: (0, 0, c)),
+            pl.BlockSpec((rows // 2, cols, chunk), lambda c: (0, 0, c)),
+            pl.BlockSpec((rows // 2, cols, chunk), lambda c: (0, 0, c)),
             whole(over),
             whole(pair),
             whole(left),
@@ -216,7 +243,7 @@
         ],
         compiler_params=params(20),
         name="conv",
-    )(hidden, over, pair, left, right, weight, weight, taps, reduce)
+    )(upper, lower, over, pair, left, right, weight, weight, taps, reduce)
 
 
 def gate_of(parts_ref, restore_ref, cell_count):
@@ -260,9 +287,9 @@
             quads.append(picked)
         groups.append(jnp.concatenate(quads, 1).astype(BF16))
     x = x + dot(jnp.concatenate(groups, 0), out_ref[...])
-    normed = layer_norm(x).astype(BF16)
+    normed = half_norm(x).astype(BF16)
     for c in range(0, up_ref.shape[1], 512):
-        hidden = gelu(dot(normed, up_ref[:, c : c + 512])).astype(BF16)
+        hidden = gelu_twice(dot(normed, up_ref[:, c : c + 512])).astype(BF16)
         x = x + dot(hidden, down_ref[c : c + 512, :])
     return x
 
@@ -364,14 +391,15 @@
     )(x, *weights)
 
 
-def down_expand_kernel(x_ref, w_ref, out_ref, cells):
+def down_expand_kernel(x_ref, w_ref, out_ref, same_ref, cells):
     rows, cols, channels = x_ref.shape
+    same_ref[...] = x_ref[...]
     put(cells, x_ref[...].reshape(rows * cols, channels).astype(F32))
     half = rows * cols // 2
     x = jnp.concatenate([take_strided(cells, parity, half, 2) for parity in range(2)], 0)
-    normed = layer_norm(x).astype(BF16)
+    normed = half_norm(x).astype(BF16)
     for c in range(0, w_ref.shape[1], 512):
-        hidden = gelu(dot(normed, w_ref[:, c : c + 512])).astype(BF16)
+        hidden = gelu_twice(dot(normed, w_ref[:, c : c + 512])).astype(BF16)
         for parity in range(2):
             out_ref[:, parity, :, c : c + 512] = hidden[parity * half : (parity + 1) * half].reshape(
                 rows, cols // 2, 512
@@ -388,8 +416,14 @@
             pl.BlockSpec((block, cols, channels), lambda i: (i, 0, 0)),
             pl.BlockSpec((channels, hidden), lambda i: (0, 0)),
         ],
-        out_specs=pl.BlockSpec((block, 2, cols // 2, hidden), lambda i: (i, 0, 0, 0)),
-        out_shape=jax.ShapeDtypeStruct((rows, 2, cols // 2, hidden), BF16),
+        out_specs=[
+            pl.BlockSpec((block, 2, cols // 2, hidden), lambda i: (i, 0, 0, 0)),
+            pl.BlockSpec((block, cols, channels), lambda i: (i, 0, 0)),
+        ],
+        out_shape=[
+            jax.ShapeDtypeStruct((rows, 2, cols // 2, hidden), BF16),
+            jax.ShapeDtypeStruct(x.shape, BF16),
+        ],
         scratch_shapes=[panels(block * cols, channels)],
         compiler_params=params(16),
         cost_estimate=cost(2 * rows * cols * channels * hidden, 2 * rows * cols * hidden),
@@ -407,11 +441,13 @@
 
     @pl.when(step == 0)
     def _():
-        put(cells, layer_norm(upper_ref[...].astype(F32)))
+        row, col = lax.axis_index("row_pair") + lax.axis_index("core"), lax.axis_index("cols")
+        has_upper, has_left = flag(row > 0), flag(col > 0)
+        put(cells, half_norm(upper_ref[...].astype(F32)) * has_upper)
         normed[0:32, :] = take_strided(cells, 0, 32, 2).astype(BF16)
         normed[32:64, :] = take_strided(cells, 1, 32, 2).astype(BF16)
-        normed[64:80, :] = layer_norm(left_ref[...].astype(F32)).astype(BF16)
-        corner = layer_norm(corner_ref[...].astype(F32))
+        normed[64:80, :] = (half_norm(left_ref[...].astype(F32)) * has_left).astype(BF16)
+        corner = half_norm(corner_ref[...].astype(F32)) * (has_upper * has_left)
         normed[80:96, :] = jnp.broadcast_to(corner, (16, corner.shape[1])).astype(BF16)
         rim_of(normed, first_ref, rim, 0)
 
@@ -420,7 +456,7 @@
     place = lax.broadcasted_iota(jnp.int32, (8, 128), 0)
     for lane in range(0, chunk, 128):
         lanes = slice(lane, lane + 128)
-        taps = [taps_ref[t : t + 1, lanes].astype(F32) for t in range(9)]
+        taps = [0.5 * taps_ref[t : t + 1, lanes].astype(F32) for t in range(9)]
         before = sum(taps[3 * a] * left[a : a + rows, lanes] for a in range(3))
         total = jnp.zeros((8, 128), F32)
 
@@ -436,7 +472,7 @@
             whole = sum(taps[3 * a + 1] * even[a] + taps[3 * a + 2] * odd[a] for a in range(3))
             shifted = pltpu.roll(shifted, 1, 0)
             first = jnp.where(place == 0, before[2 * p : 2 * p + 1], shifted[0:8])
-            act = gelu(whole + jnp.concatenate([first, shifted[8:]], 0))
+            act = gelu_twice(whole + jnp.concatenate([first, shifted[8:]], 0))
             act_ref[p, :, lanes] = act.astype(BF16)
             for s in range(0, cols, 8):
                 total = total + act[s : s + 8]
@@ -520,17 +556,15 @@
 
 def shift(x, axes, by):
     size = lax.axis_size(axes)
-    pairs = [(i, i + by) for i in range(size) if 0 <= i + by < size]
-    return lax.ppermute(x, axes, pairs)
-
-
-def shift_both(x, by_rows, by_cols):
+    return lax.ppermute(x, axes, [(i, (i + by) % size) for i in range(size)])
+
+
+def shift_both(x):
     rows, cols = lax.axis_size(ROWS), lax.axis_size("cols")
     pairs = [
-        (r * cols + c, (r + by_rows) * cols + c + by_cols)
+        (r * cols + c, (r + 1) % rows * cols + (c + 1) % cols)
         for r in range(rows)
         for c in range(cols)
-        if 0 <= r + by_rows < rows and 0 <= c + by_cols < cols
     ]
     return lax.ppermute(x, ALL, pairs)
 
@@ -551,7 +585,7 @@
     even = lax.axis_index("core") == 0
     away = jnp.where(even, first, last)
     near = jnp.where(even, last, first)
-    pairs = [(r, r - 1 if r % 2 == 0 else r + 1) for r in range(1, size - 1)]
+    pairs = [(r, (r - 1 if r % 2 == 0 else r + 1) % size) for r in range(size)]
     over = lax.ppermute(away, ROWS, pairs)
     pair = lax.ppermute(near, "core", [(0, 1), (1, 0)])
     return over, pair
@@ -585,10 +619,12 @@
 
     left = shift(image[:, cols - 1], "cols", 1)
     right = shift(image[:, 0], "cols", -1)
-    hidden = expand(image.reshape(rows * cols, channels), mb_expand)
+    upper = expand(image, mb_expand, 0, rows // 2)
+    left, right, upper = lax.optimization_barrier((left, right, upper))
     over, pair = row_rims(image, left, right)
+    lower = expand(image, mb_expand, rows // 2, rows // 2)
     act, part = conv(
-        hidden.reshape(rows, cols, -1), over, pair, left, right, mb_expand, mb_taps, mb_reduce.T,
+        upper, lower, over, pair, left, right, mb_expand, mb_taps, mb_reduce.T,
         lax.axis_size(ALL),
     )
     parts = sum_parts(part)
@@ -606,8 +642,8 @@
 
     upper = shift(section[rows - 1], ROWS, 1)
     left = shift(section[:, cols - 1], "cols", 1)
-    corner = shift_both(section[rows - 1, cols - 1 :], 1, 1)
-    hidden = down_expand_part(section, down_expand)
+    corner = shift_both(section[rows - 1, cols - 1 :])
+    hidden, section = down_expand_part(section, down_expand)
     act, part = down_conv(
         hidden, upper, left, corner, down_expand, down_taps, down_reduce.T, lax.axis_size(ALL)
     )

time: 152 us -> 139 us (0.914)
  starting transfers between devices: 23.7 us -> 15.3 us
  local copies, waits for them, and re-layouts: 5.37 us -> 2.09 us
  blocking collectives: 75.5 us -> 73.3 us
    ppermute x4, starting transfers between devices: 14 us -> 9.89 us  [shift(): return lax.ppermute(x, axes, [(i, (i + by) % size) for i in range(size)])]
    unnamed x48 -> x45, local copies, waits for them, and re-layouts: 3.41 us -> 0.14 us
    all_to_all x2, blocking collectives: 36.1 us -> 33.9 us  [sum_parts(): arrived = lax.all_to_all(part, ALL, split_axis=0, concat_axis=0, tiled=True)]
    ppermute x1, starting transfers between devices: 3.1 us -> 1.22 us  [row_rims(): over = lax.ppermute(away, ROWS, pairs)]
    ppermute x1, starting transfers between devices: 4.99 us -> 3.15 us  [shift_both(): return lax.ppermute(x, ALL, pairs)]
    pallas_call x2 -> x3, Pallas kernels: 12.8 us -> 14 us  [the longest x1 7.86 us: conv(): pl.pallas_call(conv_kernel, grid=(steps,), in_specs=[pl.BlockSpec((rows /...]
  transfers between devices with their start and end apart: 7 -> 7, of which waited for: 0 -> 0; matrix products, arithmetic and copies ran while one was open for 1% -> 1% of each run, Pallas kernels for 5% -> 7%
where the time goes in v3:
time: 139 us
  blocking collectives  73.3 us (53%)
  Pallas kernels  47 us (34%)
  starting transfers between devices  15.3 us (11%)
  local copies, waits for them, and re-layouts  2.09 us (2%)
    all_to_all x2, blocking collectives, sum_parts(): arrived = lax.all_to_all(part, ALL, split_axis=0, concat_axis=0, tiled=True)  33.9 us
    all_to_all x1, blocking collectives, local(): lax.all_to_all(mixed.reshape(sharers, held, channels), CLASS, split_axis=...  20.4 us
    all_to_all x1, blocking collectives, local(): lax.all_to_all(grouped, CLASS, split_axis=0, concat_axis=0, tiled=True)  19 us
    pallas_call x1, Pallas kernels, block_part(): pl.pallas_call(kernel, grid=(rows // WIN * across,), in_specs=[pl.BlockSp...  12.1 us
    pallas_call x1, Pallas kernels, grid_part(): pl.pallas_call(kernel, grid=(held // groups,), in_specs=[pl.BlockSpec(x.s...  11 us
    ppermute x4, starting transfers between devices, shift(): return lax.ppermute(x, axes, [(i, (i + by) % size) for i in range(size)])  9.89 us
    pallas_call x1, Pallas kernels, conv(): pl.pallas_call(conv_kernel, grid=(steps,), in_specs=[pl.BlockSpec((rows /...  7.86 us
    pallas_call x2, Pallas kernels, expand(): pl.pallas_call(expand_kernel, grid=(count // block,), in_specs=[pl.BlockS...  6.19 us
  transfers between devices with their start and end apart: 7, of which 0 were waited for; matrix products, arithmetic and copies ran while one was open for 1% of the time, Pallas kernels for 7%

profile of v3, /device:TPU:1, one launch (start us, length us, event | category | flops | bytes accessed | tf_op | source)
XLA Modules:
  0.0 138.7 jit_solution(16882738831179539296)
XLA Ops:
  0.6 1.0 fusion
  1.6 3.8 %collective-permute-start = (bf16[16,384]{1,0:T(8,128)(2,1)S(1)}, bf16[16,384]{1,0:T(8,128)(2,1)S(1)}, u32[]{:S(2)}, u32[]{:S(2)}) collective-permute-start(bf16[16,384]{1,0:T(8,128)(2,1)S(1)} %bitcast.39), channel_id=1, source_target_pairs={{0,1},{1,2},{2,3},{3,4},{4,5},{5,6},{6,7},{7,0},{8,9},{9,10},{10,1... | collective-permute-start | bytes 36872 | tf_op jit(solution)/shard_map/ppermute | solution.py:559
  5.4 3.6 %collective-permute-start.1 = (bf16[16,384]{1,0:T(8,128)(2,1)S(1)}, bf16[16,384]{1,0:T(8,128)(2,1)S(1)}, u32[]{:S(2)}, u32[]{:S(2)}) collective-permute-start(bf16[16,384]{1,0:T(8,128)(2,1)S(1)} %bitcast.40), channel_id=1, source_target_pairs={{0,7},{1,0},{2,1},{3,2},{4,3},{5,4},{6,5},{7,6},{8,15},{9,8},{10,9... | collective-permute-start | bytes 36872 | tf_op jit(solution)/shard_map/ppermute | solution.py:559
  9.0 0.8 slice_bitcast_fusion.1
  9.8 3.1 %expand.2.upper_ref = bf16[8,64,1536]{2,1,0:T(8,128)(2,1)S(1)} custom-call(bf16[16,64,384]{2,1,0:T(8,128)(2,1)} %refs_0_.1, bf16[384,1536]{1,0:T(8,128)(2,1)} %w_ref.7), custom_call_target="tpu_custom_call" | custom-call | flops 603979776 | bytes 1572864 | tf_op jit(solution)/shard_map/expand/pallas_call | solution.py:102
  13.0 0.1 pad.7.clone
  13.0 0.0 collective-permute-done.left_ref
  13.1 0.0 collective-permute-done.1.right_ref
  13.1 0.1 broadcast_select_fusion
  13.2 1.0 collective-permute-start.3
  14.2 1.2 collective-permute-start.2
  15.4 3.1 %expand.3.lower_ref = bf16[8,64,1536]{2,1,0:T(8,128)(2,1)S(1)} custom-call(bf16[16,64,384]{2,1,0:T(8,128)(2,1)} %refs_0_.1, bf16[384,1536]{1,0:T(8,128)(2,1)} %w_ref.7), custom_call_target="tpu_custom_call" | custom-call | flops 603979776 | bytes 1572864 | tf_op jit(solution)/shard_map/expand/pallas_call | solution.py:102
  18.5 0.0 collective-permute-done.3.pair_ref
  18.5 0.0 collective-permute-done.2.over_ref
  18.6 0.0 copy-done
  18.6 0.0 copy-done.13
  18.6 0.0 copy-done.19
  18.6 0.0 copy-start.1
  18.6 0.0 copy-start.4
  18.6 0.0 copy-start.5
  18.6 0.0 copy-start.6
  18.6 0.0 copy-start.9
  18.6 0.0 copy-start.14
  18.7 0.0 copy-start.15
  18.7 7.9 %conv.1 = (bf16[16,64,1536]{2,1,0:T(8,128)(2,1)S(1)}, f32[128,96]{1,0:T(8,128)S(1)}) custom-call(bf16[8,64,1536]{2,1,0:T(8,128)(2,1)S(1)} %expand.2.upper_ref, bf16[8,64,1536]{2,1,0:T(8,128)(2,1)S(1)} %expand.3.lower_ref, bf16[80,384]{1,0:T(8,128)(2,1)S(1)} %collective-permute-done.2.over_ref, bf16[80,384]{1,0:T(8,128)(2,1)S(1)} %collective-permute-done.3.pair_ref, ...), custom_call_target="tpu_custom_call" | custom-call | tf_op jit(solution)/shard_map/conv/pallas_call | solution.py:214
  26.5 17.7 %all_to_all.20 = f32[128,1,96]{2,1,0:T(1,128)S(1)} all-to-all(f32[128,1,96]{2,1,0:T(1,128)S(1)} %bitcast.36), channel_id=1, replica_groups=mesh['row_pair'=8,'core'=2,'cols'=8] {'row_pair','core','cols'}, dimensions={0} | all-to-all | bytes 98304 | tf_op jit(solution)/shard_map/all_to_all | solution.py:575
  44.2 0.0 copy-done.1
  44.2 0.0 copy-done.4
  44.2 0.0 copy-done.5
  44.2 0.0 copy-done.6
  44.3 0.0 copy-done.9
  44.3 0.0 copy-done.14
  44.3 0.0 copy-done.15
  44.3 0.0 copy-start.8
  44.3 0.0 copy-start.10
  44.3 12.1 %block_part.1 = bf16[16,64,384]{2,1,0:T(8,128)(2,1)S(1)} custom-call(bf16[16,64,384]{2,1,0:T(8,128)(2,1)S(1)} %copy-done.1, bf16[16,64,1536]{2,1,0:T(8,128)(2,1)S(1)} %get-tuple-element.14.refs_1_, f32[128,96]{1,0:T(8,128)S(1)} %bitcast.35, bf16[96,1536]{1,0:T(8,128)(2,1)S(1)} %copy-done.14, bf16[1536,384]{1,0:T(8,128)(2,1)S(1)} %copy-done.4, ...), custom_call_target="tpu_custom_call" | custom-call | tf_op jit(solution)/shard_map/block_part/pallas_call | solution.py:331
  56.4 0.0 copy-start.7
  56.4 0.0 copy-start.16
  56.5 20.4 %all_to_all.21.refs_0_ = bf16[64,16,384]{2,1,0:T(8,128)(2,1)S(1)} all-to-all(bf16[64,16,384]{2,1,0:T(8,128)(2,1)S(1)} %bitcast.28), channel_id=1, replica_groups=mesh['row_pair'=8,'core'=2,'cols'=8] {'row_pair','cols'}, dimensions={0} | all-to-all | bytes 1572864 | tf_op jit(solution)/shard_map/all_to_all | solution.py:636
  76.8 0.0 copy-done.8
  76.8 0.0 copy-done.10
  76.8 0.0 copy-done.7
  76.8 0.0 copy-done.16
  76.8 11.0 %grid_part.1 = bf16[64,16,384]{2,1,0:T(8,128)(2,1)S(1)} custom-call(bf16[64,16,384]{2,1,0:T(8,128)(2,1)S(1)} %all_to_all.21.refs_0_, bf16[384,1152]{1,0:T(8,128)(2,1)S(1)} %copy-done.10, bf16[384,384]{1,0:T(8,128)(2,1)S(1)} %copy-done.16, bf16[384,1536]{1,0:T(8,128)(2,1)S(1)} %copy-done.7, bf16[1536,384]{1,0:T(8,128)(2,1)S(1)} %copy-done.8), custom_call_target="tpu_custom_call" | custom-call | tf_op jit(solution)/shard_map/grid_part/pallas_call | solution.py:376
  87.8 0.0 copy-start.2
  87.9 19.0 %all_to_all.22 = bf16[64,16,384]{2,1,0:T(8,128)(2,1)S(1)} all-to-all(bf16[64,16,384]{2,1,0:T(8,128)(2,1)S(1)} %grid_part.1), channel_id=1, replica_groups=mesh['row_pair'=8,'core'=2,'cols'=8] {'row_pair','cols'}, dimensions={0} | all-to-all | bytes 1572864 | tf_op jit(solution)/shard_map/all_to_all | solution.py:640
  106.9 3.2 %collective-permute-start.6 = (bf16[1,384]{1,0:T(2,128)(2,1)S(1)}, bf16[1,384]{1,0:T(2,128)(2,1)S(1)}, u32[]{:S(2)}, u32[]{:S(2)}) collective-permute-start(bf16[1,384]{1,0:T(2,128)(2,1)S(1)} %slice_bitcast_fusion.2), channel_id=1, source_target_pairs={{0,9},{1,10},{2,11},{3,12},{4,13},{5,14},{6,15},{7,8},{8,17},{9,18... | collective-permute-start | bytes 2312 | tf_op jit(solution)/shard_map/ppermute | solution.py:569
  110.1 2.4 %collective-permute-start.5 = (bf16[16,384]{1,0:T(8,128)(2,1)S(1)}, bf16[16,384]{1,0:T(8,128)(2,1)S(1)}, u32[]{:S(2)}, u32[]{:S(2)}) collective-permute-start(bf16[16,384]{1,0:T(8,128)(2,1)S(1)} %bitcast.41), channel_id=1, source_target_pairs={{0,1},{1,2},{2,3},{3,4},{4,5},{5,6},{6,7},{7,0},{8,9},{9,10},{10,1... | collective-permute-start | bytes 36872 | tf_op jit(solution)/shard_map/ppermute | solution.py:559
  112.5 0.0 copy-start.20
  112.5 0.1 collective-permute-start.4
  112.6 4.1 %down_expand.1 = (bf16[16,2,32,1536]{3,2,1,0:T(8,128)(2,1)S(1)}, bf16[16,64,384]{2,1,0:T(8,128)(2,1)}) custom-call(bf16[16,64,384]{2,1,0:T(8,128)(2,1)S(1)} %bitcast.31, bf16[384,1536]{1,0:T(8,128)(2,1)S(1)} %copy-done.2), custom_call_target="tpu_custom_call" | custom-call | flops 1207959552 | bytes 3145728 | tf_op jit(solution)/shard_map/down_expand/pallas_call | solution.py:412
  116.7 0.0 collective-permute-done.6.corner_ref
  116.7 0.0 collective-permute-done.5.left_ref
  116.7 0.0 collective-permute-done.4.upper_ref
  116.8 0.0 copy-done.17
  116.8 0.0 copy-done.20
  116.8 0.0 copy-start.3
  116.8 0.0 copy-start.11
  116.8 0.0 copy-start.12
  116.8 0.0 copy-start.18
  116.8 3.8 %down_conv.1 = (bf16[8,32,1536]{2,1,0:T(8,128)(2,1)S(1)}, f32[128,96]{1,0:T(8,128)S(1)}) custom-call(bf16[16,2,32,1536]{3,2,1,0:T(8,128)(2,1)S(1)} %get-tuple-element.17.hid_ref, bf16[64,384]{1,0:T(8,128)(2,1)S(1)} %collective-permute-done.4.upper_ref, bf16[16,384]{1,0:T(8,128)(2,1)S(1)} %collective-permute-done.5.left_ref, ...), custom_call_target="tpu_custom_call" | custom-call | tf_op jit(solution)/shard_map/down_conv/pallas_call | solution.py:493
  120.6 16.2 %all_to_all.23 = f32[128,1,96]{2,1,0:T(1,128)S(1)} all-to-all(f32[128,1,96]{2,1,0:T(1,128)S(1)} %bitcast.37), channel_id=1, replica_groups=mesh['row_pair'=8,'core'=2,'cols'=8] {'row_pair','core','cols'}, dimensions={0} | all-to-all | bytes 98304 | tf_op jit(solution)/shard_map/all_to_all | solution.py:575
  136.8 0.0 copy-done.12
  136.8 1.9 %down_out.1 = bf16[8,32,768]{2,1,0:T(8,128)(2,1)} custom-call(bf16[8,32,1536]{2,1,0:T(8,128)(2,1)S(1)} %get-tuple-element.18.refs_0_, bf16[16,64,384]{2,1,0:T(8,128)(2,1)S(1)} %copy-done.11, f32[128,96]{1,0:T(8,128)S(1)} %bitcast.34, bf16[96,1536]{1,0:T(8,128)(2,1)S(1)} %copy-done.18, bf16[1536,768]{1,0:T(8,128)(2,1)S(1)} %copy-done.3, ...), custom_call_target="tpu_custom_call" | custom-call | tf_op jit(solution)/shard_map/down_out/pallas_call | solution.py:548
  (16 shorter events, 0.1 us)
Async XLA Ops:
  1.6 11.4 %collective-permute-start = (bf16[16,384]{1,0:T(8,128)(2,1)S(1)}, bf16[16,384]{1,0:T(8,128)(2,1)S(1)}, u32[]{:S(2)}, u32[]{:S(2)}) collective-permute-start(bf16[16,384]{1,0:T(8,128)(2,1)S(1)} %bitcast.39), channel_id=1, source_target_pairs={{0,1},{1,2},{2,3},{3,4},{4,5},{5,6},{6,7},{7,0},{8,9},{9,10},{10,1... | collective-permute-start | bytes 36872 | tf_op jit(solution)/shard_map/ppermute | solution.py:559
  5.4 7.6 %collective-permute-start.1 = (bf16[16,384]{1,0:T(8,128)(2,1)S(1)}, bf16[16,384]{1,0:T(8,128)(2,1)S(1)}, u32[]{:S(2)}, u32[]{:S(2)}) collective-permute-start(bf16[16,384]{1,0:T(8,128)(2,1)S(1)} %bitcast.40), channel_id=1, source_target_pairs={{0,7},{1,0},{2,1},{3,2},{4,3},{5,4},{6,5},{7,6},{8,15},{9,8},{10,9... | collective-permute-start | bytes 36872 | tf_op jit(solution)/shard_map/ppermute | solution.py:559
  13.2 5.4 %collective-permute-start.3 = (bf16[80,384]{1,0:T(8,128)(2,1)S(1)}, bf16[80,384]{1,0:T(8,128)(2,1)S(1)}, u32[]{:S(2)}, u32[]{:S(2)}) collective-permute-start(bf16[80,384]{1,0:T(8,128)(2,1)S(1)} %get-tuple-element.24), channel_id=1, source_target_pairs={{0,8},{8,0},{1,9},{9,1},{2,10},{10,2},{3,11},{11,3},{4,12},{12,4},... | collective-permute-start | bytes 184328 | tf_op jit(solution)/shard_map/ppermute | solution.py:590
  14.2 4.3 %copy-start = (bf16[384,1536]{1,0:T(8,128)(2,1)S(1)}, bf16[384,1536]{1,0:T(8,128)(2,1)}, u32[]{:S(2)}) copy-start(bf16[384,1536]{1,0:T(8,128)(2,1)} %w_ref.7) | copy-start | bytes 3538948
  14.2 4.4 %copy-start.13 = (bf16[1536,96]{0,1:T(8,128)(2,1)S(1)}, bf16[1536,96]{0,1:T(8,128)(2,1)}, u32[]{:S(2)}) copy-start(bf16[1536,96]{0,1:T(8,128)(2,1)} %param.23) | copy-start | bytes 884740
  14.2 4.4 %copy-start.19 = (bf16[9,1536]{1,0:T(8,128)(2,1)S(1)}, bf16[9,1536]{1,0:T(8,128)(2,1)}, u32[]{:S(2)}) copy-start(bf16[9,1536]{1,0:T(8,128)(2,1)} %taps_ref.2) | copy-start | bytes 82948
  14.2 4.3 %collective-permute-start.2 = (bf16[80,384]{1,0:T(8,128)(2,1)S(1)}, bf16[80,384]{1,0:T(8,128)(2,1)S(1)}, u32[]{:S(2)}, u32[]{:S(2)}) collective-permute-start(bf16[80,384]{1,0:T(8,128)(2,1)S(1)} %get-tuple-element.25), channel_id=1, source_target_pairs={{0,120},{8,16},{16,8},{24,32},{32,24},{40,48},{48,40},{56,64},{64,... | collective-permute-start | bytes 184328 | tf_op jit(solution)/shard_map/ppermute | solution.py:589
  18.6 25.7 %copy-start.1 = (bf16[16,64,384]{2,1,0:T(8,128)(2,1)S(1)}, bf16[16,64,384]{2,1,0:T(8,128)(2,1)}, u32[]{:S(2)}) copy-start(bf16[16,64,384]{2,1,0:T(8,128)(2,1)} %refs_0_.1) | copy-start | bytes 2359300
  18.6 25.6 %copy-start.4 = (bf16[1536,384]{1,0:T(8,128)(2,1)S(1)}, bf16[1536,384]{1,0:T(8,128)(2,1)}, u32[]{:S(2)}) copy-start(bf16[1536,384]{1,0:T(8,128)(2,1)} %refs_4_.3) | copy-start | bytes 3538948
  18.6 25.6 %copy-start.5 = (bf16[384,1536]{1,0:T(8,128)(2,1)S(1)}, bf16[384,1536]{1,0:T(8,128)(2,1)}, u32[]{:S(2)}) copy-start(bf16[384,1536]{1,0:T(8,128)(2,1)} %refs_7_.1) | copy-start | bytes 3538948
  18.6 25.6 %copy-start.6 = (bf16[1536,384]{1,0:T(8,128)(2,1)S(1)}, bf16[1536,384]{1,0:T(8,128)(2,1)}, u32[]{:S(2)}) copy-start(bf16[1536,384]{1,0:T(8,128)(2,1)} %refs_8_.1) | copy-start | bytes 3538948
  18.6 25.6 %copy-start.9 = (bf16[384,1152]{1,0:T(8,128)(2,1)S(1)}, bf16[384,1152]{1,0:T(8,128)(2,1)}, u32[]{:S(2)}) copy-start(bf16[384,1152]{1,0:T(8,128)(2,1)} %refs_5_.2) | copy-start | bytes 2654212
  18.6 25.6 %copy-start.14 = (bf16[96,1536]{1,0:T(8,128)(2,1)S(1)}, bf16[96,1536]{1,0:T(8,128)(2,1)}, u32[]{:S(2)}) copy-start(bf16[96,1536]{1,0:T(8,128)(2,1)} %refs_3_.3) | copy-start | bytes 884740
  18.7 25.6 %copy-start.15 = (bf16[384,384]{1,0:T(8,128)(2,1)S(1)}, bf16[384,384]{1,0:T(8,128)(2,1)}, u32[]{:S(2)}) copy-start(bf16[384,384]{1,0:T(8,128)(2,1)} %refs_6_.1) | copy-start | bytes 884740
  44.3 32.5 %copy-start.8 = (bf16[1536,384]{1,0:T(8,128)(2,1)S(1)}, bf16[1536,384]{1,0:T(8,128)(2,1)}, u32[]{:S(2)}) copy-start(bf16[1536,384]{1,0:T(8,128)(2,1)} %refs_4_.4) | copy-start | bytes 3538948
  44.3 32.5 %copy-start.10 = (bf16[384,1152]{1,0:T(8,128)(2,1)S(1)}, bf16[384,1152]{1,0:T(8,128)(2,1)}, u32[]{:S(2)}) copy-start(bf16[384,1152]{1,0:T(8,128)(2,1)} %refs_1_.1) | copy-start | bytes 2654212
  56.4 20.4 %copy-start.7 = (bf16[384,1536]{1,0:T(8,128)(2,1)S(1)}, bf16[384,1536]{1,0:T(8,128)(2,1)}, u32[]{:S(2)}) copy-start(bf16[384,1536]{1,0:T(8,128)(2,1)} %refs_3_.4) | copy-start | bytes 3538948
  56.4 20.4 %copy-start.16 = (bf16[384,384]{1,0:T(8,128)(2,1)S(1)}, bf16[384,384]{1,0:T(8,128)(2,1)}, u32[]{:S(2)}) copy-start(bf16[384,384]{1,0:T(8,128)(2,1)} %refs_2_.1) | copy-start | bytes 884740
  87.8 24.8 %copy-start.2 = (bf16[384,1536]{1,0:T(8,128)(2,1)S(1)}, bf16[384,1536]{1,0:T(8,128)(2,1)}, u32[]{:S(2)}) copy-start(bf16[384,1536]{1,0:T(8,128)(2,1)} %w_ref.9) | copy-start | bytes 3538948
  106.9 9.8 %collective-permute-start.6 = (bf16[1,384]{1,0:T(2,128)(2,1)S(1)}, bf16[1,384]{1,0:T(2,128)(2,1)S(1)}, u32[]{:S(2)}, u32[]{:S(2)}) collective-permute-start(bf16[1,384]{1,0:T(2,128)(2,1)S(1)} %slice_bitcast_fusion.2), channel_id=1, source_target_pairs={{0,9},{1,10},{2,11},{3,12},{4,13},{5,14},{6,15},{7,8},{8,17},{9,18... | collective-permute-start | bytes 2312 | tf_op jit(solution)/shard_map/ppermute | solution.py:569
  110.1 6.7 %collective-permute-start.5 = (bf16[16,384]{1,0:T(8,128)(2,1)S(1)}, bf16[16,384]{1,0:T(8,128)(2,1)S(1)}, u32[]{:S(2)}, u32[]{:S(2)}) collective-permute-start(bf16[16,384]{1,0:T(8,128)(2,1)S(1)} %bitcast.41), channel_id=1, source_target_pairs={{0,1},{1,2},{2,3},{3,4},{4,5},{5,6},{6,7},{7,0},{8,9},{9,10},{10,1... | collective-permute-start | bytes 36872 | tf_op jit(solution)/shard_map/ppermute | solution.py:559
  112.5 4.2 %copy-start.17 = (bf16[1536,96]{0,1:T(8,128)(2,1)S(1)}, bf16[1536,96]{0,1:T(8,128)(2,1)}, u32[]{:S(2)}) copy-start(bf16[1536,96]{0,1:T(8,128)(2,1)} %param.36) | copy-start | bytes 884740
  112.5 4.3 %copy-start.20 = (bf16[9,1536]{1,0:T(8,128)(2,1)S(1)}, bf16[9,1536]{1,0:T(8,128)(2,1)}, u32[]{:S(2)}) copy-start(bf16[9,1536]{1,0:T(8,128)(2,1)} %taps_ref.3) | copy-start | bytes 82948
  112.5 4.2 %collective-permute-start.4 = (bf16[64,384]{1,0:T(8,128)(2,1)S(1)}, bf16[64,384]{1,0:T(8,128)(2,1)S(1)}, u32[]{:S(2)}, u32[]{:S(2)}) collective-permute-start(bf16[64,384]{1,0:T(8,128)(2,1)S(1)} %bitcast.38), channel_id=1, source_target_pairs={{0,8},{8,16},{16,24},{24,32},{32,40},{40,48},{48,56},{56,64},{64,7... | collective-permute-start | bytes 147464 | tf_op jit(solution)/shard_map/ppermute | solution.py:559
  116.8 20.0 %copy-start.3 = (bf16[1536,768]{1,0:T(8,128)(2,1)S(1)}, bf16[1536,768]{1,0:T(8,128)(2,1)}, u32[]{:S(2)}) copy-start(bf16[1536,768]{1,0:T(8,128)(2,1)} %refs_4_.5) | copy-start | bytes 7077892
  116.8 20.0 %copy-start.11 = (bf16[16,64,384]{2,1,0:T(8,128)(2,1)S(1)}, bf16[16,64,384]{2,1,0:T(8,128)(2,1)}, u32[]{:S(2)}) copy-start(bf16[16,64,384]{2,1,0:T(8,128)(2,1)} %get-tuple-element.9.refs_1_) | copy-start | bytes 2359300
  116.8 20.0 %copy-start.12 = (bf16[384,768]{1,0:T(8,128)(2,1)S(1)}, bf16[384,768]{1,0:T(8,128)(2,1)}, u32[]{:S(2)}) copy-start(bf16[384,768]{1,0:T(8,128)(2,1)} %refs_5_.3) | copy-start | bytes 1769476
  116.8 20.0 %copy-start.18 = (bf16[96,1536]{1,0:T(8,128)(2,1)S(1)}, bf16[96,1536]{1,0:T(8,128)(2,1)}, u32[]{:S(2)}) copy-start(bf16[96,1536]{1,0:T(8,128)(2,1)} %refs_3_.5) | copy-start | bytes 884740

commit v4 on v3

v4 whole, which is shorter than its diff:
```python
import functools
import math

import jax
import jax.numpy as jnp
import numpy as np
from jax import lax
from jax.experimental import pallas as pl
from jax.experimental.pallas import tpu as pltpu
from jax.sharding import Mesh
from jax.sharding import PartitionSpec as P

HEADS = 12
WIN = 8
CELLS = WIN * WIN
QUAD = 4

epsilon = 1e-05
F32 = jnp.float32
BF16 = jnp.bfloat16
ROWS = ("row_pair", "core")
ALL = ("row_pair", "core", "cols")
CLASS = ("row_pair", "cols")


def params(megabytes):
    return pltpu.CompilerParams(vmem_limit_bytes=megabytes << 20)


def resident(kernel, outs, args, scratch, megabytes, work, name, pinned=True, free=()):
    here = pl.BlockSpec(memory_space=pltpu.VMEM)
    args = [
        a if i in free else pltpu.with_memory_space_constraint(a, pltpu.VMEM)
        for i, a in enumerate(args)
    ]
    return pl.pallas_call(
        kernel,
        in_specs=[here] * len(args),
        out_specs=[here] * len(outs),
        out_shape=[(pltpu.VMEM if pinned else jax.ShapeDtypeStruct)(*out) for out in outs],
        scratch_shapes=scratch,
        compiler_params=params(megabytes),
        cost_estimate=pl.CostEstimate(flops=int(work), bytes_accessed=1 << 20, transcendentals=0),
        name=name,
    )(*args)


def gelu_twice(h):
    inner = h * (1.5957691216057308 + 0.285419265090401 * (h * h))
    return h + h * jnp.tanh(inner)


def layer_norm(x, scale=1.0):
    average = jnp.mean(x, axis=-1, keepdims=True)
    centred = x - average
    spread = jnp.mean(centred * centred, axis=-1, keepdims=True)
    return centred * (scale * lax.rsqrt(spread + epsilon))


def half_norm(x):
    return layer_norm(x, 0.5)


def dot(a, b):
    return jnp.dot(a, b, preferred_element_type=F32)


def exact_dot(a, b, dims):
    total = None
    for _ in range(3):
        term = a.astype(BF16)
        a = a - term.astype(F32)
        product = lax.dot_general(term, b, (dims, ((), ())), preferred_element_type=F32)
        total = product if total is None else total + product
    return total


def panels(rows, channels):
    return pltpu.VMEM((channels // 128, rows, 128), F32)


def put(ref, x):
    for c in range(ref.shape[0]):
        ref[c] = x[:, c * 128 : (c + 1) * 128]


def put_strided(ref, x, start, count, stride):
    for c in range(ref.shape[0]):
        ref[c, pl.ds(start, count, stride=stride), :] = x[:, c * 128 : (c + 1) * 128]


def take(ref):
    return jnp.concatenate([ref[c] for c in range(ref.shape[0])], 1)


def take_strided(ref, start, count, stride):
    return jnp.concatenate(
        [ref[c, pl.ds(start, count, stride=stride), :] for c in range(ref.shape[0])], 1
    )


def expand(image, weight, first, count):
    _, cols, channels = image.shape
    hidden = weight.shape[1]

    def kernel(x_hbm, w_hbm, out_ref, x_ref, w_ref, x_sem, w_sem):
        x_copy = pltpu.make_async_copy(x_hbm.at[first : first + count], x_ref, x_sem)
        w_copy = pltpu.make_async_copy(w_hbm, w_ref, w_sem)
        x_copy.start()
        w_copy.start()
        x_copy.wait()
        x = x_ref[...].reshape(count * cols, channels).astype(F32)
        normed = half_norm(x).astype(BF16)
        w_copy.wait()
        for c in range(0, hidden, 256):
            wide = gelu_twice(dot(normed, w_ref[:, c : c + 256])).astype(BF16)
            out_ref[:, :, c : c + 256] = wide.reshape(count, cols, 256)

    away = pl.BlockSpec(memory_space=pl.ANY)
    work = 4 * count * cols * channels * hidden
    return pl.pallas_call(
        kernel,
        in_specs=[away, away],
        out_specs=pl.BlockSpec(memory_space=pltpu.VMEM),
        out_shape=pltpu.VMEM((count, cols, hidden), BF16),
        scratch_shapes=[
            pltpu.VMEM((count, cols, channels), BF16),
            pltpu.VMEM(weight.shape, BF16),
            pltpu.SemaphoreType.DMA,
            pltpu.SemaphoreType.DMA,
        ],
        compiler_params=params(16),
        cost_estimate=pl.CostEstimate(flops=work, bytes_accessed=1 << 20, transcendentals=0),
        name="expand",
    )(*[pltpu.with_memory_space_constraint(a, pltpu.HBM) for a in (image, weight)])


def flag(held):
    return jnp.where(held, 1.0, 0.0).astype(F32)


def rim_of(normed, weight, rim, slot):
    rim[slot] = gelu_twice(dot(normed[...], weight)).astype(BF16).astype(F32)


def squeeze_sums(sums, red_ref, part_ref):
    parts = exact_dot(sums[...], red_ref[...], ((1,), (1,)))
    part_ref[...] = jnp.broadcast_to(jnp.sum(parts, axis=0, keepdims=True), part_ref.shape)


def lanes_at(start, size=128):
    return pl.ds(pl.multiple_of(start, 128), size)


def conv_kernel(
    upper_ref, lower_ref, over_ref, pair_ref, left_ref, right_ref, w_ref, taps_ref, red_ref,
    act_ref, part_ref, normed, rim, left, right, sums, *, chunk,
):
    core = lax.axis_index("core")
    rows, cols, width = act_ref.shape
    steps = width // chunk
    row, col = lax.axis_index("row_pair"), lax.axis_index("cols")
    has_over = flag(row + core > 0) * flag(row - (1 - core) < lax.axis_size("row_pair") - 1)
    has_left, has_right = flag(col > 0), flag(col < lax.axis_size("cols") - 1)
    cell = lax.broadcasted_iota(jnp.int32, (80, 1), 0)
    corners = jnp.where(cell == cols, has_left, jnp.where(cell == cols + 1, has_right, 1.0))
    for ref, start, held in (
        (over_ref, 0, corners * has_over),
        (pair_ref, 80, corners),
        (left_ref, 160, has_left),
        (right_ref, 176, has_right),
    ):
        size = ref.shape[0]
        normed[start : start + size, :] = (half_norm(ref[...].astype(F32)) * held).astype(BF16)
    rim_of(normed, w_ref[:, :chunk], rim, 0)
    top, bottom = core * 80, (1 - core) * 80
    place = lax.broadcasted_iota(jnp.int32, (8, 128), 0)

    def advance(step, carry):
        slot = step % 2
        for ref, start, corner in ((left, 160, 64), (right, 176, 65)):
            ref[0:1, :] = rim[slot, pl.ds(top + corner, 1), :]
            ref[1:17, :] = rim[slot, start : start + 16, :]
            ref[17:18, :] = rim[slot, pl.ds(bottom + corner, 1), :]
        for lane in range(0, chunk, 128):
            lanes = slice(lane, lane + 128)
            wide = lanes_at(step * chunk + lane)
            taps = [0.5 * taps_ref[t : t + 1, wide].astype(F32) for t in range(9)]
            short = [tap.astype(BF16) for tap in taps]
            before = sum(taps[3 * a] * left[a : a + rows, lanes] for a in range(3))
            after = sum(taps[3 * a + 2] * right[a : a + rows, lanes] for a in range(3))
            total = jnp.zeros((8, 128), F32)

            def line(r):
                if r < 0:
                    return rim[slot, pl.ds(pl.multiple_of(top, 8), 64), lanes].astype(BF16)
                if r == rows:
                    return rim[slot, pl.ds(pl.multiple_of(bottom, 8), 64), lanes].astype(BF16)
                return upper_ref[r, :, wide] if r < rows // 2 else lower_ref[r - rows // 2, :, wide]

            window = [line(-1), line(0), None]
            for r in range(rows):
                window[2] = line(r + 1)
                one = [
                    short[b] * window[0] + short[3 + b] * window[1] + short[6 + b] * window[2]
                    for b in range(3)
                ]
                one = [line_sum.astype(F32) for line_sum in one]
                down = pltpu.roll(one[0], 1, 0)
                up = pltpu.roll(one[2], cols - 1, 0)
                first = jnp.where(place == 0, before[r : r + 1], down[0:8])
                last = jnp.where(place == 7, after[r : r + 1], up[cols - 8 :])
                whole = (
                    one[1]
                    + jnp.concatenate([first, down[8:]], 0)
                    + jnp.concatenate([up[: cols - 8], last], 0)
                )
                act = gelu_twice(whole)
                act_ref[r, :, wide] = act.astype(BF16)
                for s in range(0, cols, 8):
                    total = total + act[s : s + 8]
                window = [window[1], window[2], None]
            sums[:, wide] = total
        later = jnp.minimum(step + 1, steps - 1) * chunk
        rim_of(normed, w_ref[:, lanes_at(later, chunk)], rim, 1 - slot)
        return carry

    lax.fori_loop(0, steps, advance, 0)
    squeeze_sums(sums, red_ref, part_ref)


def conv(upper, lower, over, pair, left, right, weight, taps, reduce, copies, chunk=256):
    half, cols, width = upper.shape
    channels = weight.shape[0]
    outs = [((2 * half, cols, width), BF16), ((copies, reduce.shape[0]), F32)]
    scratch = [
        pltpu.VMEM((192, channels), BF16),
        pltpu.VMEM((2, 192, chunk), F32),
        pltpu.VMEM((24, chunk), F32),
        pltpu.VMEM((24, chunk), F32),
        pltpu.VMEM((8, width), F32),
    ]
    args = (upper, lower, over, pair, left, right, weight, taps, reduce)
    kernel = functools.partial(conv_kernel, chunk=chunk)
    return resident(kernel, outs, args, scratch, 8, 8e9, "conv")


def gate_of(parts_ref, restore_ref, cell_count):
    average = jnp.sum(parts_ref[...], axis=0, keepdims=True) / cell_count
    squeezed = average * jax.nn.sigmoid(average)
    squeezed = jnp.broadcast_to(squeezed, (8, squeezed.shape[1]))
    return jax.nn.sigmoid(exact_dot(squeezed, restore_ref[...], ((1,), (0,))))


def mix(x, qkv_ref, out_ref, up_ref, down_ref):
    cells, channels = x.shape
    width = channels // HEADS
    normed = layer_norm(x).astype(BF16)
    projected = dot(normed, qkv_ref[...])
    queries = (projected[:, :channels] * (1.0 / math.sqrt(width))).astype(BF16)
    keys = projected[:, channels : 2 * channels].astype(BF16)
    values = projected[:, 2 * channels :].astype(BF16)
    lane = lax.broadcasted_iota(jnp.int32, (1, 128), 1)
    masks = [((lane >= h * width) & (lane < (h + 1) * width)).astype(BF16) for h in range(QUAD)]
    groups = []
    for g in range(0, cells, CELLS):
        mine = slice(g, g + CELLS)
        quads = []
        for c in range(0, channels, 128):
            lanes = slice(c, c + 128)
            q, k, v = queries[mine, lanes], keys[mine, lanes], values[mine, lanes]
            stacked = jnp.concatenate([q * m for m in masks], 0)
            scores = lax.dot_general(
                k, stacked, (((1,), (1,)), ((), ())), preferred_element_type=F32
            )
            weights = jnp.exp(scores - jnp.max(scores, axis=0, keepdims=True))
            shares = weights * (1.0 / jnp.sum(weights, axis=0, keepdims=True))
            blended = lax.dot_general(
                shares.astype(BF16), v, (((0,), (0,)), ((), ())), preferred_element_type=F32
            )
            picked = blended[3 * CELLS :]
            for h in (2, 1, 0):
                picked = jnp.where(
                    lane < (h + 1) * width, blended[h * CELLS : (h + 1) * CELLS], picked
                )
            quads.append(picked)
        groups.append(jnp.concatenate(quads, 1).astype(BF16))
    x = x + dot(jnp.concatenate(groups, 0), out_ref[...])
    normed = half_norm(x).astype(BF16)
    for c in range(0, up_ref.shape[1], 512):
        hidden = gelu_twice(dot(normed, up_ref[:, c : c + 512])).astype(BF16)
        x = x + dot(hidden, down_ref[c : c + 512, :])
    return x


def block_kernel(
    img_ref, act_ref, parts_ref, restore_ref, project_ref, qkv_ref, out_ref, up_ref, down_ref,
    res_ref, *, cell_count,
):
    rows, cols, channels = img_ref.shape
    cells = WIN * cols
    wide = cols // WIN
    gate = gate_of(parts_ref, restore_ref, cell_count)
    for strip in range(rows // WIN):
        mine = slice(strip * WIN, (strip + 1) * WIN)
        scaled = act_ref[mine].reshape(cells, act_ref.shape[2]).astype(F32) * gate[0:1, :]
        x = img_ref[mine].reshape(cells, channels).astype(F32)
        x = x + dot(scaled.astype(BF16), project_ref[...])
        pieces = [
            x[r * cols + g * WIN : r * cols + (g + 1) * WIN]
            for g in range(wide)
            for r in range(WIN)
        ]
        y = mix(jnp.concatenate(pieces, 0), qkv_ref, out_ref, up_ref, down_ref)
        pieces = [
            y[g * CELLS + r * WIN : g * CELLS + (r + 1) * WIN]
            for r in range(WIN)
            for g in range(wide)
        ]
        res_ref[strip * cells : (strip + 1) * cells, :] = jnp.concatenate(pieces, 0).astype(BF16)


def block_part(image, act, parts, restore, project, qkv, out, up, down, cell_count):
    rows, cols, channels = image.shape
    outs = [((rows * cols, channels), BF16)]
    args = (image, act, parts, restore, project, qkv, out, up, down)
    kernel = functools.partial(block_kernel, cell_count=cell_count)
    return resident(kernel, outs, args, [], 24, 12e9, "block_part")[0]


def grid_kernel(x_ref, qkv_ref, out_ref, up_ref, down_ref, res_ref, before, after, *, batch):
    groups = x_ref.shape[0] // CELLS
    put(before, x_ref[...].astype(F32))
    for start in range(0, groups, batch):
        x = [take_strided(before, start + g, CELLS, groups) for g in range(batch)]
        y = mix(jnp.concatenate(x, 0), qkv_ref, out_ref, up_ref, down_ref)
        for g in range(batch):
            put_strided(after, y[g * CELLS : (g + 1) * CELLS], start + g, CELLS, groups)
    res_ref[...] = take(after).astype(BF16)


def grid_part(x, qkv, out, up, down, batch=8):
    scratch = [panels(*x.shape), panels(*x.shape)]
    args = (x, qkv, out, up, down)
    kernel = functools.partial(grid_kernel, batch=batch)
    return resident(kernel, [(x.shape, BF16)], args, scratch, 24, 10e9, "grid_part")[0]


def down_expand_kernel(x_ref, w_ref, out_ref, pool_ref, cells, *, block):
    rows, cols, channels = x_ref.shape
    put(cells, x_ref[...].reshape(rows * cols, channels).astype(F32))
    half = block * cols // 2
    for start in range(0, rows, block):
        x = [take_strided(cells, start * cols + parity, half, 2) for parity in range(2)]
        pairs = (x[0] + x[1]).reshape(block // 2, 2, cols // 2, channels)
        pool = 0.25 * (pairs[:, 0] + pairs[:, 1])
        pool_ref[start // 2 : (start + block) // 2] = pool.astype(BF16)
        normed = half_norm(jnp.concatenate(x, 0)).astype(BF16)
        for c in range(0, w_ref.shape[1], 256):
            hidden = gelu_twice(dot(normed, w_ref[:, c : c + 256])).astype(BF16)
            for parity in range(2):
                mine = hidden[parity * half : (parity + 1) * half]
                out_ref[start : start + block, parity, :, c : c + 256] = mine.reshape(
                    block, cols // 2, 256
                )


def down_expand_part(x, weight, block=8):
    rows, cols, channels = x.shape
    hidden = weight.shape[1]
    outs = [((rows, 2, cols // 2, hidden), BF16), ((rows // 2, cols // 2, channels), BF16)]
    work = 4 * rows * cols * channels * hidden
    scratch = [panels(rows * cols, channels)]
    kernel = functools.partial(down_expand_kernel, block=block)
    return resident(kernel, outs, (x, weight), scratch, 8, work, "down_expand")


def down_conv_kernel(
    hid_ref, sec_ref, upper_ref, left_ref, corner_ref, w_ref, taps_ref,
    red_ref, act_ref, part_ref, section_ref, cells, normed, rim, left, sums, sem, *, chunk,
):
    rows, _, cols, width = hid_ref.shape
    steps = width // chunk
    copy = pltpu.make_async_copy(sec_ref, section_ref, sem)
    copy.start()
    row, col = lax.axis_index("row_pair") + lax.axis_index("core"), lax.axis_index("cols")
    has_upper, has_left = flag(row > 0), flag(col > 0)
    put(cells, half_norm(upper_ref[...].astype(F32)) * has_upper)
    normed[0:32, :] = take_strided(cells, 0, 32, 2).astype(BF16)
    normed[32:64, :] = take_strided(cells, 1, 32, 2).astype(BF16)
    normed[64:80, :] = (half_norm(left_ref[...].astype(F32)) * has_left).astype(BF16)
    corner = half_norm(corner_ref[...].astype(F32)) * (has_upper * has_left)
    normed[80:96, :] = jnp.broadcast_to(corner, (16, corner.shape[1])).astype(BF16)
    rim_of(normed, w_ref[:, :chunk], rim, 0)
    place = lax.broadcasted_iota(jnp.int32, (8, 128), 0)

    def advance(step, carry):
        slot = step % 2
        left[0:1, :] = rim[slot, 80:81, :]
        left[1:17, :] = rim[slot, 64:80, :]
        for lane in range(0, chunk, 128):
            lanes = slice(lane, lane + 128)
            wide = lanes_at(step * chunk + lane)
            taps = [0.5 * taps_ref[t : t + 1, wide].astype(F32) for t in range(9)]
            before = sum(taps[3 * a] * left[a : a + rows, lanes] for a in range(3))
            total = jnp.zeros((8, 128), F32)

            def line(r, parity):
                if r < 0:
                    return rim[slot, 32 * parity : 32 * parity + 32, lanes]
                return hid_ref[r, parity, :, wide].astype(F32)

            for p in range(rows // 2):
                even = [line(2 * p + a - 1, 0) for a in range(3)]
                odd = [line(2 * p + a - 1, 1) for a in range(3)]
                shifted = sum(taps[3 * a] * odd[a] for a in range(3))
                whole = sum(taps[3 * a + 1] * even[a] + taps[3 * a + 2] * odd[a] for a in range(3))
                shifted = pltpu.roll(shifted, 1, 0)
                first = jnp.where(place == 0, before[2 * p : 2 * p + 1], shifted[0:8])
                act = gelu_twice(whole + jnp.concatenate([first, shifted[8:]], 0))
                act_ref[p, :, wide] = act.astype(BF16)
                for s in range(0, cols, 8):
                    total = total + act[s : s + 8]
            sums[:, wide] = total
        later = jnp.minimum(step + 1, steps - 1) * chunk
        rim_of(normed, w_ref[:, lanes_at(later, chunk)], rim, 1 - slot)
        return carry

    lax.fori_loop(0, steps, advance, 0)
    squeeze_sums(sums, red_ref, part_ref)
    copy.wait()


def down_conv(hidden, section, upper, left, corner, weight, taps, reduce, copies, chunk=256):
    rows, _, cols, width = hidden.shape
    channels = weight.shape[0]
    here = pl.BlockSpec(memory_space=pltpu.VMEM)
    args = (hidden, section, upper, left, corner, weight, taps, reduce)
    return pl.pallas_call(
        functools.partial(down_conv_kernel, chunk=chunk),
        in_specs=[here] * len(args),
        out_specs=[here, here, pl.BlockSpec(memory_space=pl.ANY)],
        out_shape=[
            pltpu.VMEM((rows // 2, cols, width), BF16),
            pltpu.VMEM((copies, reduce.shape[0]), F32),
            jax.ShapeDtypeStruct((rows, 2 * cols, channels), BF16),
        ],
        scratch_shapes=[
            panels(64, channels),
            pltpu.VMEM((96, channels), BF16),
            pltpu.VMEM((2, 96, chunk), F32),
            pltpu.VMEM((24, chunk), F32),
            pltpu.VMEM((8, width), F32),
            pltpu.SemaphoreType.DMA,
        ],
        compiler_params=params(8),
        name="down_conv",
    )(*[pltpu.with_memory_space_constraint(a, pltpu.VMEM) for a in args])


def down_out(act, pooled, parts, restore, project, short, cell_count):
    rows, cols, hidden = act.shape
    outs = project.shape[1]
    count = rows * cols // 2

    def kernel(act_ref, pool_ref, parts_ref, restore_ref, project_ref, short_ref, res_ref):
        gate = gate_of(parts_ref, restore_ref, cell_count)
        for i in range(2):
            mine = slice(i * rows // 2, (i + 1) * rows // 2)
            scaled = act_ref[mine].reshape(count, hidden).astype(F32) * gate[0:1, :]
            pool = pool_ref[mine].reshape(count, pool_ref.shape[2])
            y = dot(scaled.astype(BF16), project_ref[...]) + dot(pool, short_ref[...])
            res_ref[mine] = y.astype(BF16).reshape(rows // 2, cols, outs)

    here = pl.BlockSpec(memory_space=pltpu.VMEM)
    args = (act, pooled, parts, restore, project, short)
    return pl.pallas_call(
        kernel,
        in_specs=[here] * len(args),
        out_specs=here,
        out_shape=jax.ShapeDtypeStruct((rows, cols, outs), BF16),
        compiler_params=params(8),
        name="down_out",
    )(*[pltpu.with_memory_space_constraint(a, pltpu.VMEM) for a in args])


def shift(x, axes, by):
    size = lax.axis_size(axes)
    return lax.ppermute(x, axes, [(i, (i + by) % size) for i in range(size)])


def shift_both(x):
    rows, cols = lax.axis_size(ROWS), lax.axis_size("cols")
    pairs = [
        (r * cols + c, (r + 1) % rows * cols + (c + 1) % cols)
        for r in range(rows)
        for c in range(cols)
    ]
    return lax.ppermute(x, ALL, pairs)


def exchange(x):
    cells, channels = x.shape
    sharers = lax.axis_size(CLASS)
    pieces = x.reshape(sharers, cells // sharers, channels)
    pieces = lax.all_to_all(pieces, CLASS, split_axis=0, concat_axis=0, tiled=True)
    return pieces.reshape(cells, channels)


def sum_parts(part):
    count, squeezed = part.shape
    part = part.reshape(count, 1, squeezed)
    arrived = lax.all_to_all(part, ALL, split_axis=0, concat_axis=0, tiled=True)
    return arrived.reshape(count, squeezed)


def row_rims(image, left, right):
    rows, cols, channels = image.shape
    size = lax.axis_size(ROWS)
    pad = jnp.zeros((14, channels), image.dtype)
    first = jnp.concatenate([image[0], left[:1], right[:1], pad], 0)
    last = jnp.concatenate([image[rows - 1], left[rows - 1 :], right[rows - 1 :], pad], 0)
    even = lax.axis_index("core") == 0
    away = jnp.where(even, first, last)
    near = jnp.where(even, last, first)
    pairs = [(r, (r - 1 if r % 2 == 0 else r + 1) % size) for r in range(size)]
    over = lax.ppermute(away, ROWS, pairs)
    pair = lax.ppermute(near, "core", [(0, 1), (1, 0)])
    return over, pair


def local(
    image,
    mb_expand,
    mb_taps,
    mb_reduce,
    mb_restore,
    mb_project,
    block_qkv,
    block_out,
    first_up,
    first_down,
    grid_qkv,
    grid_out,
    second_up,
    second_down,
    down_expand,
    down_taps,
    down_reduce,
    down_restore,
    down_project,
    down_shortcut,
):
    rows, cols, channels = image.shape
    all_cells = rows * cols * lax.axis_size(ALL)

    left = shift(image[:, cols - 1], "cols", 1)
    right = shift(image[:, 0], "cols", -1)
    upper = expand(image, mb_expand, 0, rows // 2)
    left, right, upper = lax.optimization_barrier((left, right, upper))
    over, pair = row_rims(image, left, right)
    lower = expand(image, mb_expand, rows // 2, rows // 2)
    act, part = conv(
        upper, lower, over, pair, left, right, mb_expand, mb_taps, mb_reduce.T,
        lax.axis_size(ALL),
    )
    parts = sum_parts(part)
    mixed = block_part(
        image, act, parts, mb_restore, mb_project, block_qkv, block_out, first_up, first_down,
        all_cells,
    )
    mixed = grid_part(exchange(mixed), grid_qkv, grid_out, second_up, second_down)
    section = exchange(mixed).reshape(rows, cols, channels)

    upper = shift(section[rows - 1], ROWS, 1)
    left = shift(section[:, cols - 1], "cols", 1)
    corner = shift_both(section[rows - 1, cols - 1 :])
    hidden, pooled = down_expand_part(section, down_expand)
    act, part, whole = down_conv(
        hidden, section, upper, left, corner, down_expand, down_taps, down_reduce.T,
        lax.axis_size(ALL),
    )
    parts = sum_parts(part)
    downsampled = down_out(
        act, pooled, parts, down_restore, down_project, down_shortcut, all_cells // 4
    )
    return (whole, downsampled)


def solution(mesh):
    rows, cols = mesh.devices.shape
    fine = Mesh(np.asarray(mesh.devices).reshape(rows // 2, 2, cols), ALL)
    tile = P(ROWS, "cols", None)
    in_specs = (tile,) + (P(),) * 19
    return jax.shard_map(
        local, mesh=fine, in_specs=in_specs, out_specs=(tile, tile), check_vma=False
    )
```

time: 139 us -> 136 us (0.978)
  Pallas kernels: 47 us -> 42.6 us
    pallas_call x8, Pallas kernels: 47 us -> 42.6 us  [the longest x4 32 us: resident(): pl.pallas_call(kernel, in_specs=[here] * len(args), out_specs=[here] * le...]
  transfers between devices with their start and end apart: 7 -> 7, of which waited for: 0 -> 1; matrix products, arithmetic and copies ran while one was open for 1% -> 1% of each run, Pallas kernels for 7% -> 6%
where the time goes in v4:
time: 136 us; the launch traced here: 135 us
  blocking collectives  73.6 us (54%)
  Pallas kernels  42.6 us (31%)
  starting transfers between devices  15.5 us (11%)
  local copies, waits for them, and re-layouts  2.08 us (2%)
    all_to_all x2, blocking collectives, exchange(): lax.all_to_all(pieces, CLASS, split_axis=0, concat_axis=0, tiled=True)  39.4 us
    all_to_all x2, blocking collectives, sum_parts(): arrived = lax.all_to_all(part, ALL, split_axis=0, concat_axis=0, tiled=True)  34.2 us
    pallas_call x4, Pallas kernels, resident(): pl.pallas_call(kernel, in_specs=[here] * len(args), out_specs=[here] * le...  32 us
    ppermute x4, starting transfers between devices, shift(): return lax.ppermute(x, axes, [(i, (i + by) % size) for i in range(size)])  10.1 us
    pallas_call x2, Pallas kernels, expand(): pl.pallas_call(kernel, in_specs=[away, away], out_specs=pl.BlockSpec(memo...  5.31 us
    pallas_call x1, Pallas kernels, down_conv(): pl.pallas_call(functools.partial(down_conv_kernel, chunk=chunk), in_specs...  3.34 us
    ppermute x1, starting transfers between devices, shift_both(): return lax.ppermute(x, ALL, pairs)  3.13 us
  transfers between devices with their start and end apart: 7, of which 1 were waited for; matrix products, arithmetic and copies ran while one was open for 1% of the time, Pallas kernels for 6%

profile of v4, /device:TPU:1, one launch (start us, length us, event | category | flops | bytes accessed | tf_op | source)
XLA Modules:
  0.0 135.5 jit_solution(7986300989826284805)
XLA Ops:
  0.6 1.0 fusion
  1.6 3.8 %collective-permute-start = (bf16[16,384]{1,0:T(8,128)(2,1)S(1)}, bf16[16,384]{1,0:T(8,128)(2,1)S(1)}, u32[]{:S(2)}, u32[]{:S(2)}) collective-permute-start(bf16[16,384]{1,0:T(8,128)(2,1)S(1)} %bitcast.44), channel_id=1, source_target_pairs={{0,1},{1,2},{2,3},{3,4},{4,5},{5,6},{6,7},{7,0},{8,9},{9,10},{10,1... | collective-permute-start | bytes 36872 | tf_op jit(solution)/shard_map/ppermute | solution.py:489
  5.4 3.6 %collective-permute-start.1 = (bf16[16,384]{1,0:T(8,128)(2,1)S(1)}, bf16[16,384]{1,0:T(8,128)(2,1)S(1)}, u32[]{:S(2)}, u32[]{:S(2)}) collective-permute-start(bf16[16,384]{1,0:T(8,128)(2,1)S(1)} %bitcast.45), channel_id=1, source_target_pairs={{0,7},{1,0},{2,1},{3,2},{4,3},{5,4},{6,5},{7,6},{8,15},{9,8},{10,9... | collective-permute-start | bytes 36872 | tf_op jit(solution)/shard_map/ppermute | solution.py:489
  9.0 0.8 slice_bitcast_fusion.1
  9.8 2.7 %expand.2.upper_ref = bf16[8,64,1536]{2,1,0:T(8,128)(2,1)S(1)} custom-call(bf16[16,64,384]{2,1,0:T(8,128)(2,1)} %img_ref.1, bf16[384,1536]{1,0:T(8,128)(2,1)} %w_ref.3), custom_call_target="tpu_custom_call" | custom-call | flops 1207959552 | bytes 1048576 | tf_op jit(solution)/shard_map/expand/pallas_call | solution.py:121
  12.5 0.1 pad.7.clone
  12.6 0.0 collective-permute-done.left_ref
  12.6 0.0 collective-permute-done.1.right_ref
  12.6 0.1 broadcast_select_fusion
  12.7 1.0 collective-permute-start.3
  13.8 1.2 collective-permute-start.2
  15.0 2.7 %expand.3.lower_ref = bf16[8,64,1536]{2,1,0:T(8,128)(2,1)S(1)} custom-call(bf16[16,64,384]{2,1,0:T(8,128)(2,1)} %img_ref.1, bf16[384,1536]{1,0:T(8,128)(2,1)} %w_ref.3), custom_call_target="tpu_custom_call" | custom-call | flops 1207959552 | bytes 1048576 | tf_op jit(solution)/shard_map/expand/pallas_call | solution.py:121
  17.7 0.0 collective-permute-done.3.pair_ref
  17.7 0.0 collective-permute-done.2.over_ref
  17.7 0.0 copy-done.7
  17.7 0.0 copy-done.15
  17.7 0.0 copy-done.19
  17.7 0.0 copy-start.6
  17.7 0.0 copy-start.8
  17.7 0.0 copy-start.9
  17.7 0.0 copy-start.10
  17.8 0.0 copy-start.13
  17.8 0.0 copy-start.16
  17.8 0.0 copy-start.17
  17.8 7.3 %conv.1 = (bf16[16,64,1536]{2,1,0:T(8,128)(2,1)S(1)}, f32[128,96]{1,0:T(8,128)S(1)}) custom-call(bf16[8,64,1536]{2,1,0:T(8,128)(2,1)S(1)} %expand.2.upper_ref, bf16[8,64,1536]{2,1,0:T(8,128)(2,1)S(1)} %expand.3.lower_ref, bf16[80,384]{1,0:T(8,128)(2,1)S(1)} %collective-permute-done.2.over_ref, bf16[80,384]{1,0:T(8,128)(2,1)S(1)} %collective-permute-done.3.pair_ref, ...), custom_call_target="tpu_custom_call" | custom-call | flops 8000000000 | bytes 1048576 | tf_op jit(solution)/shard_map/conv/pallas_call | solution.py:36
  25.1 18.6 %all_to_all.20 = f32[128,1,96]{2,1,0:T(1,128)S(1)} all-to-all(f32[128,1,96]{2,1,0:T(1,128)S(1)} %bitcast.39), channel_id=1, replica_groups=mesh['row_pair'=8,'core'=2,'cols'=8] {'row_pair','core','cols'}, dimensions={0} | all-to-all | bytes 98304 | tf_op jit(solution)/shard_map/all_to_all | solution.py:513
  43.7 0.0 copy-done.6
  43.7 0.0 copy-done.8
  43.7 0.0 copy-done.9
  43.7 0.0 copy-done.10
  43.7 0.0 copy-done.13
  43.8 0.0 copy-done.16
  43.8 0.0 copy-done.17
  43.8 0.0 copy-start.12
  43.8 0.0 copy-start.14
  43.8 11.5 %block_part.1 = bf16[1024,384]{1,0:T(8,128)(2,1)S(1)} custom-call(bf16[16,64,384]{2,1,0:T(8,128)(2,1)S(1)} %copy-done.6, bf16[16,64,1536]{2,1,0:T(8,128)(2,1)S(1)} %get-tuple-element.15.act_ref, f32[128,96]{1,0:T(8,128)S(1)} %bitcast.41, bf16[96,1536]{1,0:T(8,128)(2,1)S(1)} %copy-done.16, bf16[1536,384]{1,0:T(8,128)(2,1)S(1)} %copy-done.8, ...), custom_call_target="tpu_custom_call" | custom-call | flops 12000000000 | bytes 1048576 | tf_op jit(solution)/shard_map/block_part/pallas_call | solution.py:36
  55.3 0.0 copy-start.11
  55.4 0.0 copy-start.18
  55.4 20.4 %all_to_all.21 = bf16[64,16,384]{2,1,0:T(8,128)(2,1)S(1)} all-to-all(bf16[64,16,384]{2,1,0:T(8,128)(2,1)S(1)} %bitcast.34), channel_id=1, replica_groups=mesh['row_pair'=8,'core'=2,'cols'=8] {'row_pair','cols'}, dimensions={0} | all-to-all | bytes 1572864 | tf_op jit(solution)/shard_map/all_to_all | solution.py:506
  75.8 0.0 copy-done.12
  75.8 0.0 copy-done.14
  75.8 0.0 copy-done.11
  75.8 0.0 copy-done.18
  75.8 10.4 %grid_part.1 = bf16[1024,384]{1,0:T(8,128)(2,1)S(1)} custom-call(bf16[1024,384]{1,0:T(8,128)(2,1)S(1)} %bitcast.35, bf16[384,1152]{1,0:T(8,128)(2,1)S(1)} %copy-done.14, bf16[384,384]{1,0:T(8,128)(2,1)S(1)} %copy-done.18, bf16[384,1536]{1,0:T(8,128)(2,1)S(1)} %copy-done.11, bf16[1536,384]{1,0:T(8,128)(2,1)S(1)} %copy-done.12), custom_call_target="tpu_custom_call" | custom-call | flops 10000000000 | bytes 1048576 | tf_op jit(solution)/shard_map/grid_part/pallas_call | solution.py:36
  86.2 0.0 copy-start.1
  86.2 19.0 %all_to_all.22 = bf16[64,16,384]{2,1,0:T(8,128)(2,1)S(1)} all-to-all(bf16[64,16,384]{2,1,0:T(8,128)(2,1)S(1)} %bitcast.36), channel_id=1, replica_groups=mesh['row_pair'=8,'core'=2,'cols'=8] {'row_pair','cols'}, dimensions={0} | all-to-all | bytes 1572864 | tf_op jit(solution)/shard_map/all_to_all | solution.py:506
  105.3 3.1 %collective-permute-start.6 = (bf16[1,384]{1,0:T(2,128)(2,1)S(1)}, bf16[1,384]{1,0:T(2,128)(2,1)S(1)}, u32[]{:S(2)}, u32[]{:S(2)}) collective-permute-start(bf16[1,384]{1,0:T(2,128)(2,1)S(1)} %slice_bitcast_fusion.2), channel_id=1, source_target_pairs={{0,9},{1,10},{2,11},{3,12},{4,13},{5,14},{6,15},{7,8},{8,17},{9,18... | collective-permute-start | bytes 2312 | tf_op jit(solution)/shard_map/ppermute | solution.py:499
  108.4 2.4 %collective-permute-start.5 = (bf16[16,384]{1,0:T(8,128)(2,1)S(1)}, bf16[16,384]{1,0:T(8,128)(2,1)S(1)}, u32[]{:S(2)}, u32[]{:S(2)}) collective-permute-start(bf16[16,384]{1,0:T(8,128)(2,1)S(1)} %bitcast.46), channel_id=1, source_target_pairs={{0,1},{1,2},{2,3},{3,4},{4,5},{5,6},{6,7},{7,0},{8,9},{9,10},{10,1... | collective-permute-start | bytes 36872 | tf_op jit(solution)/shard_map/ppermute | solution.py:489
  110.9 0.0 copy-start.5
  110.9 0.3 collective-permute-start.4
  111.2 0.0 copy-done.1
  111.2 2.7 %down_expand.1 = (bf16[16,2,32,1536]{3,2,1,0:T(8,128)(2,1)S(1)}, bf16[8,32,384]{2,1,0:T(8,128)(2,1)S(1)}) custom-call(bf16[16,64,384]{2,1,0:T(8,128)(2,1)S(1)} %bitcast.32, bf16[384,1536]{1,0:T(8,128)(2,1)S(1)} %copy-done.1), custom_call_target="tpu_custom_call" | custom-call | flops 2415919104 | bytes 1048576 | tf_op jit(solution)/shard_map/down_expand/pallas_call | solution.py:36
  114.0 0.0 collective-permute-done.6.corner_ref
  114.0 0.6 collective-permute-done.5.left_ref
  114.6 0.0 collective-permute-done.4.upper_ref
  114.6 0.0 copy-done.3
  114.6 0.0 copy-done.5
  114.6 0.0 copy-start
  114.6 0.0 copy-start.2
  114.6 0.0 copy-start.4
  114.6 3.3 %down_conv.1 = (bf16[8,32,1536]{2,1,0:T(8,128)(2,1)S(1)}, f32[128,96]{1,0:T(8,128)S(1)}, bf16[16,64,384]{2,1,0:T(8,128)(2,1)}) custom-call(bf16[16,2,32,1536]{3,2,1,0:T(8,128)(2,1)S(1)} %get-tuple-element.17.hid_ref, bf16[16,64,384]{2,1,0:T(8,128)(2,1)S(1)} %bitcast.33, bf16[64,384]{1,0:T(8,128)(2,1)S(1)} %collective-permute-done.4.upper_ref, ...), custom_call_target="tpu_custom_call" | custom-call | tf_op jit(solution)/shard_map/down_conv/pallas_call | solution.py:439
  118.0 15.6 %all_to_all.23 = f32[128,1,96]{2,1,0:T(1,128)S(1)} all-to-all(f32[128,1,96]{2,1,0:T(1,128)S(1)} %bitcast.40), channel_id=1, replica_groups=mesh['row_pair'=8,'core'=2,'cols'=8] {'row_pair','core','cols'}, dimensions={0} | all-to-all | bytes 98304 | tf_op jit(solution)/shard_map/all_to_all | solution.py:513
  133.6 0.0 copy-done.2
  133.6 1.9 %down_out.1 = bf16[8,32,768]{2,1,0:T(8,128)(2,1)} custom-call(bf16[8,32,1536]{2,1,0:T(8,128)(2,1)S(1)} %get-tuple-element.19.act_ref, bf16[8,32,384]{2,1,0:T(8,128)(2,1)S(1)} %get-tuple-element.20.pool_ref, f32[128,96]{1,0:T(8,128)S(1)} %bitcast.38, bf16[96,1536]{1,0:T(8,128)(2,1)S(1)} %copy-done.4, bf16[1536,768]{1,0:T(8,128)(2,1)S(1)} %copy-done, ...), custom_call_target="tpu_custom_call" | custom-call | tf_op jit(solution)/shard_map/down_out/pallas_call | solution.py:477
  (14 shorter events, 0.1 us)
Async XLA Ops:
  1.6 11.0 %collective-permute-start = (bf16[16,384]{1,0:T(8,128)(2,1)S(1)}, bf16[16,384]{1,0:T(8,128)(2,1)S(1)}, u32[]{:S(2)}, u32[]{:S(2)}) collective-permute-start(bf16[16,384]{1,0:T(8,128)(2,1)S(1)} %bitcast.44), channel_id=1, source_target_pairs={{0,1},{1,2},{2,3},{3,4},{4,5},{5,6},{6,7},{7,0},{8,9},{9,10},{10,1... | collective-permute-start | bytes 36872 | tf_op jit(solution)/shard_map/ppermute | solution.py:489
  5.4 7.2 %collective-permute-start.1 = (bf16[16,384]{1,0:T(8,128)(2,1)S(1)}, bf16[16,384]{1,0:T(8,128)(2,1)S(1)}, u32[]{:S(2)}, u32[]{:S(2)}) collective-permute-start(bf16[16,384]{1,0:T(8,128)(2,1)S(1)} %bitcast.45), channel_id=1, source_target_pairs={{0,7},{1,0},{2,1},{3,2},{4,3},{5,4},{6,5},{7,6},{8,15},{9,8},{10,9... | collective-permute-start | bytes 36872 | tf_op jit(solution)/shard_map/ppermute | solution.py:489
  12.7 4.9 %collective-permute-start.3 = (bf16[80,384]{1,0:T(8,128)(2,1)S(1)}, bf16[80,384]{1,0:T(8,128)(2,1)S(1)}, u32[]{:S(2)}, u32[]{:S(2)}) collective-permute-start(bf16[80,384]{1,0:T(8,128)(2,1)S(1)} %get-tuple-element.26), channel_id=1, source_target_pairs={{0,8},{8,0},{1,9},{9,1},{2,10},{10,2},{3,11},{11,3},{4,12},{12,4},... | collective-permute-start | bytes 184328 | tf_op jit(solution)/shard_map/ppermute | solution.py:528
  13.8 3.9 %copy-start.7 = (bf16[384,1536]{1,0:T(8,128)(2,1)S(1)}, bf16[384,1536]{1,0:T(8,128)(2,1)}, u32[]{:S(2)}) copy-start(bf16[384,1536]{1,0:T(8,128)(2,1)} %w_ref.3) | copy-start | bytes 3538948
  13.8 3.9 %copy-start.15 = (bf16[1536,96]{0,1:T(8,128)(2,1)S(1)}, bf16[1536,96]{0,1:T(8,128)(2,1)}, u32[]{:S(2)}) copy-start(bf16[1536,96]{0,1:T(8,128)(2,1)} %param.23) | copy-start | bytes 884740
  13.8 3.9 %copy-start.19 = (bf16[9,1536]{1,0:T(8,128)(2,1)S(1)}, bf16[9,1536]{1,0:T(8,128)(2,1)}, u32[]{:S(2)}) copy-start(bf16[9,1536]{1,0:T(8,128)(2,1)} %taps_ref.2) | copy-start | bytes 82948
  13.8 3.9 %collective-permute-start.2 = (bf16[80,384]{1,0:T(8,128)(2,1)S(1)}, bf16[80,384]{1,0:T(8,128)(2,1)S(1)}, u32[]{:S(2)}, u32[]{:S(2)}) collective-permute-start(bf16[80,384]{1,0:T(8,128)(2,1)S(1)} %get-tuple-element.27), channel_id=1, source_target_pairs={{0,120},{8,16},{16,8},{24,32},{32,24},{40,48},{48,40},{56,64},{64,... | collective-permute-start | bytes 184328 | tf_op jit(solution)/shard_map/ppermute | solution.py:527
  17.7 26.0 %copy-start.6 = (bf16[16,64,384]{2,1,0:T(8,128)(2,1)S(1)}, bf16[16,64,384]{2,1,0:T(8,128)(2,1)}, u32[]{:S(2)}) copy-start(bf16[16,64,384]{2,1,0:T(8,128)(2,1)} %img_ref.1) | copy-start | bytes 2359300
  17.7 26.0 %copy-start.8 = (bf16[1536,384]{1,0:T(8,128)(2,1)S(1)}, bf16[1536,384]{1,0:T(8,128)(2,1)}, u32[]{:S(2)}) copy-start(bf16[1536,384]{1,0:T(8,128)(2,1)} %project_ref.2) | copy-start | bytes 3538948
  17.7 26.0 %copy-start.9 = (bf16[384,1536]{1,0:T(8,128)(2,1)S(1)}, bf16[384,1536]{1,0:T(8,128)(2,1)}, u32[]{:S(2)}) copy-start(bf16[384,1536]{1,0:T(8,128)(2,1)} %up_ref.2) | copy-start | bytes 3538948
  17.7 26.0 %copy-start.10 = (bf16[1536,384]{1,0:T(8,128)(2,1)S(1)}, bf16[1536,384]{1,0:T(8,128)(2,1)}, u32[]{:S(2)}) copy-start(bf16[1536,384]{1,0:T(8,128)(2,1)} %down_ref.2) | copy-start | bytes 3538948
  17.8 26.0 %copy-start.13 = (bf16[384,1152]{1,0:T(8,128)(2,1)S(1)}, bf16[384,1152]{1,0:T(8,128)(2,1)}, u32[]{:S(2)}) copy-start(bf16[384,1152]{1,0:T(8,128)(2,1)} %qkv_ref.2) | copy-start | bytes 2654212
  17.8 26.0 %copy-start.16 = (bf16[96,1536]{1,0:T(8,128)(2,1)S(1)}, bf16[96,1536]{1,0:T(8,128)(2,1)}, u32[]{:S(2)}) copy-start(bf16[96,1536]{1,0:T(8,128)(2,1)} %restore_ref.2) | copy-start | bytes 884740
  17.8 26.0 %copy-start.17 = (bf16[384,384]{1,0:T(8,128)(2,1)S(1)}, bf16[384,384]{1,0:T(8,128)(2,1)}, u32[]{:S(2)}) copy-start(bf16[384,384]{1,0:T(8,128)(2,1)} %out_ref.2) | copy-start | bytes 884740
  43.8 32.0 %copy-start.12 = (bf16[1536,384]{1,0:T(8,128)(2,1)S(1)}, bf16[1536,384]{1,0:T(8,128)(2,1)}, u32[]{:S(2)}) copy-start(bf16[1536,384]{1,0:T(8,128)(2,1)} %down_ref.3) | copy-start | bytes 3538948
  43.8 32.0 %copy-start.14 = (bf16[384,1152]{1,0:T(8,128)(2,1)S(1)}, bf16[384,1152]{1,0:T(8,128)(2,1)}, u32[]{:S(2)}) copy-start(bf16[384,1152]{1,0:T(8,128)(2,1)} %qkv_ref.3) | copy-start | bytes 2654212
  55.3 20.4 %copy-start.11 = (bf16[384,1536]{1,0:T(8,128)(2,1)S(1)}, bf16[384,1536]{1,0:T(8,128)(2,1)}, u32[]{:S(2)}) copy-start(bf16[384,1536]{1,0:T(8,128)(2,1)} %up_ref.3) | copy-start | bytes 3538948
  55.4 20.4 %copy-start.18 = (bf16[384,384]{1,0:T(8,128)(2,1)S(1)}, bf16[384,384]{1,0:T(8,128)(2,1)}, u32[]{:S(2)}) copy-start(bf16[384,384]{1,0:T(8,128)(2,1)} %out_ref.3) | copy-start | bytes 884740
  86.2 25.0 %copy-start.1 = (bf16[384,1536]{1,0:T(8,128)(2,1)S(1)}, bf16[384,1536]{1,0:T(8,128)(2,1)}, u32[]{:S(2)}) copy-start(bf16[384,1536]{1,0:T(8,128)(2,1)} %w_ref.5) | copy-start | bytes 3538948
  105.3 8.7 %collective-permute-start.6 = (bf16[1,384]{1,0:T(2,128)(2,1)S(1)}, bf16[1,384]{1,0:T(2,128)(2,1)S(1)}, u32[]{:S(2)}, u32[]{:S(2)}) collective-permute-start(bf16[1,384]{1,0:T(2,128)(2,1)S(1)} %slice_bitcast_fusion.2), channel_id=1, source_target_pairs={{0,9},{1,10},{2,11},{3,12},{4,13},{5,14},{6,15},{7,8},{8,17},{9,18... | collective-permute-start | bytes 2312 | tf_op jit(solution)/shard_map/ppermute | solution.py:499
  108.4 6.2 %collective-permute-start.5 = (bf16[16,384]{1,0:T(8,128)(2,1)S(1)}, bf16[16,384]{1,0:T(8,128)(2,1)S(1)}, u32[]{:S(2)}, u32[]{:S(2)}) collective-permute-start(bf16[16,384]{1,0:T(8,128)(2,1)S(1)} %bitcast.46), channel_id=1, source_target_pairs={{0,1},{1,2},{2,3},{3,4},{4,5},{5,6},{6,7},{7,0},{8,9},{9,10},{10,1... | collective-permute-start | bytes 36872 | tf_op jit(solution)/shard_map/ppermute | solution.py:489
  110.9 3.7 %copy-start.3 = (bf16[1536,96]{0,1:T(8,128)(2,1)S(1)}, bf16[1536,96]{0,1:T(8,128)(2,1)}, u32[]{:S(2)}) copy-start(bf16[1536,96]{0,1:T(8,128)(2,1)} %param.36) | copy-start | bytes 884740
  110.9 3.7 %copy-start.5 = (bf16[9,1536]{1,0:T(8,128)(2,1)S(1)}, bf16[9,1536]{1,0:T(8,128)(2,1)}, u32[]{:S(2)}) copy-start(bf16[9,1536]{1,0:T(8,128)(2,1)} %taps_ref.3) | copy-start | bytes 82948
  110.9 3.7 %collective-permute-start.4 = (bf16[64,384]{1,0:T(8,128)(2,1)S(1)}, bf16[64,384]{1,0:T(8,128)(2,1)S(1)}, u32[]{:S(2)}, u32[]{:S(2)}) collective-permute-start(bf16[64,384]{1,0:T(8,128)(2,1)S(1)} %bitcast.43), channel_id=1, source_target_pairs={{0,8},{8,16},{16,24},{24,32},{32,40},{40,48},{48,56},{56,64},{64,7... | collective-permute-start | bytes 147464 | tf_op jit(solution)/shard_map/ppermute | solution.py:489
  114.6 19.0 %copy-start = (bf16[1536,768]{1,0:T(8,128)(2,1)S(1)}, bf16[1536,768]{1,0:T(8,128)(2,1)}, u32[]{:S(2)}) copy-start(bf16[1536,768]{1,0:T(8,128)(2,1)} %project_ref.3) | copy-start | bytes 7077892
  114.6 19.0 %copy-start.2 = (bf16[384,768]{1,0:T(8,128)(2,1)S(1)}, bf16[384,768]{1,0:T(8,128)(2,1)}, u32[]{:S(2)}) copy-start(bf16[384,768]{1,0:T(8,128)(2,1)} %short_ref.1) | copy-start | bytes 1769476
  114.6 19.0 %copy-start.4 = (bf16[96,1536]{1,0:T(8,128)(2,1)S(1)}, bf16[96,1536]{1,0:T(8,128)(2,1)}, u32[]{:S(2)}) copy-start(bf16[96,1536]{1,0:T(8,128)(2,1)} %restore_ref.3) | copy-start | bytes 884740

commit v5 on v4

--- a/solution.py
+++ b/solution.py
@@ -19,25 +19,24 @@
 F32 = jnp.float32
 BF16 = jnp.bfloat16
 ROWS = ("row_pair", "core")
-ALL = ("row_pair", "core", "cols")
-CLASS = ("row_pair", "cols")
+COLS = ("depth", "col_pair")
+AXES = ("row_pair", "core", "depth", "col_pair")
+ALL = ("core", "row_pair", "col_pair", "depth")
+CLASS = ("row_pair", "col_pair", "depth")
 
 
 def params(megabytes):
     return pltpu.CompilerParams(vmem_limit_bytes=megabytes << 20)
 
 
-def resident(kernel, outs, args, scratch, megabytes, work, name, pinned=True, free=()):
+def resident(kernel, outs, args, scratch, megabytes, work, name):
     here = pl.BlockSpec(memory_space=pltpu.VMEM)
-    args = [
-        a if i in free else pltpu.with_memory_space_constraint(a, pltpu.VMEM)
-        for i, a in enumerate(args)
-    ]
+    args = [pltpu.with_memory_space_constraint(a, pltpu.VMEM) for a in args]
     return pl.pallas_call(
         kernel,
         in_specs=[here] * len(args),
         out_specs=[here] * len(outs),
-        out_shape=[(pltpu.VMEM if pinned else jax.ShapeDtypeStruct)(*out) for out in outs],
+        out_shape=[pltpu.VMEM(*out) for out in outs],
         scratch_shapes=scratch,
         compiler_params=params(megabytes),
         cost_estimate=pl.CostEstimate(flops=int(work), bytes_accessed=1 << 20, transcendentals=0),
@@ -99,38 +98,50 @@
     )
 
 
-def expand(image, weight, first, count):
-    _, cols, channels = image.shape
+def expand_kernel(x_ref, w_ref, out_ref, near_ref, first_ref, last_ref):
+    step = pl.program_id(0)
+    rows, cols, channels = x_ref.shape
+    normed = half_norm(x_ref[...].reshape(rows * cols, channels).astype(F32)).astype(BF16)
+    for c in range(0, w_ref.shape[1], 256):
+        wide = gelu_twice(dot(normed, w_ref[:, c : c + 256])).astype(BF16)
+        out_ref[:, :, c : c + 256] = wide.reshape(rows, cols, 256)
+
+    @pl.when(step == 0)
+    def _():
+        near_ref[0:2] = out_ref[0:2]
+        first_ref[...] = x_ref[0]
+
+    @pl.when(step == pl.num_programs(0) - 1)
+    def _():
+        near_ref[2:4] = out_ref[rows - 2 : rows]
+        last_ref[...] = x_ref[rows - 1]
+
+
+def expand(image, weight, block=4):
+    rows, cols, channels = image.shape
     hidden = weight.shape[1]
-
-    def kernel(x_hbm, w_hbm, out_ref, x_ref, w_ref, x_sem, w_sem):
-        x_copy = pltpu.make_async_copy(x_hbm.at[first : first + count], x_ref, x_sem)
-        w_copy = pltpu.make_async_copy(w_hbm, w_ref, w_sem)
-        x_copy.start()
-        w_copy.start()
-        x_copy.wait()
-        x = x_ref[...].reshape(count * cols, channels).astype(F32)
-        normed = half_norm(x).astype(BF16)
-        w_copy.wait()
-        for c in range(0, hidden, 256):
-            wide = gelu_twice(dot(normed, w_ref[:, c : c + 256])).astype(BF16)
-            out_ref[:, :, c : c + 256] = wide.reshape(count, cols, 256)
-
-    away = pl.BlockSpec(memory_space=pl.ANY)
-    work = 4 * count * cols * channels * hidden
+    still = lambda *shape: pl.BlockSpec(shape, lambda i: (0,) * len(shape))
     return pl.pallas_call(
-        kernel,
-        in_specs=[away, away],
-        out_specs=pl.BlockSpec(memory_space=pltpu.VMEM),
-        out_shape=pltpu.VMEM((count, cols, hidden), BF16),
-        scratch_shapes=[
-            pltpu.VMEM((count, cols, channels), BF16),
-            pltpu.VMEM(weight.shape, BF16),
-            pltpu.SemaphoreType.DMA,
-            pltpu.SemaphoreType.DMA,
+        expand_kernel,
+        grid=(rows // block,),
+        in_specs=[
+            pl.BlockSpec((block, cols, channels), lambda i: (i, 0, 0)),
+            still(channels, hidden),
+        ],
+        out_specs=[
+            pl.BlockSpec((block, cols, hidden), lambda i: (i, 0, 0)),
+            still(4, cols, hidden),
+            still(cols, channels),
+            still(cols, channels),
+        ],
+        out_shape=[
+            pltpu.HBM((rows, cols, hidden), BF16),
+            jax.ShapeDtypeStruct((4, cols, hidden), BF16),
+            jax.ShapeDtypeStruct((cols, channels), BF16),
+            jax.ShapeDtypeStruct((cols, channels), BF16),
         ],
         compiler_params=params(16),
-        cost_estimate=pl.CostEstimate(flops=work, bytes_accessed=1 << 20, transcendentals=0),
+        cost_estimate=pl.CostEstimate(flops=int(4e9), bytes_accessed=1 << 20, transcendentals=0),
         name="expand",
     )(*[pltpu.with_memory_space_constraint(a, pltpu.HBM) for a in (image, weight)])
 
@@ -152,74 +163,146 @@
     return pl.ds(pl.multiple_of(start, 128), size)
 
 
-def conv_kernel(
-    upper_ref, lower_ref, over_ref, pair_ref, left_ref, right_ref, w_ref, taps_ref, red_ref,
-    act_ref, part_ref, normed, rim, left, right, sums, *, chunk,
+def conv_row(lines, short, before, after, place):
+    cols = lines[0].shape[0]
+    one = [
+        (short[b] * lines[0] + short[3 + b] * lines[1] + short[6 + b] * lines[2]).astype(F32)
+        for b in range(3)
+    ]
+    down = pltpu.roll(one[0], 1, 0)
+    up = pltpu.roll(one[2], cols - 1, 0)
+    first = jnp.where(place == 0, before, down[0:8])
+    last = jnp.where(place == 7, after, up[cols - 8 :])
+    whole = (
+        one[1]
+        + jnp.concatenate([first, down[8:]], 0)
+        + jnp.concatenate([up[: cols - 8], last], 0)
+    )
+    act = gelu_twice(whole)
+    return act, sum(act[s : s + 8] for s in range(0, cols, 8))
+
+
+def half_taps(taps_ref, wide):
+    taps = [0.5 * taps_ref[t : t + 1, wide].astype(F32) for t in range(9)]
+    return taps, [tap.astype(BF16) for tap in taps]
+
+
+def side_norms(normed, start, left_ref, right_ref):
+    col = lax.axis_index(COLS)
+    has_left, has_right = flag(col > 0), flag(col < lax.axis_size(COLS) - 1)
+    for ref, at, held in ((left_ref, start, has_left), (right_ref, start + 16, has_right)):
+        normed[at : at + 16, :] = (half_norm(ref[...].astype(F32)) * held).astype(BF16)
+    return has_left, has_right
+
+
+def inner_kernel(
+    hid_ref, left_ref, right_ref, start_ref, w_ref, taps_ref, act_ref, sums_ref, normed, rim
 ):
-    core = lax.axis_index("core")
-    rows, cols, width = act_ref.shape
+    step = pl.program_id(0)
+    rows, cols, chunk = hid_ref.shape
+    slot = step % 2
+
+    @pl.when(step == 0)
+    def _():
+        side_norms(normed, 0, left_ref, right_ref)
+        rim_of(normed, start_ref[...], rim, 0)
+
+    place = lax.broadcasted_iota(jnp.int32, (8, 128), 0)
+    inner = rows - 2
+    for lane in range(0, chunk, 128):
+        lanes = slice(lane, lane + 128)
+        taps, short = half_taps(taps_ref, lanes)
+        before = sum(taps[3 * a] * rim[slot, a : a + inner, lanes] for a in range(3))
+        after = sum(taps[3 * a + 2] * rim[slot, 16 + a : 16 + a + inner, lanes] for a in range(3))
+        total = jnp.zeros((8, 128), F32)
+        lines = [hid_ref[0, :, lanes], hid_ref[1, :, lanes], None]
+        for r in range(1, rows - 1):
+            lines[2] = hid_ref[r + 1, :, lanes]
+            act, part = conv_row(lines, short, before[r - 1 : r], after[r - 1 : r], place)
+            act_ref[r, :, lanes] = act.astype(BF16)
+            total = total + part
+            lines = [lines[1], lines[2], None]
+        sums_ref[:, lanes] = total
+    rim_of(normed, w_ref[...], rim, 1 - slot)
+
+
+def conv_inner(hidden, left, right, weight, taps, chunk=256):
+    rows, cols, width = hidden.shape
+    channels = weight.shape[0]
     steps = width // chunk
-    row, col = lax.axis_index("row_pair"), lax.axis_index("cols")
+    whole = lambda a: pl.BlockSpec(a.shape, lambda c: (0, 0))
+    tall = pl.BlockSpec((rows, cols, chunk), lambda c: (0, 0, c))
+    return pl.pallas_call(
+        inner_kernel,
+        grid=(steps,),
+        in_specs=[
+            tall,
+            whole(left),
+            whole(right),
+            pl.BlockSpec((channels, chunk), lambda c: (0, 0)),
+            pl.BlockSpec((channels, chunk), lambda c: (0, jnp.minimum(c + 1, steps - 1))),
+            pl.BlockSpec((9, chunk), lambda c: (0, c)),
+        ],
+        out_specs=[tall, pl.BlockSpec((8, chunk), lambda c: (0, c))],
+        out_shape=[jax.ShapeDtypeStruct(hidden.shape, BF16), jax.ShapeDtypeStruct((8, width), F32)],
+        scratch_shapes=[pltpu.VMEM((32, channels), BF16), pltpu.VMEM((2, 32, chunk), F32)],
+        compiler_params=params(16),
+        cost_estimate=pl.CostEstimate(flops=int(7e9), bytes_accessed=1 << 20, transcendentals=0),
+        name="conv_inner",
+    )(
+        pltpu.with_memory_space_constraint(hidden, pltpu.HBM), left, right, weight, weight, taps
+    )
+
+
+def outer_kernel(
+    near_ref, over_ref, pair_ref, left_ref, right_ref, w_ref, taps_ref, red_ref, sums_ref,
+    act_ref, part_ref, normed, rim, sums, *, chunk,
+):
+    _, cols, width = near_ref.shape
+    steps = width // chunk
+    row, core = lax.axis_index("row_pair"), lax.axis_index("core")
     has_over = flag(row + core > 0) * flag(row - (1 - core) < lax.axis_size("row_pair") - 1)
-    has_left, has_right = flag(col > 0), flag(col < lax.axis_size("cols") - 1)
+    has_left, has_right = side_norms(normed, 160, left_ref, right_ref)
     cell = lax.broadcasted_iota(jnp.int32, (80, 1), 0)
     corners = jnp.where(cell == cols, has_left, jnp.where(cell == cols + 1, has_right, 1.0))
-    for ref, start, held in (
-        (over_ref, 0, corners * has_over),
-        (pair_ref, 80, corners),
-        (left_ref, 160, has_left),
-        (right_ref, 176, has_right),
-    ):
-        size = ref.shape[0]
-        normed[start : start + size, :] = (half_norm(ref[...].astype(F32)) * held).astype(BF16)
+    for ref, start, held in ((over_ref, 0, corners * has_over), (pair_ref, 80, corners)):
+        normed[start : start + 80, :] = (half_norm(ref[...].astype(F32)) * held).astype(BF16)
     rim_of(normed, w_ref[:, :chunk], rim, 0)
     top, bottom = core * 80, (1 - core) * 80
     place = lax.broadcasted_iota(jnp.int32, (8, 128), 0)
 
     def advance(step, carry):
         slot = step % 2
-        for ref, start, corner in ((left, 160, 64), (right, 176, 65)):
-            ref[0:1, :] = rim[slot, pl.ds(top + corner, 1), :]
-            ref[1:17, :] = rim[slot, start : start + 16, :]
-            ref[17:18, :] = rim[slot, pl.ds(bottom + corner, 1), :]
         for lane in range(0, chunk, 128):
             lanes = slice(lane, lane + 128)
             wide = lanes_at(step * chunk + lane)
-            taps = [0.5 * taps_ref[t : t + 1, wide].astype(F32) for t in range(9)]
-            short = [tap.astype(BF16) for tap in taps]
-            before = sum(taps[3 * a] * left[a : a + rows, lanes] for a in range(3))
-            after = sum(taps[3 * a + 2] * right[a : a + rows, lanes] for a in range(3))
-            total = jnp.zeros((8, 128), F32)
-
-            def line(r):
-                if r < 0:
-                    return rim[slot, pl.ds(pl.multiple_of(top, 8), 64), lanes].astype(BF16)
-                if r == rows:
-                    return rim[slot, pl.ds(pl.multiple_of(bottom, 8), 64), lanes].astype(BF16)
-                return upper_ref[r, :, wide] if r < rows // 2 else lower_ref[r - rows // 2, :, wide]
-
-            window = [line(-1), line(0), None]
-            for r in range(rows):
-                window[2] = line(r + 1)
-                one = [
-                    short[b] * window[0] + short[3 + b] * window[1] + short[6 + b] * window[2]
-                    for b in range(3)
+            taps, short = half_taps(taps_ref, wide)
+
+            def cells(at, side):
+                return rim[slot, pl.ds(pl.multiple_of(at, 8), 8), lanes][side : side + 1]
+
+            def line(at):
+                return rim[slot, pl.ds(pl.multiple_of(at, 8), 64), lanes].astype(BF16)
+
+            total = sums_ref[:, wide]
+            near = [near_ref[r, :, wide] for r in range(4)]
+            edges = (
+                ([line(top), near[0], near[1]], (top, 0), (160, 161)),
+                ([near[2], near[3], line(bottom)], (bottom, 2), (174, 175)),
+            )
+            for i, (lines, (corner, turn), (one, two)) in enumerate(edges):
+                beside = [[], []]
+                for side in range(2):
+                    beside[side].append(cells(corner + 64, side))
+                    for at in (one, two):
+                        beside[side].append(rim[slot, at + 16 * side : at + 16 * side + 1, lanes])
+                before, after = [
+                    sum(taps[3 * ((a + turn) % 3) + 2 * side] * beside[side][a] for a in range(3))
+                    for side in range(2)
                 ]
-                one = [line_sum.astype(F32) for line_sum in one]
-                down = pltpu.roll(one[0], 1, 0)
-                up = pltpu.roll(one[2], cols - 1, 0)
-                first = jnp.where(place == 0, before[r : r + 1], down[0:8])
-                last = jnp.where(place == 7, after[r : r + 1], up[cols - 8 :])
-                whole = (
-                    one[1]
-                    + jnp.concatenate([first, down[8:]], 0)
-                    + jnp.concatenate([up[: cols - 8], last], 0)
-                )
-                act = gelu_twice(whole)
-                act_ref[r, :, wide] = act.astype(BF16)
-                for s in range(0, cols, 8):
-                    total = total + act[s : s + 8]
-                window = [window[1], window[2], None]
+                act, part = conv_row(lines, short, before, after, place)
+                act_ref[i, :, wide] = act.astype(BF16)
+                total = total + part
             sums[:, wide] = total
         later = jnp.minimum(step + 1, steps - 1) * chunk
         rim_of(normed, w_ref[:, lanes_at(later, chunk)], rim, 1 - slot)
@@ -229,20 +312,18 @@
     squeeze_sums(sums, red_ref, part_ref)
 
 
-def conv(upper, lower, over, pair, left, right, weight, taps, reduce, copies, chunk=256):
-    half, cols, width = upper.shape
+def conv_outer(near, over, pair, left, right, weight, taps, reduce, sums, copies, chunk=256):
+    _, cols, width = near.shape
     channels = weight.shape[0]
-    outs = [((2 * half, cols, width), BF16), ((copies, reduce.shape[0]), F32)]
+    outs = [((2, cols, width), BF16), ((copies, reduce.shape[0]), F32)]
     scratch = [
         pltpu.VMEM((192, channels), BF16),
         pltpu.VMEM((2, 192, chunk), F32),
-        pltpu.VMEM((24, chunk), F32),
-        pltpu.VMEM((24, chunk), F32),
         pltpu.VMEM((8, width), F32),
     ]
-    args = (upper, lower, over, pair, left, right, weight, taps, reduce)
-    kernel = functools.partial(conv_kernel, chunk=chunk)
-    return resident(kernel, outs, args, scratch, 8, 8e9, "conv")
+    args = (near, over, pair, left, right, weight, taps, reduce, sums)
+    kernel = functools.partial(outer_kernel, chunk=chunk)
+    return resident(kernel, outs, args, scratch, 16, 2e9, "conv_outer")
 
 
 def gate_of(parts_ref, restore_ref, cell_count):
@@ -252,7 +333,7 @@
     return jax.nn.sigmoid(exact_dot(squeezed, restore_ref[...], ((1,), (0,))))
 
 
-def mix(x, qkv_ref, out_ref, up_ref, down_ref):
+def attend(x, qkv_ref, out_ref):
     cells, channels = x.shape
     width = channels // HEADS
     normed = layer_norm(x).astype(BF16)
@@ -285,25 +366,33 @@
                 )
             quads.append(picked)
         groups.append(jnp.concatenate(quads, 1).astype(BF16))
-    x = x + dot(jnp.concatenate(groups, 0), out_ref[...])
+    return x + dot(jnp.concatenate(groups, 0), out_ref[...])
+
+
+def feed(x, up_ref, down_ref):
     normed = half_norm(x).astype(BF16)
-    for c in range(0, up_ref.shape[1], 512):
-        hidden = gelu_twice(dot(normed, up_ref[:, c : c + 512])).astype(BF16)
-        x = x + dot(hidden, down_ref[c : c + 512, :])
-    return x
+    hidden = [
+        gelu_twice(dot(normed, up_ref[:, c : c + 256])).astype(BF16)
+        for c in range(0, up_ref.shape[1], 256)
+    ]
+    return x + dot(jnp.concatenate(hidden, 1), down_ref[...])
 
 
 def block_kernel(
-    img_ref, act_ref, parts_ref, restore_ref, project_ref, qkv_ref, out_ref, up_ref, down_ref,
-    res_ref, *, cell_count,
+    img_ref, act_ref, edge_ref, parts_ref, restore_ref, project_ref, qkv_ref, out_ref, up_ref,
+    down_ref, res_ref, middle, *, cell_count,
 ):
     rows, cols, channels = img_ref.shape
     cells = WIN * cols
     wide = cols // WIN
     gate = gate_of(parts_ref, restore_ref, cell_count)
-    for strip in range(rows // WIN):
+    acts = [
+        jnp.concatenate([edge_ref[0:1], act_ref[1:WIN]], 0),
+        jnp.concatenate([act_ref[WIN : rows - 1], edge_ref[1:2]], 0),
+    ]
+    for strip, act in enumerate(acts):
         mine = slice(strip * WIN, (strip + 1) * WIN)
-        scaled = act_ref[mine].reshape(cells, act_ref.shape[2]).astype(F32) * gate[0:1, :]
+        scaled = act.reshape(cells, act.shape[2]).astype(F32) * gate[0:1, :]
         x = img_ref[mine].reshape(cells, channels).astype(F32)
         x = x + dot(scaled.astype(BF16), project_ref[...])
         pieces = [
@@ -311,36 +400,40 @@
             for g in range(wide)
             for r in range(WIN)
         ]
-        y = mix(jnp.concatenate(pieces, 0), qkv_ref, out_ref, up_ref, down_ref)
+        y = attend(jnp.concatenate(pieces, 0), qkv_ref, out_ref)
         pieces = [
             y[g * CELLS + r * WIN : g * CELLS + (r + 1) * WIN]
             for r in range(WIN)
             for g in range(wide)
         ]
-        res_ref[strip * cells : (strip + 1) * cells, :] = jnp.concatenate(pieces, 0).astype(BF16)
-
-
-def block_part(image, act, parts, restore, project, qkv, out, up, down, cell_count):
+        middle[strip * cells : (strip + 1) * cells, :] = jnp.concatenate(pieces, 0)
+    res_ref[...] = feed(middle[...], up_ref, down_ref).astype(BF16)
+
+
+def block_part(image, act, edges, parts, restore, project, qkv, out, up, down, cell_count):
     rows, cols, channels = image.shape
     outs = [((rows * cols, channels), BF16)]
-    args = (image, act, parts, restore, project, qkv, out, up, down)
+    args = (image, act, edges, parts, restore, project, qkv, out, up, down)
+    scratch = [pltpu.VMEM((rows * cols, channels), F32)]
     kernel = functools.partial(block_kernel, cell_count=cell_count)
-    return resident(kernel, outs, args, [], 24, 12e9, "block_part")[0]
-
-
-def grid_kernel(x_ref, qkv_ref, out_ref, up_ref, down_ref, res_ref, before, after, *, batch):
+    return resident(kernel, outs, args, scratch, 24, 12e9, "block_part")[0]
+
+
+def grid_kernel(x_ref, qkv_ref, out_ref, up_ref, down_ref, res_ref, cells, middle, *, batch):
     groups = x_ref.shape[0] // CELLS
-    put(before, x_ref[...].astype(F32))
+    put(cells, x_ref[...].astype(F32))
     for start in range(0, groups, batch):
-        x = [take_strided(before, start + g, CELLS, groups) for g in range(batch)]
-        y = mix(jnp.concatenate(x, 0), qkv_ref, out_ref, up_ref, down_ref)
-        for g in range(batch):
-            put_strided(after, y[g * CELLS : (g + 1) * CELLS], start + g, CELLS, groups)
-    res_ref[...] = take(after).astype(BF16)
+        x = [take_strided(cells, start + g, CELLS, groups) for g in range(batch)]
+        y = attend(jnp.concatenate(x, 0), qkv_ref, out_ref)
+        middle[start * CELLS : (start + batch) * CELLS, :] = y
+    y = feed(middle[...], up_ref, down_ref)
+    for g in range(groups):
+        put_strided(cells, y[g * CELLS : (g + 1) * CELLS], g, CELLS, groups)
+    res_ref[...] = take(cells).astype(BF16)
 
 
 def grid_part(x, qkv, out, up, down, batch=8):
-    scratch = [panels(*x.shape), panels(*x.shape)]
+    scratch = [panels(*x.shape), pltpu.VMEM(x.shape, F32)]
     args = (x, qkv, out, up, down)
     kernel = functools.partial(grid_kernel, batch=batch)
     return resident(kernel, [(x.shape, BF16)], args, scratch, 24, 10e9, "grid_part")[0]
@@ -383,7 +476,7 @@
     steps = width // chunk
     copy = pltpu.make_async_copy(sec_ref, section_ref, sem)
     copy.start()
-    row, col = lax.axis_index("row_pair") + lax.axis_index("core"), lax.axis_index("cols")
+    row, col = lax.axis_index("row_pair") + lax.axis_index("core"), lax.axis_index(COLS)
     has_upper, has_left = flag(row > 0), flag(col > 0)
     put(cells, half_norm(upper_ref[...].astype(F32)) * has_upper)
     normed[0:32, :] = take_strided(cells, 0, 32, 2).astype(BF16)
@@ -490,13 +583,13 @@
 
 
 def shift_both(x):
-    rows, cols = lax.axis_size(ROWS), lax.axis_size("cols")
+    rows, cols = lax.axis_size(ROWS), lax.axis_size(COLS)
     pairs = [
         (r * cols + c, (r + 1) % rows * cols + (c + 1) % cols)
         for r in range(rows)
         for c in range(cols)
     ]
-    return lax.ppermute(x, ALL, pairs)
+    return lax.ppermute(x, AXES, pairs)
 
 
 def exchange(x):
@@ -514,12 +607,11 @@
     return arrived.reshape(count, squeezed)
 
 
-def row_rims(image, left, right):
-    rows, cols, channels = image.shape
+def row_rims(first, last, left, right):
     size = lax.axis_size(ROWS)
-    pad = jnp.zeros((14, channels), image.dtype)
-    first = jnp.concatenate([image[0], left[:1], right[:1], pad], 0)
-    last = jnp.concatenate([image[rows - 1], left[rows - 1 :], right[rows - 1 :], pad], 0)
+    pad = jnp.zeros((14, first.shape[1]), first.dtype)
+    first = jnp.concatenate([first, left[:1], right[:1], pad], 0)
+    last = jnp.concatenate([last, left[-1:], right[-1:], pad], 0)
     even = lax.axis_index("core") == 0
     away = jnp.where(even, first, last)
     near = jnp.where(even, last, first)
@@ -554,26 +646,24 @@
     rows, cols, channels = image.shape
     all_cells = rows * cols * lax.axis_size(ALL)
 
-    left = shift(image[:, cols - 1], "cols", 1)
-    right = shift(image[:, 0], "cols", -1)
-    upper = expand(image, mb_expand, 0, rows // 2)
-    left, right, upper = lax.optimization_barrier((left, right, upper))
-    over, pair = row_rims(image, left, right)
-    lower = expand(image, mb_expand, rows // 2, rows // 2)
-    act, part = conv(
-        upper, lower, over, pair, left, right, mb_expand, mb_taps, mb_reduce.T,
-        lax.axis_size(ALL),
+    left = shift(image[:, cols - 1], COLS, 1)
+    right = shift(image[:, 0], COLS, -1)
+    hidden, near, first, last = expand(image, mb_expand)
+    over, pair = row_rims(first, last, left, right)
+    act, sums = conv_inner(hidden, left, right, mb_expand, mb_taps)
+    edges, part = conv_outer(
+        near, over, pair, left, right, mb_expand, mb_taps, mb_reduce.T, sums, lax.axis_size(ALL)
     )
     parts = sum_parts(part)
     mixed = block_part(
-        image, act, parts, mb_restore, mb_project, block_qkv, block_out, first_up, first_down,
+        image, act, edges, parts, mb_restore, mb_project, block_qkv, block_out, first_up, first_down,
         all_cells,
     )
     mixed = grid_part(exchange(mixed), grid_qkv, grid_out, second_up, second_down)
     section = exchange(mixed).reshape(rows, cols, channels)
 
     upper = shift(section[rows - 1], ROWS, 1)
-    left = shift(section[:, cols - 1], "cols", 1)
+    left = shift(section[:, cols - 1], COLS, 1)
     corner = shift_both(section[rows - 1, cols - 1 :])
     hidden, pooled = down_expand_part(section, down_expand)
     act, part, whole = down_conv(
@@ -589,8 +679,8 @@
 
 def solution(mesh):
     rows, cols = mesh.devices.shape
-    fine = Mesh(np.asarray(mesh.devices).reshape(rows // 2, 2, cols), ALL)
-    tile = P(ROWS, "cols", None)
+    fine = Mesh(np.asarray(mesh.devices).reshape(rows // 2, 2, cols // 2, 2), AXES)
+    tile = P(ROWS, COLS, None)
     in_specs = (tile,) + (P(),) * 19
     return jax.shard_map(
         local, mesh=fine, in_specs=in_specs, out_specs=(tile, tile), check_vma=False

time: 136 us -> 134 us (0.985)
  blocking collectives: 73.6 us -> 68.2 us
  starting transfers between devices: 15.5 us -> 17.3 us
    pallas_call x2, Pallas kernels: 5.31 us -> 13.5 us  [the longest x1 7.45 us: conv_inner(): pl.pallas_call(inner_kernel, grid=(steps,), in_specs=[tall, whole(left),...]
    pallas_call x4, Pallas kernels: 32 us -> 24.9 us  [resident(): pl.pallas_call(kernel, in_specs=[here] * len(args), out_specs=[here] * le...]
    all_to_all x2, blocking collectives: 39.4 us -> 36.5 us  [exchange(): lax.all_to_all(pieces, CLASS, split_axis=0, concat_axis=0, tiled=True)]
    all_to_all x2, blocking collectives: 34.2 us -> 31.7 us  [sum_parts(): arrived = lax.all_to_all(part, ALL, split_axis=0, concat_axis=0, tiled=True)]
    ppermute x4, starting transfers between devices: 10.1 us -> 12.2 us  [shift(): return lax.ppermute(x, axes, [(i, (i + by) % size) for i in range(size)])]
    ppermute x1, waiting for transfers between devices: 0.01 us -> 1.9 us  [shift_both(): return lax.ppermute(x, AXES, pairs)]
  transfers between devices with their start and end apart: 7 -> 7, of which waited for: 1 -> 1; matrix products, arithmetic and copies ran while one was open for 1% -> 0% of each run, Pallas kernels for 6% -> 12%
where the time goes in v5:
time: 134 us; the launch traced here: 133 us
  blocking collectives  68.2 us (51%)
  Pallas kernels  43.7 us (33%)
  starting transfers between devices  17.3 us (13%)
  waiting for transfers between devices  1.92 us (1%)
    all_to_all x2, blocking collectives, exchange(): lax.all_to_all(pieces, CLASS, split_axis=0, concat_axis=0, tiled=True)  36.5 us
    all_to_all x2, blocking collectives, sum_parts(): arrived = lax.all_to_all(part, ALL, split_axis=0, concat_axis=0, tiled=True)  31.7 us
    pallas_call x4, Pallas kernels, resident(): pl.pallas_call(kernel, in_specs=[here] * len(args), out_specs=[here] * le...  24.9 us
    ppermute x4, starting transfers between devices, shift(): return lax.ppermute(x, axes, [(i, (i + by) % size) for i in range(size)])  12.2 us
    pallas_call x1, Pallas kernels, conv_inner(): pl.pallas_call(inner_kernel, grid=(steps,), in_specs=[tall, whole(left),...  7.45 us
    pallas_call x1, Pallas kernels, expand(): pl.pallas_call(expand_kernel, grid=(rows // block,), in_specs=[pl.BlockSp...  6.06 us
    pallas_call x1, Pallas kernels, down_conv(): pl.pallas_call(functools.partial(down_conv_kernel, chunk=chunk), in_specs...  3.34 us
  transfers between devices with their start and end apart: 7, of which 1 were waited for; matrix products, arithmetic and copies ran while one was open for 0% of the time, Pallas kernels for 12%

profile of v5, /device:TPU:1, one launch (start us, length us, event | category | flops | bytes accessed | tf_op | source)
XLA Modules:
  0.0 133.4 jit_solution(1273087210312267776)
XLA Ops:
  0.6 1.0 fusion
  1.6 3.8 %collective-permute-start = (bf16[16,384]{1,0:T(8,128)(2,1)S(1)}, bf16[16,384]{1,0:T(8,128)(2,1)S(1)}, u32[]{:S(2)}, u32[]{:S(2)}) collective-permute-start(bf16[16,384]{1,0:T(8,128)(2,1)S(1)} %bitcast.40), channel_id=1, source_target_pairs={{0,1},{1,2},{2,3},{3,4},{4,5},{5,6},{6,7},{7,0},{8,9},{9,10},{10,1... | collective-permute-start | bytes 36872 | tf_op jit(solution)/shard_map/ppermute | solution.py:582
  5.5 3.6 %collective-permute-start.1 = (bf16[16,384]{1,0:T(8,128)(2,1)S(1)}, bf16[16,384]{1,0:T(8,128)(2,1)S(1)}, u32[]{:S(2)}, u32[]{:S(2)}) collective-permute-start(bf16[16,384]{1,0:T(8,128)(2,1)S(1)} %bitcast.41), channel_id=1, source_target_pairs={{0,7},{1,0},{2,1},{3,2},{4,3},{5,4},{6,5},{7,6},{8,15},{9,8},{10,9... | collective-permute-start | bytes 36872 | tf_op jit(solution)/shard_map/ppermute | solution.py:582
  9.0 6.1 %expand.1 = (bf16[16,64,1536]{2,1,0:T(8,128)(2,1)}, bf16[4,64,1536]{2,1,0:T(8,128)(2,1)S(1)}, bf16[64,384]{1,0:T(8,128)(2,1)S(1)}, bf16[64,384]{1,0:T(8,128)(2,1)S(1)}) custom-call(bf16[16,64,384]{2,1,0:T(8,128)(2,1)} %img_ref.1, bf16[384,1536]{1,0:T(8,128)(2,1)} %w_ref.7), custom_call_target="tpu_custom_call" | custom-call | flops 4000000000 | bytes 1048576 | tf_op jit(solution)/shard_map/expand/pallas_call | solution.py:124
  15.1 0.1 pad.7.clone
  15.2 0.0 collective-permute-done.1.right_ref
  15.2 0.0 collective-permute-done.left_ref
  15.2 0.1 broadcast_select_fusion
  15.3 2.1 %collective-permute-start.2 = (bf16[80,384]{1,0:T(8,128)(2,1)S(1)}, bf16[80,384]{1,0:T(8,128)(2,1)S(1)}, u32[]{:S(2)}, u32[]{:S(2)}) collective-permute-start(bf16[80,384]{1,0:T(8,128)(2,1)S(1)} %get-tuple-element.31), channel_id=1, source_target_pairs={{0,120},{8,16},{16,8},{24,32},{32,24},{40,48},{48,40},{56,64},{64,... | collective-permute-start | bytes 184328 | tf_op jit(solution)/shard_map/ppermute | solution.py:619
  17.5 0.9 collective-permute-start.3
  18.4 0.0 copy-done.7
  18.4 0.0 copy-done.19
  18.4 7.4 %conv_inner.1 = (bf16[16,64,1536]{2,1,0:T(8,128)(2,1)S(1)}, f32[8,1536]{1,0:T(8,128)S(1)}) custom-call(bf16[16,64,1536]{2,1,0:T(8,128)(2,1)} %get-tuple-element.15.hid_ref, bf16[16,384]{1,0:T(8,128)(2,1)S(1)} %collective-permute-done.left_ref, bf16[16,384]{1,0:T(8,128)(2,1)S(1)} %collective-permute-done.1.right_ref, bf16[384,1536]{1,0:T(8,128)(2,1)S(1)} %copy-done.7, ...), custom_call_target="tpu_custom_call" | custom-call | flops 7000000000 | bytes 1048576 | tf_op jit(solution)/shard_map/conv_inner/pallas_call | solution.py:235
  25.9 0.0 collective-permute-done.2.over_ref
  25.9 0.0 collective-permute-done.3.pair_ref
  25.9 0.0 copy-done.15
  25.9 0.0 copy-start.6
  25.9 0.0 copy-start.8
  25.9 0.0 copy-start.9
  25.9 0.0 copy-start.10
  25.9 0.0 copy-start.13
  25.9 0.0 copy-start.16
  26.0 0.0 copy-start.17
  26.0 2.4 %conv_outer.1 = (bf16[2,64,1536]{2,1,0:T(8,128)(2,1)S(1)}, f32[128,96]{1,0:T(8,128)S(1)}) custom-call(bf16[4,64,1536]{2,1,0:T(8,128)(2,1)S(1)} %get-tuple-element.17.near_ref, bf16[80,384]{1,0:T(8,128)(2,1)S(1)} %collective-permute-done.2.over_ref, bf16[80,384]{1,0:T(8,128)(2,1)S(1)} %collective-permute-done.3.pair_ref, ...), custom_call_target="tpu_custom_call" | custom-call | flops 2000000000 | bytes 1048576 | tf_op jit(solution)/shard_map/conv_outer/pallas_call | solution.py:35
  28.4 15.8 %all_to_all.20 = f32[128,1,96]{2,1,0:T(1,128)S(1)} all-to-all(f32[128,1,96]{2,1,0:T(1,128)S(1)} %bitcast.35), channel_id=1, replica_groups=mesh['row_pair'=8,'core'=2,'depth'=4,'col_pair'=2] {'core','row_pair','c..., dimensions={0} | all-to-all | bytes 98304 | tf_op jit(solution)/shard_map/all_to_all | solution.py:606
  44.2 0.0 copy-done.6
  44.2 0.0 copy-done.8
  44.2 0.0 copy-done.9
  44.2 0.0 copy-done.10
  44.2 0.0 copy-done.13
  44.2 0.0 copy-done.16
  44.2 0.0 copy-done.17
  44.2 0.0 copy-start.12
  44.2 0.0 copy-start.14
  44.3 10.6 %block_part.1 = bf16[1024,384]{1,0:T(8,128)(2,1)S(1)} custom-call(bf16[16,64,384]{2,1,0:T(8,128)(2,1)S(1)} %copy-done.6, bf16[16,64,1536]{2,1,0:T(8,128)(2,1)S(1)} %get-tuple-element.16.act_ref, bf16[2,64,1536]{2,1,0:T(8,128)(2,1)S(1)} %get-tuple-element.21.edge_ref, f32[128,96]{1,0:T(8,128)S(1)} %bitcast.37, bf16[96,1536]{1,0:T(8,128)(2,1)S(1)} %copy-done.16, ...), custom_call_target="tpu_custom_call" | custom-call | flops 12000000000 | bytes 1048576 | tf_op jit(solution)/shard_map/block_part/pallas_call | solution.py:35
  54.9 0.0 copy-start.11
  54.9 0.0 copy-start.18
  54.9 18.0 %all_to_all.21 = bf16[64,16,384]{2,1,0:T(8,128)(2,1)S(1)} all-to-all(bf16[64,16,384]{2,1,0:T(8,128)(2,1)S(1)} %bitcast.30), channel_id=1, replica_groups=mesh['row_pair'=8,'core'=2,'depth'=4,'col_pair'=2] {'row_pair','col_pair..., dimensions={0} | all-to-all | bytes 1572864 | tf_op jit(solution)/shard_map/all_to_all | solution.py:599
  72.9 0.0 copy-done.12
  72.9 0.0 copy-done.14
  72.9 0.0 copy-done.11
  72.9 0.0 copy-done.18
  72.9 9.2 %grid_part.1 = bf16[1024,384]{1,0:T(8,128)(2,1)S(1)} custom-call(bf16[1024,384]{1,0:T(8,128)(2,1)S(1)} %bitcast.31, bf16[384,1152]{1,0:T(8,128)(2,1)S(1)} %copy-done.14, bf16[384,384]{1,0:T(8,128)(2,1)S(1)} %copy-done.18, bf16[384,1536]{1,0:T(8,128)(2,1)S(1)} %copy-done.11, bf16[1536,384]{1,0:T(8,128)(2,1)S(1)} %copy-done.12), custom_call_target="tpu_custom_call" | custom-call | flops 10000000000 | bytes 1048576 | tf_op jit(solution)/shard_map/grid_part/pallas_call | solution.py:35
  82.1 0.0 copy-start.1
  82.1 18.6 %all_to_all.22 = bf16[64,16,384]{2,1,0:T(8,128)(2,1)S(1)} all-to-all(bf16[64,16,384]{2,1,0:T(8,128)(2,1)S(1)} %bitcast.32), channel_id=1, replica_groups=mesh['row_pair'=8,'core'=2,'depth'=4,'col_pair'=2] {'row_pair','col_pair..., dimensions={0} | all-to-all | bytes 1572864 | tf_op jit(solution)/shard_map/all_to_all | solution.py:599
  100.8 3.6 %collective-permute-start.4 = (bf16[64,384]{1,0:T(8,128)(2,1)S(1)}, bf16[64,384]{1,0:T(8,128)(2,1)S(1)}, u32[]{:S(2)}, u32[]{:S(2)}) collective-permute-start(bf16[64,384]{1,0:T(8,128)(2,1)S(1)} %bitcast.39), channel_id=1, source_target_pairs={{0,8},{8,16},{16,24},{24,32},{32,40},{40,48},{48,56},{56,64},{64,7... | collective-permute-start | bytes 147464 | tf_op jit(solution)/shard_map/ppermute | solution.py:582
  104.4 1.2 collective-permute-start.5
  105.6 2.0 %collective-permute-start.6 = (bf16[1,384]{1,0:T(2,128)(2,1)S(1)}, bf16[1,384]{1,0:T(2,128)(2,1)S(1)}, u32[]{:S(2)}, u32[]{:S(2)}) collective-permute-start(bf16[1,384]{1,0:T(2,128)(2,1)S(1)} %slice_bitcast_fusion), channel_id=1, source_target_pairs={{0,9},{1,10},{2,11},{3,12},{4,13},{5,14},{6,15},{7,8},{8,17},{9,18... | collective-permute-start | bytes 2312 | tf_op jit(solution)/shard_map/ppermute | solution.py:592
  107.6 0.0 copy-done.1
  107.6 2.7 %down_expand.1 = (bf16[16,2,32,1536]{3,2,1,0:T(8,128)(2,1)S(1)}, bf16[8,32,384]{2,1,0:T(8,128)(2,1)S(1)}) custom-call(bf16[16,64,384]{2,1,0:T(8,128)(2,1)S(1)} %bitcast.28, bf16[384,1536]{1,0:T(8,128)(2,1)S(1)} %copy-done.1), custom_call_target="tpu_custom_call" | custom-call | flops 2415919104 | bytes 1048576 | tf_op jit(solution)/shard_map/down_expand/pallas_call | solution.py:35
  110.4 1.9 %collective-permute-done.6.corner_ref = bf16[1,384]{1,0:T(2,128)(2,1)S(1)} collective-permute-done((bf16[1,384]{1,0:T(2,128)(2,1)S(1)}, bf16[1,384]{1,0:T(2,128)(2,1)S(1)}, u32[]{:S(2)}, u32[]{:S(2)}) %collective-permute-start.6) | collective-permute-done | bytes 800 | tf_op jit(solution)/shard_map/ppermute | solution.py:592
  112.3 0.0 collective-permute-done.5.left_ref
  112.3 0.0 collective-permute-done.4.upper_ref
  112.3 0.0 copy-done.3
  112.3 0.0 copy-done.5
  112.3 0.0 copy-start
  112.3 0.0 copy-start.2
  112.3 0.0 copy-start.4
  112.3 3.3 %down_conv.1 = (bf16[8,32,1536]{2,1,0:T(8,128)(2,1)S(1)}, f32[128,96]{1,0:T(8,128)S(1)}, bf16[16,64,384]{2,1,0:T(8,128)(2,1)}) custom-call(bf16[16,2,32,1536]{3,2,1,0:T(8,128)(2,1)S(1)} %get-tuple-element.23.hid_ref, bf16[16,64,384]{2,1,0:T(8,128)(2,1)S(1)} %bitcast.29, bf16[64,384]{1,0:T(8,128)(2,1)S(1)} %collective-permute-done.4.upper_ref, ...), custom_call_target="tpu_custom_call" | custom-call | tf_op jit(solution)/shard_map/down_conv/pallas_call | solution.py:532
  115.7 15.9 %all_to_all.23 = f32[128,1,96]{2,1,0:T(1,128)S(1)} all-to-all(f32[128,1,96]{2,1,0:T(1,128)S(1)} %bitcast.36), channel_id=1, replica_groups=mesh['row_pair'=8,'core'=2,'depth'=4,'col_pair'=2] {'core','row_pair','c..., dimensions={0} | all-to-all | bytes 98304 | tf_op jit(solution)/shard_map/all_to_all | solution.py:606
  131.5 0.0 copy-done
  131.5 0.0 copy-done.2
  131.5 0.0 copy-done.4
  131.5 1.9 %down_out.1 = bf16[8,32,768]{2,1,0:T(8,128)(2,1)} custom-call(bf16[8,32,1536]{2,1,0:T(8,128)(2,1)S(1)} %get-tuple-element.25.act_ref, bf16[8,32,384]{2,1,0:T(8,128)(2,1)S(1)} %get-tuple-element.26.pool_ref, f32[128,96]{1,0:T(8,128)S(1)} %bitcast.34, bf16[96,1536]{1,0:T(8,128)(2,1)S(1)} %copy-done.4, bf16[1536,768]{1,0:T(8,128)(2,1)S(1)} %copy-done, ...), custom_call_target="tpu_custom_call" | custom-call | tf_op jit(solution)/shard_map/down_out/pallas_call | solution.py:570
  (14 shorter events, 0.1 us)
Async XLA Ops:
  1.6 13.6 %collective-permute-start = (bf16[16,384]{1,0:T(8,128)(2,1)S(1)}, bf16[16,384]{1,0:T(8,128)(2,1)S(1)}, u32[]{:S(2)}, u32[]{:S(2)}) collective-permute-start(bf16[16,384]{1,0:T(8,128)(2,1)S(1)} %bitcast.40), channel_id=1, source_target_pairs={{0,1},{1,2},{2,3},{3,4},{4,5},{5,6},{6,7},{7,0},{8,9},{9,10},{10,1... | collective-permute-start | bytes 36872 | tf_op jit(solution)/shard_map/ppermute | solution.py:582
  5.4 12.9 %copy-start.7 = (bf16[384,1536]{1,0:T(8,128)(2,1)S(1)}, bf16[384,1536]{1,0:T(8,128)(2,1)}, u32[]{:S(2)}) copy-start(bf16[384,1536]{1,0:T(8,128)(2,1)} %w_ref.7) | copy-start | bytes 3538948
  5.5 12.9 %copy-start.19 = (bf16[9,1536]{1,0:T(8,128)(2,1)S(1)}, bf16[9,1536]{1,0:T(8,128)(2,1)}, u32[]{:S(2)}) copy-start(bf16[9,1536]{1,0:T(8,128)(2,1)} %taps_ref.4) | copy-start | bytes 82948
  5.5 9.7 %collective-permute-start.1 = (bf16[16,384]{1,0:T(8,128)(2,1)S(1)}, bf16[16,384]{1,0:T(8,128)(2,1)S(1)}, u32[]{:S(2)}, u32[]{:S(2)}) collective-permute-start(bf16[16,384]{1,0:T(8,128)(2,1)S(1)} %bitcast.41), channel_id=1, source_target_pairs={{0,7},{1,0},{2,1},{3,2},{4,3},{5,4},{6,5},{7,6},{8,15},{9,8},{10,9... | collective-permute-start | bytes 36872 | tf_op jit(solution)/shard_map/ppermute | solution.py:582
  15.3 10.5 %collective-permute-start.2 = (bf16[80,384]{1,0:T(8,128)(2,1)S(1)}, bf16[80,384]{1,0:T(8,128)(2,1)S(1)}, u32[]{:S(2)}, u32[]{:S(2)}) collective-permute-start(bf16[80,384]{1,0:T(8,128)(2,1)S(1)} %get-tuple-element.31), channel_id=1, source_target_pairs={{0,120},{8,16},{16,8},{24,32},{32,24},{40,48},{48,40},{56,64},{64,... | collective-permute-start | bytes 184328 | tf_op jit(solution)/shard_map/ppermute | solution.py:619
  17.5 8.4 %collective-permute-start.3 = (bf16[80,384]{1,0:T(8,128)(2,1)S(1)}, bf16[80,384]{1,0:T(8,128)(2,1)S(1)}, u32[]{:S(2)}, u32[]{:S(2)}) collective-permute-start(bf16[80,384]{1,0:T(8,128)(2,1)S(1)} %get-tuple-element.30), channel_id=1, source_target_pairs={{0,8},{8,0},{1,9},{9,1},{2,10},{10,2},{3,11},{11,3},{4,12},{12,4},... | collective-permute-start | bytes 184328 | tf_op jit(solution)/shard_map/ppermute | solution.py:620
  18.4 7.5 %copy-start.15 = (bf16[1536,96]{0,1:T(8,128)(2,1)S(1)}, bf16[1536,96]{0,1:T(8,128)(2,1)}, u32[]{:S(2)}) copy-start(bf16[1536,96]{0,1:T(8,128)(2,1)} %param.23) | copy-start | bytes 884740
  25.9 18.3 %copy-start.6 = (bf16[16,64,384]{2,1,0:T(8,128)(2,1)S(1)}, bf16[16,64,384]{2,1,0:T(8,128)(2,1)}, u32[]{:S(2)}) copy-start(bf16[16,64,384]{2,1,0:T(8,128)(2,1)} %img_ref.1) | copy-start | bytes 2359300
  25.9 18.3 %copy-start.8 = (bf16[1536,384]{1,0:T(8,128)(2,1)S(1)}, bf16[1536,384]{1,0:T(8,128)(2,1)}, u32[]{:S(2)}) copy-start(bf16[1536,384]{1,0:T(8,128)(2,1)} %project_ref.2) | copy-start | bytes 3538948
  25.9 18.3 %copy-start.9 = (bf16[384,1536]{1,0:T(8,128)(2,1)S(1)}, bf16[384,1536]{1,0:T(8,128)(2,1)}, u32[]{:S(2)}) copy-start(bf16[384,1536]{1,0:T(8,128)(2,1)} %up_ref.2) | copy-start | bytes 3538948
  25.9 18.3 %copy-start.10 = (bf16[1536,384]{1,0:T(8,128)(2,1)S(1)}, bf16[1536,384]{1,0:T(8,128)(2,1)}, u32[]{:S(2)}) copy-start(bf16[1536,384]{1,0:T(8,128)(2,1)} %down_ref.2) | copy-start | bytes 3538948
  25.9 18.3 %copy-start.13 = (bf16[384,1152]{1,0:T(8,128)(2,1)S(1)}, bf16[384,1152]{1,0:T(8,128)(2,1)}, u32[]{:S(2)}) copy-start(bf16[384,1152]{1,0:T(8,128)(2,1)} %qkv_ref.2) | copy-start | bytes 2654212
  25.9 18.3 %copy-start.16 = (bf16[96,1536]{1,0:T(8,128)(2,1)S(1)}, bf16[96,1536]{1,0:T(8,128)(2,1)}, u32[]{:S(2)}) copy-start(bf16[96,1536]{1,0:T(8,128)(2,1)} %restore_ref.2) | copy-start | bytes 884740
  26.0 18.3 %copy-start.17 = (bf16[384,384]{1,0:T(8,128)(2,1)S(1)}, bf16[384,384]{1,0:T(8,128)(2,1)}, u32[]{:S(2)}) copy-start(bf16[384,384]{1,0:T(8,128)(2,1)} %out_ref.2) | copy-start | bytes 884740
  44.2 28.6 %copy-start.12 = (bf16[1536,384]{1,0:T(8,128)(2,1)S(1)}, bf16[1536,384]{1,0:T(8,128)(2,1)}, u32[]{:S(2)}) copy-start(bf16[1536,384]{1,0:T(8,128)(2,1)} %down_ref.3) | copy-start | bytes 3538948
  44.2 28.6 %copy-start.14 = (bf16[384,1152]{1,0:T(8,128)(2,1)S(1)}, bf16[384,1152]{1,0:T(8,128)(2,1)}, u32[]{:S(2)}) copy-start(bf16[384,1152]{1,0:T(8,128)(2,1)} %qkv_ref.3) | copy-start | bytes 2654212
  54.9 18.0 %copy-start.11 = (bf16[384,1536]{1,0:T(8,128)(2,1)S(1)}, bf16[384,1536]{1,0:T(8,128)(2,1)}, u32[]{:S(2)}) copy-start(bf16[384,1536]{1,0:T(8,128)(2,1)} %up_ref.3) | copy-start | bytes 3538948
  54.9 18.0 %copy-start.18 = (bf16[384,384]{1,0:T(8,128)(2,1)S(1)}, bf16[384,384]{1,0:T(8,128)(2,1)}, u32[]{:S(2)}) copy-start(bf16[384,384]{1,0:T(8,128)(2,1)} %out_ref.3) | copy-start | bytes 884740
  82.1 25.5 %copy-start.1 = (bf16[384,1536]{1,0:T(8,128)(2,1)S(1)}, bf16[384,1536]{1,0:T(8,128)(2,1)}, u32[]{:S(2)}) copy-start(bf16[384,1536]{1,0:T(8,128)(2,1)} %w_ref.9) | copy-start | bytes 3538948
  100.8 11.5 %collective-permute-start.4 = (bf16[64,384]{1,0:T(8,128)(2,1)S(1)}, bf16[64,384]{1,0:T(8,128)(2,1)S(1)}, u32[]{:S(2)}, u32[]{:S(2)}) collective-permute-start(bf16[64,384]{1,0:T(8,128)(2,1)S(1)} %bitcast.39), channel_id=1, source_target_pairs={{0,8},{8,16},{16,24},{24,32},{32,40},{40,48},{48,56},{56,64},{64,7... | collective-permute-start | bytes 147464 | tf_op jit(solution)/shard_map/ppermute | solution.py:582
  104.4 7.9 %copy-start.3 = (bf16[1536,96]{0,1:T(8,128)(2,1)S(1)}, bf16[1536,96]{0,1:T(8,128)(2,1)}, u32[]{:S(2)}) copy-start(bf16[1536,96]{0,1:T(8,128)(2,1)} %param.36) | copy-start | bytes 884740
  104.4 7.9 %copy-start.5 = (bf16[9,1536]{1,0:T(8,128)(2,1)S(1)}, bf16[9,1536]{1,0:T(8,128)(2,1)}, u32[]{:S(2)}) copy-start(bf16[9,1536]{1,0:T(8,128)(2,1)} %taps_ref.5) | copy-start | bytes 82948
  104.4 7.8 %collective-permute-start.5 = (bf16[16,384]{1,0:T(8,128)(2,1)S(1)}, bf16[16,384]{1,0:T(8,128)(2,1)S(1)}, u32[]{:S(2)}, u32[]{:S(2)}) collective-permute-start(bf16[16,384]{1,0:T(8,128)(2,1)S(1)} %bitcast.42), channel_id=1, source_target_pairs={{0,1},{1,2},{2,3},{3,4},{4,5},{5,6},{6,7},{7,0},{8,9},{9,10},{10,1... | collective-permute-start | bytes 36872 | tf_op jit(solution)/shard_map/ppermute | solution.py:582
  105.6 6.6 %collective-permute-start.6 = (bf16[1,384]{1,0:T(2,128)(2,1)S(1)}, bf16[1,384]{1,0:T(2,128)(2,1)S(1)}, u32[]{:S(2)}, u32[]{:S(2)}) collective-permute-start(bf16[1,384]{1,0:T(2,128)(2,1)S(1)} %slice_bitcast_fusion), channel_id=1, source_target_pairs={{0,9},{1,10},{2,11},{3,12},{4,13},{5,14},{6,15},{7,8},{8,17},{9,18... | collective-permute-start | bytes 2312 | tf_op jit(solution)/shard_map/ppermute | solution.py:592
  112.3 19.2 %copy-start = (bf16[1536,768]{1,0:T(8,128)(2,1)S(1)}, bf16[1536,768]{1,0:T(8,128)(2,1)}, u32[]{:S(2)}) copy-start(bf16[1536,768]{1,0:T(8,128)(2,1)} %project_ref.3) | copy-start | bytes 7077892
  112.3 19.2 %copy-start.2 = (bf16[384,768]{1,0:T(8,128)(2,1)S(1)}, bf16[384,768]{1,0:T(8,128)(2,1)}, u32[]{:S(2)}) copy-start(bf16[384,768]{1,0:T(8,128)(2,1)} %short_ref.1) | copy-start | bytes 1769476
  112.3 19.2 %copy-start.4 = (bf16[96,1536]{1,0:T(8,128)(2,1)S(1)}, bf16[96,1536]{1,0:T(8,128)(2,1)}, u32[]{:S(2)}) copy-start(bf16[96,1536]{1,0:T(8,128)(2,1)} %restore_ref.3) | copy-start | bytes 884740

commit v6 on v5

--- a/solution.py
+++ b/solution.py
@@ -98,51 +98,52 @@
     )
 
 
-def expand_kernel(x_ref, w_ref, out_ref, near_ref, first_ref, last_ref):
-    step = pl.program_id(0)
-    rows, cols, channels = x_ref.shape
-    normed = half_norm(x_ref[...].reshape(rows * cols, channels).astype(F32)).astype(BF16)
-    for c in range(0, w_ref.shape[1], 256):
-        wide = gelu_twice(dot(normed, w_ref[:, c : c + 256])).astype(BF16)
-        out_ref[:, :, c : c + 256] = wide.reshape(rows, cols, 256)
-
-    @pl.when(step == 0)
-    def _():
-        near_ref[0:2] = out_ref[0:2]
+def expand_upper(image, weight):
+    rows, cols, channels = image.shape
+    half, hidden = rows // 2, weight.shape[1]
+
+    def kernel(
+        x_hbm, w_hbm, up_ref, near_ref, first_ref, last_ref, x_ref, w_ref, x_sem, w_sem, last_sem
+    ):
+        x_copy = pltpu.make_async_copy(x_hbm.at[0:half], x_ref, x_sem)
+        w_copy = pltpu.make_async_copy(w_hbm, w_ref, w_sem)
+        last_copy = pltpu.make_async_copy(x_hbm.at[rows - 1], last_ref, last_sem)
+        x_copy.start()
+        w_copy.start()
+        last_copy.start()
+        x_copy.wait()
         first_ref[...] = x_ref[0]
-
-    @pl.when(step == pl.num_programs(0) - 1)
-    def _():
-        near_ref[2:4] = out_ref[rows - 2 : rows]
-        last_ref[...] = x_ref[rows - 1]
-
-
-def expand(image, weight, block=4):
-    rows, cols, channels = image.shape
-    hidden = weight.shape[1]
-    still = lambda *shape: pl.BlockSpec(shape, lambda i: (0,) * len(shape))
+        normed = half_norm(x_ref[...].reshape(half * cols, channels).astype(F32)).astype(BF16)
+        w_copy.wait()
+        for c in range(0, hidden, 256):
+            wide = gelu_twice(dot(normed, w_ref[:, c : c + 256])).astype(BF16)
+            wide = wide.reshape(half, cols, 256)
+            up_ref[:, :, c : c + 256] = wide
+            near_ref[:, :, c : c + 256] = wide[0:2]
+        last_copy.wait()
+
+    away = pl.BlockSpec(memory_space=pl.ANY)
+    here = pl.BlockSpec(memory_space=pltpu.VMEM)
     return pl.pallas_call(
-        expand_kernel,
-        grid=(rows // block,),
-        in_specs=[
-            pl.BlockSpec((block, cols, channels), lambda i: (i, 0, 0)),
-            still(channels, hidden),
+        kernel,
+        in_specs=[away, away],
+        out_specs=[here] * 4,
+        out_shape=[
+            pltpu.VMEM((half, cols, hidden), BF16),
+            pltpu.VMEM((2, cols, hidden), BF16),
+            pltpu.VMEM((cols, channels), BF16),
+            pltpu.VMEM((cols, channels), BF16),
         ],
-        out_specs=[
-            pl.BlockSpec((block, cols, hidden), lambda i: (i, 0, 0)),
-            still(4, cols, hidden),
-            still(cols, channels),
-            still(cols, channels),
-        ],
-        out_shape=[
-            pltpu.HBM((rows, cols, hidden), BF16),
-            jax.ShapeDtypeStruct((4, cols, hidden), BF16),
-            jax.ShapeDtypeStruct((cols, channels), BF16),
-            jax.ShapeDtypeStruct((cols, channels), BF16),
+        scratch_shapes=[
+            pltpu.VMEM((half, cols, channels), BF16),
+            pltpu.VMEM(weight.shape, BF16),
+            pltpu.SemaphoreType.DMA,
+            pltpu.SemaphoreType.DMA,
+            pltpu.SemaphoreType.DMA,
         ],
         compiler_params=params(16),
-        cost_estimate=pl.CostEstimate(flops=int(4e9), bytes_accessed=1 << 20, transcendentals=0),
-        name="expand",
+        cost_estimate=pl.CostEstimate(flops=int(2e9), bytes_accessed=1 << 20, transcendentals=0),
+        name="expand_upper",
     )(*[pltpu.with_memory_space_constraint(a, pltpu.HBM) for a in (image, weight)])
 
 
@@ -196,69 +197,95 @@
 
 
 def inner_kernel(
-    hid_ref, left_ref, right_ref, start_ref, w_ref, taps_ref, act_ref, sums_ref, normed, rim
+    x_hbm, up_ref, left_ref, right_ref, w_ref, taps_ref, act_ref, sums_ref, near_ref,
+    x_ref, x_normed, low, normed, rim, x_sem, *, chunk,
 ):
-    step = pl.program_id(0)
-    rows, cols, chunk = hid_ref.shape
-    slot = step % 2
-
-    @pl.when(step == 0)
-    def _():
-        side_norms(normed, 0, left_ref, right_ref)
-        rim_of(normed, start_ref[...], rim, 0)
-
+    rows, cols, width = act_ref.shape
+    half = rows // 2
+    steps = width // chunk
+    copy = pltpu.make_async_copy(x_hbm.at[half:rows], x_ref, x_sem)
+    copy.start()
+    side_norms(normed, 0, left_ref, right_ref)
+    rim_of(normed, w_ref[:, :chunk], rim, 0)
+    copy.wait()
+    x = x_ref[...].reshape(half * cols, x_ref.shape[2]).astype(F32)
+    x_normed[...] = half_norm(x).astype(BF16)
+
+    def expand_lower(step, slot):
+        weight = w_ref[:, lanes_at(step * chunk, chunk)]
+        wide = gelu_twice(dot(x_normed[...], weight)).astype(BF16).reshape(half, cols, chunk)
+        low[slot] = wide
+        near_ref[:, :, lanes_at(step * chunk, chunk)] = wide[half - 2 :]
+        return weight
+
+    expand_lower(0, 0)
     place = lax.broadcasted_iota(jnp.int32, (8, 128), 0)
     inner = rows - 2
-    for lane in range(0, chunk, 128):
-        lanes = slice(lane, lane + 128)
-        taps, short = half_taps(taps_ref, lanes)
-        before = sum(taps[3 * a] * rim[slot, a : a + inner, lanes] for a in range(3))
-        after = sum(taps[3 * a + 2] * rim[slot, 16 + a : 16 + a + inner, lanes] for a in range(3))
-        total = jnp.zeros((8, 128), F32)
-        lines = [hid_ref[0, :, lanes], hid_ref[1, :, lanes], None]
-        for r in range(1, rows - 1):
-            lines[2] = hid_ref[r + 1, :, lanes]
-            act, part = conv_row(lines, short, before[r - 1 : r], after[r - 1 : r], place)
-            act_ref[r, :, lanes] = act.astype(BF16)
-            total = total + part
-            lines = [lines[1], lines[2], None]
-        sums_ref[:, lanes] = total
-    rim_of(normed, w_ref[...], rim, 1 - slot)
-
-
-def conv_inner(hidden, left, right, weight, taps, chunk=256):
-    rows, cols, width = hidden.shape
-    channels = weight.shape[0]
-    steps = width // chunk
-    whole = lambda a: pl.BlockSpec(a.shape, lambda c: (0, 0))
-    tall = pl.BlockSpec((rows, cols, chunk), lambda c: (0, 0, c))
+
+    def advance(step, carry):
+        slot = step % 2
+        for lane in range(0, chunk, 128):
+            lanes = slice(lane, lane + 128)
+            wide = lanes_at(step * chunk + lane)
+            taps, short = half_taps(taps_ref, wide)
+            before = sum(taps[3 * a] * rim[slot, a : a + inner, lanes] for a in range(3))
+            after = sum(taps[3 * a + 2] * rim[slot, 16 + a : 16 + a + inner, lanes] for a in range(3))
+            total = jnp.zeros((8, 128), F32)
+
+            def line(r):
+                return up_ref[r, :, wide] if r < half else low[slot, r - half, :, lanes]
+
+            lines = [line(0), line(1), None]
+            for r in range(1, rows - 1):
+                lines[2] = line(r + 1)
+                act, part = conv_row(lines, short, before[r - 1 : r], after[r - 1 : r], place)
+                act_ref[r, :, wide] = act.astype(BF16)
+                total = total + part
+                lines = [lines[1], lines[2], None]
+            sums_ref[:, wide] = total
+        weight = expand_lower(jnp.minimum(step + 1, steps - 1), 1 - slot)
+        rim_of(normed, weight, rim, 1 - slot)
+        return carry
+
+    lax.fori_loop(0, steps, advance, 0)
+
+
+def conv_inner(image, upper, left, right, weight, taps, chunk=256):
+    rows, cols, channels = image.shape
+    half, _, width = upper.shape
+    here = pl.BlockSpec(memory_space=pltpu.VMEM)
+    args = [
+        pltpu.with_memory_space_constraint(a, pltpu.VMEM)
+        for a in (upper, left, right, weight, taps)
+    ]
     return pl.pallas_call(
-        inner_kernel,
-        grid=(steps,),
-        in_specs=[
-            tall,
-            whole(left),
-            whole(right),
-            pl.BlockSpec((channels, chunk), lambda c: (0, 0)),
-            pl.BlockSpec((channels, chunk), lambda c: (0, jnp.minimum(c + 1, steps - 1))),
-            pl.BlockSpec((9, chunk), lambda c: (0, c)),
+        functools.partial(inner_kernel, chunk=chunk),
+        in_specs=[pl.BlockSpec(memory_space=pl.ANY)] + [here] * len(args),
+        out_specs=[here] * 3,
+        out_shape=[
+            pltpu.VMEM((rows, cols, width), BF16),
+            pltpu.VMEM((8, width), F32),
+            pltpu.VMEM((2, cols, width), BF16),
         ],
-        out_specs=[tall, pl.BlockSpec((8, chunk), lambda c: (0, c))],
-        out_shape=[jax.ShapeDtypeStruct(hidden.shape, BF16), jax.ShapeDtypeStruct((8, width), F32)],
-        scratch_shapes=[pltpu.VMEM((32, channels), BF16), pltpu.VMEM((2, 32, chunk), F32)],
+        scratch_shapes=[
+            pltpu.VMEM((half, cols, channels), BF16),
+            pltpu.VMEM((half * cols, channels), BF16),
+            pltpu.VMEM((2, half, cols, chunk), BF16),
+            pltpu.VMEM((32, channels), BF16),
+            pltpu.VMEM((2, 32, chunk), F32),
+            pltpu.SemaphoreType.DMA,
+        ],
         compiler_params=params(16),
-        cost_estimate=pl.CostEstimate(flops=int(7e9), bytes_accessed=1 << 20, transcendentals=0),
+        cost_estimate=pl.CostEstimate(flops=int(8e9), bytes_accessed=1 << 20, transcendentals=0),
         name="conv_inner",
-    )(
-        pltpu.with_memory_space_constraint(hidden, pltpu.HBM), left, right, weight, weight, taps
-    )
+    )(pltpu.with_memory_space_constraint(image, pltpu.HBM), *args)
 
 
 def outer_kernel(
-    near_ref, over_ref, pair_ref, left_ref, right_ref, w_ref, taps_ref, red_ref, sums_ref,
+    near0_ref, near1_ref, over_ref, pair_ref, left_ref, right_ref, w_ref, taps_ref, red_ref, sums_ref,
     act_ref, part_ref, normed, rim, sums, *, chunk,
 ):
-    _, cols, width = near_ref.shape
+    _, cols, width = near0_ref.shape
     steps = width // chunk
     row, core = lax.axis_index("row_pair"), lax.axis_index("core")
     has_over = flag(row + core > 0) * flag(row - (1 - core) < lax.axis_size("row_pair") - 1)
@@ -285,7 +312,7 @@
                 return rim[slot, pl.ds(pl.multiple_of(at, 8), 64), lanes].astype(BF16)
 
             total = sums_ref[:, wide]
-            near = [near_ref[r, :, wide] for r in range(4)]
+            near = [ref[r, :, wide] for ref in (near0_ref, near1_ref) for r in range(2)]
             edges = (
                 ([line(top), near[0], near[1]], (top, 0), (160, 161)),
                 ([near[2], near[3], line(bottom)], (bottom, 2), (174, 175)),
@@ -313,7 +340,7 @@
 
 
 def conv_outer(near, over, pair, left, right, weight, taps, reduce, sums, copies, chunk=256):
-    _, cols, width = near.shape
+    _, cols, width = near[0].shape
     channels = weight.shape[0]
     outs = [((2, cols, width), BF16), ((copies, reduce.shape[0]), F32)]
     scratch = [
@@ -321,7 +348,7 @@
         pltpu.VMEM((2, 192, chunk), F32),
         pltpu.VMEM((8, width), F32),
     ]
-    args = (near, over, pair, left, right, weight, taps, reduce, sums)
+    args = (*near, over, pair, left, right, weight, taps, reduce, sums)
     kernel = functools.partial(outer_kernel, chunk=chunk)
     return resident(kernel, outs, args, scratch, 16, 2e9, "conv_outer")
 
@@ -648,11 +675,12 @@
 
     left = shift(image[:, cols - 1], COLS, 1)
     right = shift(image[:, 0], COLS, -1)
-    hidden, near, first, last = expand(image, mb_expand)
+    upper, near_top, first, last = expand_upper(image, mb_expand)
     over, pair = row_rims(first, last, left, right)
-    act, sums = conv_inner(hidden, left, right, mb_expand, mb_taps)
+    act, sums, near_end = conv_inner(image, upper, left, right, mb_expand, mb_taps)
     edges, part = conv_outer(
-        near, over, pair, left, right, mb_expand, mb_taps, mb_reduce.T, sums, lax.axis_size(ALL)
+        (near_top, near_end), over, pair, left, right, mb_expand, mb_taps, mb_reduce.T, sums,
+        lax.axis_size(ALL),
     )
     parts = sum_parts(part)
     mixed = block_part(

time: 134 us -> 132 us (0.985)
  blocking collectives: 68.2 us -> 70.6 us
  Pallas kernels: 43.7 us -> 41.5 us
    ppermute x4, starting transfers between devices: 12.2 us -> 9.68 us  [shift(): return lax.ppermute(x, axes, [(i, (i + by) % size) for i in range(size)])]
    ppermute x1, starting transfers between devices: 1.99 us -> 4.52 us  [shift_both(): return lax.ppermute(x, AXES, pairs)]
    all_to_all x2, blocking collectives: 31.7 us -> 34 us  [sum_parts(): arrived = lax.all_to_all(part, ALL, split_axis=0, concat_axis=0, tiled=True)]
    pallas_call x2, Pallas kernels: 13.5 us -> 11.4 us  [the longest x1 8.75 us: conv_inner(): pl.pallas_call(functools.partial(inner_kernel, chunk=chunk), in_specs=[pl...]
    ppermute x1, waiting for transfers between devices: 1.9 us -> 0.01 us  [shift_both(): return lax.ppermute(x, AXES, pairs)]
  transfers between devices with their start and end apart: 7 -> 7, of which waited for: 1 -> 1; matrix products, arithmetic and copies ran while one was open for 0% -> 0% of each run, Pallas kernels for 12% -> 11%
where the time goes in v6:
time: 132 us
  blocking collectives  70.6 us (53%)
  Pallas kernels  41.5 us (31%)
  starting transfers between devices  16.4 us (12%)
    all_to_all x2, blocking collectives, exchange(): lax.all_to_all(pieces, CLASS, split_axis=0, concat_axis=0, tiled=True)  36.5 us
    all_to_all x2, blocking collectives, sum_parts(): arrived = lax.all_to_all(part, ALL, split_axis=0, concat_axis=0, tiled=True)  34 us
    pallas_call x4, Pallas kernels, resident(): pl.pallas_call(kernel, in_specs=[here] * len(args), out_specs=[here] * le...  24.9 us
    ppermute x4, starting transfers between devices, shift(): return lax.ppermute(x, axes, [(i, (i + by) % size) for i in range(size)])  9.68 us
    pallas_call x1, Pallas kernels, conv_inner(): pl.pallas_call(functools.partial(inner_kernel, chunk=chunk), in_specs=[pl...  8.75 us
    ppermute x1, starting transfers between devices, shift_both(): return lax.ppermute(x, AXES, pairs)  4.52 us
    pallas_call x1, Pallas kernels, down_conv(): pl.pallas_call(functools.partial(down_conv_kernel, chunk=chunk), in_specs...  3.34 us
    pallas_call x1, Pallas kernels, expand_upper(): pl.pallas_call(kernel, in_specs=[away, away], out_specs=[here] * 4, out_s...  2.67 us
  transfers between devices with their start and end apart: 7, of which 1 were waited for; matrix products, arithmetic and copies ran while one was open for 0% of the time, Pallas kernels for 11%

profile of v6, /device:TPU:1, one launch (start us, length us, event | category | flops | bytes accessed | tf_op | source)
XLA Modules:
  0.0 132.2 jit_solution(8692961102397567031)
XLA Ops:
  0.6 1.0 fusion
  1.6 3.8 %collective-permute-start = (bf16[16,384]{1,0:T(8,128)(2,1)S(1)}, bf16[16,384]{1,0:T(8,128)(2,1)S(1)}, u32[]{:S(2)}, u32[]{:S(2)}) collective-permute-start(bf16[16,384]{1,0:T(8,128)(2,1)S(1)} %bitcast.40), channel_id=1, source_target_pairs={{0,1},{1,2},{2,3},{3,4},{4,5},{5,6},{6,7},{7,0},{8,9},{9,10},{10,1... | collective-permute-start | bytes 36872 | tf_op jit(solution)/shard_map/ppermute | solution.py:609
  5.5 3.6 %collective-permute-start.1 = (bf16[16,384]{1,0:T(8,128)(2,1)S(1)}, bf16[16,384]{1,0:T(8,128)(2,1)S(1)}, u32[]{:S(2)}, u32[]{:S(2)}) collective-permute-start(bf16[16,384]{1,0:T(8,128)(2,1)S(1)} %bitcast.41), channel_id=1, source_target_pairs={{0,7},{1,0},{2,1},{3,2},{4,3},{5,4},{6,5},{7,6},{8,15},{9,8},{10,9... | collective-permute-start | bytes 36872 | tf_op jit(solution)/shard_map/ppermute | solution.py:609
  9.0 2.7 %expand_upper.1 = (bf16[8,64,1536]{2,1,0:T(8,128)(2,1)S(1)}, bf16[2,64,1536]{2,1,0:T(8,128)(2,1)S(1)}, bf16[64,384]{1,0:T(8,128)(2,1)S(1)}, bf16[64,384]{1,0:T(8,128)(2,1)S(1)}) custom-call(bf16[16,64,384]{2,1,0:T(8,128)(2,1)} %img_ref.1, bf16[384,1536]{1,0:T(8,128)(2,1)} %w_ref.5), custom_call_target="tpu_custom_call" | custom-call | flops 2000000000 | bytes 1048576 | tf_op jit(solution)/shard_map/expand_upper/pallas_call | solution.py:127
  11.7 0.1 pad.7.clone
  11.8 0.0 collective-permute-done.left_ref
  11.8 0.0 collective-permute-done.1.right_ref
  11.8 0.1 broadcast_select_fusion
  12.0 1.0 collective-permute-start.3
  13.0 1.2 collective-permute-start.2
  14.2 0.0 copy-done.7
  14.2 0.0 copy-done.19
  14.2 8.7 %conv_inner.1 = (bf16[16,64,1536]{2,1,0:T(8,128)(2,1)S(1)}, f32[8,1536]{1,0:T(8,128)S(1)}, bf16[2,64,1536]{2,1,0:T(8,128)(2,1)S(1)}) custom-call(bf16[16,64,384]{2,1,0:T(8,128)(2,1)} %img_ref.1, bf16[8,64,1536]{2,1,0:T(8,128)(2,1)S(1)} %get-tuple-element.16.up_ref, bf16[16,384]{1,0:T(8,128)(2,1)S(1)} %collective-permute-done.left_ref, ...), custom_call_target="tpu_custom_call" | custom-call | flops 8000000000 | bytes 1048576 | tf_op jit(solution)/shard_map/conv_inner/pallas_call | solution.py:261
  22.9 0.0 collective-permute-done.3.pair_ref
  22.9 0.0 collective-permute-done.2.over_ref
  23.0 0.0 copy-done.15
  23.0 0.0 copy-start.6
  23.0 0.0 copy-start.8
  23.0 0.0 copy-start.9
  23.0 0.0 copy-start.10
  23.0 0.0 copy-start.13
  23.0 0.0 copy-start.16
  23.0 0.0 copy-start.17
  23.0 2.4 %conv_outer.1 = (bf16[2,64,1536]{2,1,0:T(8,128)(2,1)S(1)}, f32[128,96]{1,0:T(8,128)S(1)}) custom-call(bf16[2,64,1536]{2,1,0:T(8,128)(2,1)S(1)} %get-tuple-element.18.near0_ref, bf16[2,64,1536]{2,1,0:T(8,128)(2,1)S(1)} %get-tuple-element.19.near1_ref, bf16[80,384]{1,0:T(8,128)(2,1)S(1)} %collective-permute-done.2.over_ref, ...), custom_call_target="tpu_custom_call" | custom-call | flops 2000000000 | bytes 1048576 | tf_op jit(solution)/shard_map/conv_outer/pallas_call | solution.py:35
  25.4 18.4 %all_to_all.20 = f32[128,1,96]{2,1,0:T(1,128)S(1)} all-to-all(f32[128,1,96]{2,1,0:T(1,128)S(1)} %bitcast.35), channel_id=1, replica_groups=mesh['row_pair'=8,'core'=2,'depth'=4,'col_pair'=2] {'core','row_pair','c..., dimensions={0} | all-to-all | bytes 98304 | tf_op jit(solution)/shard_map/all_to_all | solution.py:633
  43.8 0.0 copy-done.6
  43.8 0.0 copy-done.8
  43.8 0.0 copy-done.9
  43.8 0.0 copy-done.10
  43.8 0.0 copy-done.13
  43.9 0.0 copy-done.16
  43.9 0.0 copy-done.17
  43.9 0.0 copy-start.12
  43.9 0.0 copy-start.14
  43.9 10.6 %block_part.1 = bf16[1024,384]{1,0:T(8,128)(2,1)S(1)} custom-call(bf16[16,64,384]{2,1,0:T(8,128)(2,1)S(1)} %copy-done.6, bf16[16,64,1536]{2,1,0:T(8,128)(2,1)S(1)} %get-tuple-element.17.act_ref, bf16[2,64,1536]{2,1,0:T(8,128)(2,1)S(1)} %get-tuple-element.23.edge_ref, f32[128,96]{1,0:T(8,128)S(1)} %bitcast.37, bf16[96,1536]{1,0:T(8,128)(2,1)S(1)} %copy-done.16, ...), custom_call_target="tpu_custom_call" | custom-call | flops 12000000000 | bytes 1048576 | tf_op jit(solution)/shard_map/block_part/pallas_call | solution.py:35
  54.5 0.0 copy-start.11
  54.5 0.0 copy-start.18
  54.5 18.0 %all_to_all.21 = bf16[64,16,384]{2,1,0:T(8,128)(2,1)S(1)} all-to-all(bf16[64,16,384]{2,1,0:T(8,128)(2,1)S(1)} %bitcast.30), channel_id=1, replica_groups=mesh['row_pair'=8,'core'=2,'depth'=4,'col_pair'=2] {'row_pair','col_pair..., dimensions={0} | all-to-all | bytes 1572864 | tf_op jit(solution)/shard_map/all_to_all | solution.py:626
  72.5 0.0 copy-done.12
  72.5 0.0 copy-done.14
  72.6 0.0 copy-done.11
  72.6 0.0 copy-done.18
  72.6 9.2 %grid_part.1 = bf16[1024,384]{1,0:T(8,128)(2,1)S(1)} custom-call(bf16[1024,384]{1,0:T(8,128)(2,1)S(1)} %bitcast.31, bf16[384,1152]{1,0:T(8,128)(2,1)S(1)} %copy-done.14, bf16[384,384]{1,0:T(8,128)(2,1)S(1)} %copy-done.18, bf16[384,1536]{1,0:T(8,128)(2,1)S(1)} %copy-done.11, bf16[1536,384]{1,0:T(8,128)(2,1)S(1)} %copy-done.12), custom_call_target="tpu_custom_call" | custom-call | flops 10000000000 | bytes 1048576 | tf_op jit(solution)/shard_map/grid_part/pallas_call | solution.py:35
  81.8 0.0 copy-start.1
  81.8 18.5 %all_to_all.22 = bf16[64,16,384]{2,1,0:T(8,128)(2,1)S(1)} all-to-all(bf16[64,16,384]{2,1,0:T(8,128)(2,1)S(1)} %bitcast.32), channel_id=1, replica_groups=mesh['row_pair'=8,'core'=2,'depth'=4,'col_pair'=2] {'row_pair','col_pair..., dimensions={0} | all-to-all | bytes 1572864 | tf_op jit(solution)/shard_map/all_to_all | solution.py:626
  100.4 4.5 %collective-permute-start.6 = (bf16[1,384]{1,0:T(2,128)(2,1)S(1)}, bf16[1,384]{1,0:T(2,128)(2,1)S(1)}, u32[]{:S(2)}, u32[]{:S(2)}) collective-permute-start(bf16[1,384]{1,0:T(2,128)(2,1)S(1)} %slice_bitcast_fusion), channel_id=1, source_target_pairs={{0,9},{1,10},{2,11},{3,12},{4,13},{5,14},{6,15},{7,8},{8,17},{9,18... | collective-permute-start | bytes 2312 | tf_op jit(solution)/shard_map/ppermute | solution.py:619
  104.9 2.0 %collective-permute-start.5 = (bf16[16,384]{1,0:T(8,128)(2,1)S(1)}, bf16[16,384]{1,0:T(8,128)(2,1)S(1)}, u32[]{:S(2)}, u32[]{:S(2)}) collective-permute-start(bf16[16,384]{1,0:T(8,128)(2,1)S(1)} %bitcast.42), channel_id=1, source_target_pairs={{0,1},{1,2},{2,3},{3,4},{4,5},{5,6},{6,7},{7,0},{8,9},{9,10},{10,1... | collective-permute-start | bytes 36872 | tf_op jit(solution)/shard_map/ppermute | solution.py:609
  106.9 0.0 copy-start.5
  106.9 0.3 collective-permute-start.4
  107.2 0.0 copy-done.1
  107.2 2.7 %down_expand.1 = (bf16[16,2,32,1536]{3,2,1,0:T(8,128)(2,1)S(1)}, bf16[8,32,384]{2,1,0:T(8,128)(2,1)S(1)}) custom-call(bf16[16,64,384]{2,1,0:T(8,128)(2,1)S(1)} %bitcast.28, bf16[384,1536]{1,0:T(8,128)(2,1)S(1)} %copy-done.1), custom_call_target="tpu_custom_call" | custom-call | flops 2415919104 | bytes 1048576 | tf_op jit(solution)/shard_map/down_expand/pallas_call | solution.py:35
  110.0 0.0 collective-permute-done.6.corner_ref
  110.0 1.2 collective-permute-done.5.left_ref
  111.2 0.0 collective-permute-done.4.upper_ref
  111.2 0.0 copy-done.3
  111.2 0.0 copy-done.5
  111.2 0.0 copy-start
  111.2 0.0 copy-start.2
  111.3 0.0 copy-start.4
  111.3 3.3 %down_conv.1 = (bf16[8,32,1536]{2,1,0:T(8,128)(2,1)S(1)}, f32[128,96]{1,0:T(8,128)S(1)}, bf16[16,64,384]{2,1,0:T(8,128)(2,1)}) custom-call(bf16[16,2,32,1536]{3,2,1,0:T(8,128)(2,1)S(1)} %get-tuple-element.25.hid_ref, bf16[16,64,384]{2,1,0:T(8,128)(2,1)S(1)} %bitcast.29, bf16[64,384]{1,0:T(8,128)(2,1)S(1)} %collective-permute-done.4.upper_ref, ...), custom_call_target="tpu_custom_call" | custom-call | tf_op jit(solution)/shard_map/down_conv/pallas_call | solution.py:559
  114.6 15.6 %all_to_all.23 = f32[128,1,96]{2,1,0:T(1,128)S(1)} all-to-all(f32[128,1,96]{2,1,0:T(1,128)S(1)} %bitcast.36), channel_id=1, replica_groups=mesh['row_pair'=8,'core'=2,'depth'=4,'col_pair'=2] {'core','row_pair','c..., dimensions={0} | all-to-all | bytes 98304 | tf_op jit(solution)/shard_map/all_to_all | solution.py:633
  130.3 0.0 copy-done
  130.3 0.0 copy-done.2
  130.3 1.9 %down_out.1 = bf16[8,32,768]{2,1,0:T(8,128)(2,1)} custom-call(bf16[8,32,1536]{2,1,0:T(8,128)(2,1)S(1)} %get-tuple-element.27.act_ref, bf16[8,32,384]{2,1,0:T(8,128)(2,1)S(1)} %get-tuple-element.28.pool_ref, f32[128,96]{1,0:T(8,128)S(1)} %bitcast.34, bf16[96,1536]{1,0:T(8,128)(2,1)S(1)} %copy-done.4, bf16[1536,768]{1,0:T(8,128)(2,1)S(1)} %copy-done, ...), custom_call_target="tpu_custom_call" | custom-call | tf_op jit(solution)/shard_map/down_out/pallas_call | solution.py:597
  (14 shorter events, 0.1 us)
Async XLA Ops:
  1.6 10.2 %collective-permute-start = (bf16[16,384]{1,0:T(8,128)(2,1)S(1)}, bf16[16,384]{1,0:T(8,128)(2,1)S(1)}, u32[]{:S(2)}, u32[]{:S(2)}) collective-permute-start(bf16[16,384]{1,0:T(8,128)(2,1)S(1)} %bitcast.40), channel_id=1, source_target_pairs={{0,1},{1,2},{2,3},{3,4},{4,5},{5,6},{6,7},{7,0},{8,9},{9,10},{10,1... | collective-permute-start | bytes 36872 | tf_op jit(solution)/shard_map/ppermute | solution.py:609
  5.4 8.7 %copy-start.7 = (bf16[384,1536]{1,0:T(8,128)(2,1)S(1)}, bf16[384,1536]{1,0:T(8,128)(2,1)}, u32[]{:S(2)}) copy-start(bf16[384,1536]{1,0:T(8,128)(2,1)} %w_ref.5) | copy-start | bytes 3538948
  5.5 8.7 %copy-start.19 = (bf16[9,1536]{1,0:T(8,128)(2,1)S(1)}, bf16[9,1536]{1,0:T(8,128)(2,1)}, u32[]{:S(2)}) copy-start(bf16[9,1536]{1,0:T(8,128)(2,1)} %taps_ref.4) | copy-start | bytes 82948
  5.5 6.4 %collective-permute-start.1 = (bf16[16,384]{1,0:T(8,128)(2,1)S(1)}, bf16[16,384]{1,0:T(8,128)(2,1)S(1)}, u32[]{:S(2)}, u32[]{:S(2)}) collective-permute-start(bf16[16,384]{1,0:T(8,128)(2,1)S(1)} %bitcast.41), channel_id=1, source_target_pairs={{0,7},{1,0},{2,1},{3,2},{4,3},{5,4},{6,5},{7,6},{8,15},{9,8},{10,9... | collective-permute-start | bytes 36872 | tf_op jit(solution)/shard_map/ppermute | solution.py:609
  12.0 11.0 %collective-permute-start.3 = (bf16[80,384]{1,0:T(8,128)(2,1)S(1)}, bf16[80,384]{1,0:T(8,128)(2,1)S(1)}, u32[]{:S(2)}, u32[]{:S(2)}) collective-permute-start(bf16[80,384]{1,0:T(8,128)(2,1)S(1)} %get-tuple-element.32), channel_id=1, source_target_pairs={{0,8},{8,0},{1,9},{9,1},{2,10},{10,2},{3,11},{11,3},{4,12},{12,4},... | collective-permute-start | bytes 184328 | tf_op jit(solution)/shard_map/ppermute | solution.py:647
  13.0 10.0 %collective-permute-start.2 = (bf16[80,384]{1,0:T(8,128)(2,1)S(1)}, bf16[80,384]{1,0:T(8,128)(2,1)S(1)}, u32[]{:S(2)}, u32[]{:S(2)}) collective-permute-start(bf16[80,384]{1,0:T(8,128)(2,1)S(1)} %get-tuple-element.33), channel_id=1, source_target_pairs={{0,120},{8,16},{16,8},{24,32},{32,24},{40,48},{48,40},{56,64},{64,... | collective-permute-start | bytes 184328 | tf_op jit(solution)/shard_map/ppermute | solution.py:646
  14.2 8.8 %copy-start.15 = (bf16[1536,96]{0,1:T(8,128)(2,1)S(1)}, bf16[1536,96]{0,1:T(8,128)(2,1)}, u32[]{:S(2)}) copy-start(bf16[1536,96]{0,1:T(8,128)(2,1)} %param.23) | copy-start | bytes 884740
  23.0 20.9 %copy-start.6 = (bf16[16,64,384]{2,1,0:T(8,128)(2,1)S(1)}, bf16[16,64,384]{2,1,0:T(8,128)(2,1)}, u32[]{:S(2)}) copy-start(bf16[16,64,384]{2,1,0:T(8,128)(2,1)} %img_ref.1) | copy-start | bytes 2359300
  23.0 20.9 %copy-start.8 = (bf16[1536,384]{1,0:T(8,128)(2,1)S(1)}, bf16[1536,384]{1,0:T(8,128)(2,1)}, u32[]{:S(2)}) copy-start(bf16[1536,384]{1,0:T(8,128)(2,1)} %project_ref.2) | copy-start | bytes 3538948
  23.0 20.8 %copy-start.9 = (bf16[384,1536]{1,0:T(8,128)(2,1)S(1)}, bf16[384,1536]{1,0:T(8,128)(2,1)}, u32[]{:S(2)}) copy-start(bf16[384,1536]{1,0:T(8,128)(2,1)} %up_ref.2) | copy-start | bytes 3538948
  23.0 20.8 %copy-start.10 = (bf16[1536,384]{1,0:T(8,128)(2,1)S(1)}, bf16[1536,384]{1,0:T(8,128)(2,1)}, u32[]{:S(2)}) copy-start(bf16[1536,384]{1,0:T(8,128)(2,1)} %down_ref.2) | copy-start | bytes 3538948
  23.0 20.8 %copy-start.13 = (bf16[384,1152]{1,0:T(8,128)(2,1)S(1)}, bf16[384,1152]{1,0:T(8,128)(2,1)}, u32[]{:S(2)}) copy-start(bf16[384,1152]{1,0:T(8,128)(2,1)} %qkv_ref.2) | copy-start | bytes 2654212
  23.0 20.8 %copy-start.16 = (bf16[96,1536]{1,0:T(8,128)(2,1)S(1)}, bf16[96,1536]{1,0:T(8,128)(2,1)}, u32[]{:S(2)}) copy-start(bf16[96,1536]{1,0:T(8,128)(2,1)} %restore_ref.2) | copy-start | bytes 884740
  23.0 20.8 %copy-start.17 = (bf16[384,384]{1,0:T(8,128)(2,1)S(1)}, bf16[384,384]{1,0:T(8,128)(2,1)}, u32[]{:S(2)}) copy-start(bf16[384,384]{1,0:T(8,128)(2,1)} %out_ref.2) | copy-start | bytes 884740
  43.9 28.7 %copy-start.12 = (bf16[1536,384]{1,0:T(8,128)(2,1)S(1)}, bf16[1536,384]{1,0:T(8,128)(2,1)}, u32[]{:S(2)}) copy-start(bf16[1536,384]{1,0:T(8,128)(2,1)} %down_ref.3) | copy-start | bytes 3538948
  43.9 28.7 %copy-start.14 = (bf16[384,1152]{1,0:T(8,128)(2,1)S(1)}, bf16[384,1152]{1,0:T(8,128)(2,1)}, u32[]{:S(2)}) copy-start(bf16[384,1152]{1,0:T(8,128)(2,1)} %qkv_ref.3) | copy-start | bytes 2654212
  54.5 18.1 %copy-start.11 = (bf16[384,1536]{1,0:T(8,128)(2,1)S(1)}, bf16[384,1536]{1,0:T(8,128)(2,1)}, u32[]{:S(2)}) copy-start(bf16[384,1536]{1,0:T(8,128)(2,1)} %up_ref.3) | copy-start | bytes 3538948
  54.5 18.0 %copy-start.18 = (bf16[384,384]{1,0:T(8,128)(2,1)S(1)}, bf16[384,384]{1,0:T(8,128)(2,1)}, u32[]{:S(2)}) copy-start(bf16[384,384]{1,0:T(8,128)(2,1)} %out_ref.3) | copy-start | bytes 884740
  81.8 25.4 %copy-start.1 = (bf16[384,1536]{1,0:T(8,128)(2,1)S(1)}, bf16[384,1536]{1,0:T(8,128)(2,1)}, u32[]{:S(2)}) copy-start(bf16[384,1536]{1,0:T(8,128)(2,1)} %w_ref.7) | copy-start | bytes 3538948
  100.4 9.6 %collective-permute-start.6 = (bf16[1,384]{1,0:T(2,128)(2,1)S(1)}, bf16[1,384]{1,0:T(2,128)(2,1)S(1)}, u32[]{:S(2)}, u32[]{:S(2)}) collective-permute-start(bf16[1,384]{1,0:T(2,128)(2,1)S(1)} %slice_bitcast_fusion), channel_id=1, source_target_pairs={{0,9},{1,10},{2,11},{3,12},{4,13},{5,14},{6,15},{7,8},{8,17},{9,18... | collective-permute-start | bytes 2312 | tf_op jit(solution)/shard_map/ppermute | solution.py:619
  104.9 6.3 %collective-permute-start.5 = (bf16[16,384]{1,0:T(8,128)(2,1)S(1)}, bf16[16,384]{1,0:T(8,128)(2,1)S(1)}, u32[]{:S(2)}, u32[]{:S(2)}) collective-permute-start(bf16[16,384]{1,0:T(8,128)(2,1)S(1)} %bitcast.42), channel_id=1, source_target_pairs={{0,1},{1,2},{2,3},{3,4},{4,5},{5,6},{6,7},{7,0},{8,9},{9,10},{10,1... | collective-permute-start | bytes 36872 | tf_op jit(solution)/shard_map/ppermute | solution.py:609
  106.9 4.4 %copy-start.3 = (bf16[1536,96]{0,1:T(8,128)(2,1)S(1)}, bf16[1536,96]{0,1:T(8,128)(2,1)}, u32[]{:S(2)}) copy-start(bf16[1536,96]{0,1:T(8,128)(2,1)} %param.36) | copy-start | bytes 884740
  106.9 4.3 %copy-start.5 = (bf16[9,1536]{1,0:T(8,128)(2,1)S(1)}, bf16[9,1536]{1,0:T(8,128)(2,1)}, u32[]{:S(2)}) copy-start(bf16[9,1536]{1,0:T(8,128)(2,1)} %taps_ref.5) | copy-start | bytes 82948
  106.9 4.3 %collective-permute-start.4 = (bf16[64,384]{1,0:T(8,128)(2,1)S(1)}, bf16[64,384]{1,0:T(8,128)(2,1)S(1)}, u32[]{:S(2)}, u32[]{:S(2)}) collective-permute-start(bf16[64,384]{1,0:T(8,128)(2,1)S(1)} %bitcast.39), channel_id=1, source_target_pairs={{0,8},{8,16},{16,24},{24,32},{32,40},{40,48},{48,56},{56,64},{64,7... | collective-permute-start | bytes 147464 | tf_op jit(solution)/shard_map/ppermute | solution.py:609
  111.2 19.0 %copy-start = (bf16[1536,768]{1,0:T(8,128)(2,1)S(1)}, bf16[1536,768]{1,0:T(8,128)(2,1)}, u32[]{:S(2)}) copy-start(bf16[1536,768]{1,0:T(8,128)(2,1)} %project_ref.3) | copy-start | bytes 7077892
  111.2 19.0 %copy-start.2 = (bf16[384,768]{1,0:T(8,128)(2,1)S(1)}, bf16[384,768]{1,0:T(8,128)(2,1)}, u32[]{:S(2)}) copy-start(bf16[384,768]{1,0:T(8,128)(2,1)} %short_ref.1) | copy-start | bytes 1769476
  111.3 19.0 %copy-start.4 = (bf16[96,1536]{1,0:T(8,128)(2,1)S(1)}, bf16[96,1536]{1,0:T(8,128)(2,1)}, u32[]{:S(2)}) copy-start(bf16[96,1536]{1,0:T(8,128)(2,1)} %restore_ref.3) | copy-start | bytes 884740

commit v7 on v6

--- a/solution.py
+++ b/solution.py
@@ -98,47 +98,64 @@
     )
 
 
-def expand_upper(image, weight):
+def expand_upper(image, weight, chunk=256):
     rows, cols, channels = image.shape
     half, hidden = rows // 2, weight.shape[1]
 
     def kernel(
-        x_hbm, w_hbm, up_ref, near_ref, first_ref, last_ref, x_ref, w_ref, x_sem, w_sem, last_sem
+        x_hbm, w_hbm, up_ref, near_ref, first_ref, last_ref, normed_ref, start_ref,
+        x_ref, w_ref, x_sems, w_sem,
     ):
-        x_copy = pltpu.make_async_copy(x_hbm.at[0:half], x_ref, x_sem)
+        parts = [slice(0, half), slice(half, rows)]
+        x_copies = [
+            pltpu.make_async_copy(x_hbm.at[part], x_ref.at[part], x_sems.at[i])
+            for i, part in enumerate(parts)
+        ]
         w_copy = pltpu.make_async_copy(w_hbm, w_ref, w_sem)
-        last_copy = pltpu.make_async_copy(x_hbm.at[rows - 1], last_ref, last_sem)
-        x_copy.start()
+        x_copies[0].start()
         w_copy.start()
-        last_copy.start()
-        x_copy.wait()
+        x_copies[1].start()
+
+        def norm(part):
+            x = x_ref[part].reshape(half * cols, channels).astype(F32)
+            return half_norm(x).astype(BF16)
+
+        def wide(normed, c):
+            hidden = gelu_twice(dot(normed, w_ref[:, c : c + chunk])).astype(BF16)
+            return hidden.reshape(half, cols, chunk)
+
+        x_copies[0].wait()
         first_ref[...] = x_ref[0]
-        normed = half_norm(x_ref[...].reshape(half * cols, channels).astype(F32)).astype(BF16)
+        normed = norm(parts[0])
         w_copy.wait()
-        for c in range(0, hidden, 256):
-            wide = gelu_twice(dot(normed, w_ref[:, c : c + 256])).astype(BF16)
-            wide = wide.reshape(half, cols, 256)
-            up_ref[:, :, c : c + 256] = wide
-            near_ref[:, :, c : c + 256] = wide[0:2]
-        last_copy.wait()
+        for c in range(0, hidden, chunk):
+            upper = wide(normed, c)
+            up_ref[:, :, c : c + chunk] = upper
+            near_ref[:, :, c : c + chunk] = upper[0:2]
+        x_copies[1].wait()
+        last_ref[...] = x_ref[rows - 1]
+        normed = norm(parts[1])
+        normed_ref[...] = normed
+        start_ref[...] = wide(normed, 0)
 
     away = pl.BlockSpec(memory_space=pl.ANY)
     here = pl.BlockSpec(memory_space=pltpu.VMEM)
     return pl.pallas_call(
         kernel,
         in_specs=[away, away],
-        out_specs=[here] * 4,
+        out_specs=[here] * 6,
         out_shape=[
             pltpu.VMEM((half, cols, hidden), BF16),
             pltpu.VMEM((2, cols, hidden), BF16),
             pltpu.VMEM((cols, channels), BF16),
             pltpu.VMEM((cols, channels), BF16),
+            pltpu.VMEM((half * cols, channels), BF16),
+            pltpu.VMEM((half, cols, chunk), BF16),
         ],
         scratch_shapes=[
-            pltpu.VMEM((half, cols, channels), BF16),
+            pltpu.VMEM(image.shape, BF16),
             pltpu.VMEM(weight.shape, BF16),
-            pltpu.SemaphoreType.DMA,
-            pltpu.SemaphoreType.DMA,
+            pltpu.SemaphoreType.DMA((2,)),
             pltpu.SemaphoreType.DMA,
         ],
         compiler_params=params(16),
@@ -197,28 +214,24 @@
 
 
 def inner_kernel(
-    x_hbm, up_ref, left_ref, right_ref, w_ref, taps_ref, act_ref, sums_ref, near_ref,
-    x_ref, x_normed, low, normed, rim, x_sem, *, chunk,
+    up_ref, x_ref, start_ref, left_ref, right_ref, w_ref, taps_ref, act_ref, sums_ref, near_ref,
+    low, normed, rim, *, chunk,
 ):
     rows, cols, width = act_ref.shape
     half = rows // 2
     steps = width // chunk
-    copy = pltpu.make_async_copy(x_hbm.at[half:rows], x_ref, x_sem)
-    copy.start()
     side_norms(normed, 0, left_ref, right_ref)
     rim_of(normed, w_ref[:, :chunk], rim, 0)
-    copy.wait()
-    x = x_ref[...].reshape(half * cols, x_ref.shape[2]).astype(F32)
-    x_normed[...] = half_norm(x).astype(BF16)
+    low[0] = start_ref[...]
+    near_ref[:, :, :chunk] = start_ref[half - 2 : half]
 
     def expand_lower(step, slot):
         weight = w_ref[:, lanes_at(step * chunk, chunk)]
-        wide = gelu_twice(dot(x_normed[...], weight)).astype(BF16).reshape(half, cols, chunk)
+        wide = gelu_twice(dot(x_ref[...], weight)).astype(BF16).reshape(half, cols, chunk)
         low[slot] = wide
         near_ref[:, :, lanes_at(step * chunk, chunk)] = wide[half - 2 :]
         return weight
 
-    expand_lower(0, 0)
     place = lax.broadcasted_iota(jnp.int32, (8, 128), 0)
     inner = rows - 2
 
@@ -250,35 +263,18 @@
     lax.fori_loop(0, steps, advance, 0)
 
 
-def conv_inner(image, upper, left, right, weight, taps, chunk=256):
-    rows, cols, channels = image.shape
-    half, _, width = upper.shape
-    here = pl.BlockSpec(memory_space=pltpu.VMEM)
-    args = [
-        pltpu.with_memory_space_constraint(a, pltpu.VMEM)
-        for a in (upper, left, right, weight, taps)
+def conv_inner(upper, normed, start, left, right, weight, taps):
+    half, cols, width = upper.shape
+    channels, chunk = weight.shape[0], start.shape[2]
+    outs = [((2 * half, cols, width), BF16), ((8, width), F32), ((2, cols, width), BF16)]
+    scratch = [
+        pltpu.VMEM((2, half, cols, chunk), BF16),
+        pltpu.VMEM((32, channels), BF16),
+        pltpu.VMEM((2, 32, chunk), F32),
     ]
-    return pl.pallas_call(
-        functools.partial(inner_kernel, chunk=chunk),
-        in_specs=[pl.BlockSpec(memory_space=pl.ANY)] + [here] * len(args),
-        out_specs=[here] * 3,
-        out_shape=[
-            pltpu.VMEM((rows, cols, width), BF16),
-            pltpu.VMEM((8, width), F32),
-            pltpu.VMEM((2, cols, width), BF16),
-        ],
-        scratch_shapes=[
-            pltpu.VMEM((half, cols, channels), BF16),
-            pltpu.VMEM((half * cols, channels), BF16),
-            pltpu.VMEM((2, half, cols, chunk), BF16),
-            pltpu.VMEM((32, channels), BF16),
-            pltpu.VMEM((2, 32, chunk), F32),
-            pltpu.SemaphoreType.DMA,
-        ],
-        compiler_params=params(16),
-        cost_estimate=pl.CostEstimate(flops=int(8e9), bytes_accessed=1 << 20, transcendentals=0),
-        name="conv_inner",
-    )(pltpu.with_memory_space_constraint(image, pltpu.HBM), *args)
+    args = (upper, normed, start, left, right, weight, taps)
+    kernel = functools.partial(inner_kernel, chunk=chunk)
+    return resident(kernel, outs, args, scratch, 16, 8e9, "conv_inner")
 
 
 def outer_kernel(
@@ -339,7 +335,7 @@
     squeeze_sums(sums, red_ref, part_ref)
 
 
-def conv_outer(near, over, pair, left, right, weight, taps, reduce, sums, copies, chunk=256):
+def conv_outer(near, over, pair, left, right, weight, taps, reduce, sums, copies, chunk=768):
     _, cols, width = near[0].shape
     channels = weight.shape[0]
     outs = [((2, cols, width), BF16), ((copies, reduce.shape[0]), F32)]
@@ -551,7 +547,7 @@
     copy.wait()
 
 
-def down_conv(hidden, section, upper, left, corner, weight, taps, reduce, copies, chunk=256):
+def down_conv(hidden, section, upper, left, corner, weight, taps, reduce, copies, chunk=768):
     rows, _, cols, width = hidden.shape
     channels = weight.shape[0]
     here = pl.BlockSpec(memory_space=pltpu.VMEM)
@@ -634,14 +630,28 @@
     return arrived.reshape(count, squeezed)
 
 
+def rims_kernel(first_ref, last_ref, left_ref, right_ref, away_ref, near_ref):
+    cols = first_ref.shape[0]
+    even = (lax.axis_index("core") == 0).astype(jnp.int32)
+    cell = lax.broadcasted_iota(jnp.int32, (16, 1), 0)
+    left, right = left_ref[...].astype(F32), right_ref[...].astype(F32)
+
+    def corners(r):
+        tail = jnp.where(cell == 1, right[r : r + 1], 0.0)
+        return jnp.where(cell == 0, left[r : r + 1], tail)
+
+    first = jnp.concatenate([first_ref[...].astype(F32), corners(0)], 0)
+    last = jnp.concatenate([last_ref[...].astype(F32), corners(15)], 0)
+    turned = jnp.zeros((cols + 16, 1), jnp.int32) + even
+    away_ref[...] = jnp.where(turned == 1, first, last).astype(BF16)
+    near_ref[...] = jnp.where(turned == 1, last, first).astype(BF16)
+
+
 def row_rims(first, last, left, right):
     size = lax.axis_size(ROWS)
-    pad = jnp.zeros((14, first.shape[1]), first.dtype)
-    first = jnp.concatenate([first, left[:1], right[:1], pad], 0)
-    last = jnp.concatenate([last, left[-1:], right[-1:], pad], 0)
-    even = lax.axis_index("core") == 0
-    away = jnp.where(even, first, last)
-    near = jnp.where(even, last, first)
+    cols, channels = first.shape
+    outs = [((cols + 16, channels), BF16)] * 2
+    away, near = resident(rims_kernel, outs, (first, last, left, right), [], 4, 1e6, "rims")
     pairs = [(r, (r - 1 if r % 2 == 0 else r + 1) % size) for r in range(size)]
     over = lax.ppermute(away, ROWS, pairs)
     pair = lax.ppermute(near, "core", [(0, 1), (1, 0)])
@@ -675,9 +685,9 @@
 
     left = shift(image[:, cols - 1], COLS, 1)
     right = shift(image[:, 0], COLS, -1)
-    upper, near_top, first, last = expand_upper(image, mb_expand)
+    upper, near_top, first, last, normed, start = expand_upper(image, mb_expand)
     over, pair = row_rims(first, last, left, right)
-    act, sums, near_end = conv_inner(image, upper, left, right, mb_expand, mb_taps)
+    act, sums, near_end = conv_inner(upper, normed, start, left, right, mb_expand, mb_taps)
     edges, part = conv_outer(
         (near_top, near_end), over, pair, left, right, mb_expand, mb_taps, mb_reduce.T, sums,
         lax.axis_size(ALL),

time: 132 us -> 132 us (level)
    pallas_call x2 -> x1, Pallas kernels: 11.4 us -> 3.21 us  [expand_upper(): pl.pallas_call(kernel, in_specs=[away, away], out_specs=[here] * 6, out_s...]
    pallas_call x4 -> x6, Pallas kernels: 24.9 us -> 32.3 us  [resident(): pl.pallas_call(kernel, in_specs=[here] * len(args), out_specs=[here] * le...]
    ppermute x4, starting transfers between devices: 9.68 us -> 12.3 us  [shift(): return lax.ppermute(x, axes, [(i, (i + by) % size) for i in range(size)])]
    ppermute x1, starting transfers between devices: 4.52 us -> 1.99 us  [shift_both(): return lax.ppermute(x, AXES, pairs)]
    ppermute x1, waiting for transfers between devices: 0.01 us -> 1.9 us  [shift_both(): return lax.ppermute(x, AXES, pairs)]
  transfers between devices with their start and end apart: 7 -> 7, of which waited for: 1 -> 1; matrix products, arithmetic and copies ran while one was open for 0% -> 0% of each run, Pallas kernels for 11% -> 10%
where the time goes in v7:
time: 132 us; the launch traced here: 131 us
  blocking collectives  69.5 us (53%)
  Pallas kernels  40.5 us (31%)
  starting transfers between devices  17.3 us (13%)
  waiting for transfers between devices  1.92 us (1%)
    all_to_all x2, blocking collectives, exchange(): lax.all_to_all(pieces, CLASS, split_axis=0, concat_axis=0, tiled=True)  36.6 us
    all_to_all x2, blocking collectives, sum_parts(): arrived = lax.all_to_all(part, ALL, split_axis=0, concat_axis=0, tiled=True)  33 us
    pallas_call x6, Pallas kernels, resident(): pl.pallas_call(kernel, in_specs=[here] * len(args), out_specs=[here] * le...  32.3 us
    ppermute x4, starting transfers between devices, shift(): return lax.ppermute(x, axes, [(i, (i + by) % size) for i in range(size)])  12.3 us
    pallas_call x1, Pallas kernels, expand_upper(): pl.pallas_call(kernel, in_specs=[away, away], out_specs=[here] * 6, out_s...  3.21 us
    pallas_call x1, Pallas kernels, down_conv(): pl.pallas_call(functools.partial(down_conv_kernel, chunk=chunk), in_specs...  3.08 us
  transfers between devices with their start and end apart: 7, of which 1 were waited for; matrix products, arithmetic and copies ran while one was open for 0% of the time, Pallas kernels for 10%

profile of v7, /device:TPU:1, one launch (start us, length us, event | category | flops | bytes accessed | tf_op | source)
XLA Modules:
  0.0 131.3 jit_solution(13752194518642497923)
XLA Ops:
  0.6 1.0 fusion
  1.6 3.8 %collective-permute-start = (bf16[16,384]{1,0:T(8,128)(2,1)S(1)}, bf16[16,384]{1,0:T(8,128)(2,1)S(1)}, u32[]{:S(2)}, u32[]{:S(2)}) collective-permute-start(bf16[16,384]{1,0:T(8,128)(2,1)S(1)} %bitcast.40), channel_id=1, source_target_pairs={{0,1},{1,2},{2,3},{3,4},{4,5},{5,6},{6,7},{7,0},{8,9},{9,10},{10,1... | collective-permute-start | bytes 36872 | tf_op jit(solution)/shard_map/ppermute | solution.py:605
  5.4 0.0 copy-start.7
  5.5 0.0 copy-start.19
  5.5 3.6 %collective-permute-start.1 = (bf16[16,384]{1,0:T(8,128)(2,1)S(1)}, bf16[16,384]{1,0:T(8,128)(2,1)S(1)}, u32[]{:S(2)}, u32[]{:S(2)}) collective-permute-start(bf16[16,384]{1,0:T(8,128)(2,1)S(1)} %bitcast.41), channel_id=1, source_target_pairs={{0,7},{1,0},{2,1},{3,2},{4,3},{5,4},{6,5},{7,6},{8,15},{9,8},{10,9... | collective-permute-start | bytes 36872 | tf_op jit(solution)/shard_map/ppermute | solution.py:605
  9.0 3.2 %expand_upper.1 = (bf16[8,64,1536]{2,1,0:T(8,128)(2,1)S(1)}, bf16[2,64,1536]{2,1,0:T(8,128)(2,1)S(1)}, bf16[64,384]{1,0:T(8,128)(2,1)S(1)}, bf16[64,384]{1,0:T(8...) custom-call(bf16[16,64,384]{2,1,0:T(8,128)(2,1)} %img_ref.1, bf16[384,1536]{1,0:T(8,128)(2,1)} %w_ref.5), custom_call_target="tpu_custom_call" | custom-call | flops 2000000000 | bytes 1048576 | tf_op jit(solution)/shard_map/expand_upper/pallas_call | solution.py:143
  12.3 0.0 collective-permute-done.left_ref
  12.3 0.0 collective-permute-done.1.right_ref
  12.3 2.1 %collective-permute-start.2 = (bf16[80,384]{1,0:T(8,128)(2,1)S(1)}, bf16[80,384]{1,0:T(8,128)(2,1)S(1)}, u32[]{:S(2)}, u32[]{:S(2)}) collective-permute-start(bf16[80,384]{1,0:T(8,128)(2,1)S(1)} %get-tuple-element.28), channel_id=1, source_target_pairs={{0,120},{8,16},{16,8},{24,32},{32,24},{40,48},{48,40},{56,64},{64,... | collective-permute-start | bytes 184328 | tf_op jit(solution)/shard_map/ppermute | solution.py:656
  14.4 0.9 collective-permute-start.3
  15.4 0.0 copy-done.7
  15.4 0.0 copy-done.19
  15.4 7.4 %conv_inner.1 = (bf16[16,64,1536]{2,1,0:T(8,128)(2,1)S(1)}, f32[8,1536]{1,0:T(8,128)S(1)}, bf16[2,64,1536]{2,1,0:T(8,128)(2,1)S(1)}) custom-call(bf16[8,64,1536]{2,1,0:T(8,128)(2,1)S(1)} %get-tuple-element.20.up_ref, bf16[512,384]{1,0:T(8,128)(2,1)S(1)} %get-tuple-element.21.x_ref, bf16[8,64,256]{2,1,0:T(8,128)(2,1)S(1)} %get-tuple-element.22.start_ref, ...), custom_call_target="tpu_custom_call" | custom-call | flops 8000000000 | bytes 1048576 | tf_op jit(solution)/shard_map/conv_inner/pallas_call | solution.py:35
  22.8 0.0 collective-permute-done.2.over_ref
  22.8 0.0 collective-permute-done.3.pair_ref
  22.8 0.0 copy-done.15
  22.8 0.0 copy-start.6
  22.9 0.0 copy-start.8
  22.9 0.0 copy-start.9
  22.9 0.0 copy-start.10
  22.9 0.0 copy-start.13
  22.9 0.0 copy-start.16
  22.9 0.0 copy-start.17
  22.9 2.3 %conv_outer.1 = (bf16[2,64,1536]{2,1,0:T(8,128)(2,1)S(1)}, f32[128,96]{1,0:T(8,128)S(1)}) custom-call(bf16[2,64,1536]{2,1,0:T(8,128)(2,1)S(1)} %get-tuple-element.24.near0_ref, bf16[2,64,1536]{2,1,0:T(8,128)(2,1)S(1)} %get-tuple-element.25.near1_ref, bf16[80,384]{1,0:T(8,128)(2,1)S(1)} %collective-permute-done.2.over_ref, ...), custom_call_target="tpu_custom_call" | custom-call | flops 2000000000 | bytes 1048576 | tf_op jit(solution)/shard_map/conv_outer/pallas_call | solution.py:35
  25.3 17.1 %all_to_all.20 = f32[128,1,96]{2,1,0:T(1,128)S(1)} all-to-all(f32[128,1,96]{2,1,0:T(1,128)S(1)} %bitcast.35), channel_id=1, replica_groups=mesh['row_pair'=8,'core'=2,'depth'=4,'col_pair'=2] {'core','row_pair','c..., dimensions={0} | all-to-all | bytes 98304 | tf_op jit(solution)/shard_map/all_to_all | solution.py:629
  42.4 0.0 copy-done.6
  42.4 0.0 copy-done.8
  42.4 0.0 copy-done.9
  42.4 0.0 copy-done.10
  42.4 0.0 copy-done.13
  42.4 0.0 copy-done.16
  42.4 0.0 copy-done.17
  42.4 0.0 copy-start.12
  42.4 0.0 copy-start.14
  42.4 10.6 %block_part.1 = bf16[1024,384]{1,0:T(8,128)(2,1)S(1)} custom-call(bf16[16,64,384]{2,1,0:T(8,128)(2,1)S(1)} %copy-done.6, bf16[16,64,1536]{2,1,0:T(8,128)(2,1)S(1)} %get-tuple-element.23.act_ref, bf16[2,64,1536]{2,1,0:T(8,128)(2,1)S(1)} %get-tuple-element.31.edge_ref, f32[128,96]{1,0:T(8,128)S(1)} %bitcast.37, bf16[96,1536]{1,0:T(8,128)(2,1)S(1)} %copy-done.16, ...), custom_call_target="tpu_custom_call" | custom-call | flops 12000000000 | bytes 1048576 | tf_op jit(solution)/shard_map/block_part/pallas_call | solution.py:35
  53.0 0.0 copy-start.11
  53.0 0.0 copy-start.18
  53.0 18.0 %all_to_all.21 = bf16[64,16,384]{2,1,0:T(8,128)(2,1)S(1)} all-to-all(bf16[64,16,384]{2,1,0:T(8,128)(2,1)S(1)} %bitcast.30), channel_id=1, replica_groups=mesh['row_pair'=8,'core'=2,'depth'=4,'col_pair'=2] {'row_pair','col_pair..., dimensions={0} | all-to-all | bytes 1572864 | tf_op jit(solution)/shard_map/all_to_all | solution.py:622
  71.1 0.0 copy-done.12
  71.1 0.0 copy-done.14
  71.1 0.0 copy-done.11
  71.1 0.0 copy-done.18
  71.1 9.2 %grid_part.1 = bf16[1024,384]{1,0:T(8,128)(2,1)S(1)} custom-call(bf16[1024,384]{1,0:T(8,128)(2,1)S(1)} %bitcast.31, bf16[384,1152]{1,0:T(8,128)(2,1)S(1)} %copy-done.14, bf16[384,384]{1,0:T(8,128)(2,1)S(1)} %copy-done.18, bf16[384,1536]{1,0:T(8,128)(2,1)S(1)} %copy-done.11, bf16[1536,384]{1,0:T(8,128)(2,1)S(1)} %copy-done.12), custom_call_target="tpu_custom_call" | custom-call | flops 10000000000 | bytes 1048576 | tf_op jit(solution)/shard_map/grid_part/pallas_call | solution.py:35
  80.3 0.0 copy-start.1
  80.4 18.5 %all_to_all.22 = bf16[64,16,384]{2,1,0:T(8,128)(2,1)S(1)} all-to-all(bf16[64,16,384]{2,1,0:T(8,128)(2,1)S(1)} %bitcast.32), channel_id=1, replica_groups=mesh['row_pair'=8,'core'=2,'depth'=4,'col_pair'=2] {'row_pair','col_pair..., dimensions={0} | all-to-all | bytes 1572864 | tf_op jit(solution)/shard_map/all_to_all | solution.py:622
  98.9 3.6 %collective-permute-start.4 = (bf16[64,384]{1,0:T(8,128)(2,1)S(1)}, bf16[64,384]{1,0:T(8,128)(2,1)S(1)}, u32[]{:S(2)}, u32[]{:S(2)}) collective-permute-start(bf16[64,384]{1,0:T(8,128)(2,1)S(1)} %bitcast.39), channel_id=1, source_target_pairs={{0,8},{8,16},{16,24},{24,32},{32,40},{40,48},{48,56},{56,64},{64,7... | collective-permute-start | bytes 147464 | tf_op jit(solution)/shard_map/ppermute | solution.py:605
  102.6 1.2 collective-permute-start.5
  103.8 2.0 %collective-permute-start.6 = (bf16[1,384]{1,0:T(2,128)(2,1)S(1)}, bf16[1,384]{1,0:T(2,128)(2,1)S(1)}, u32[]{:S(2)}, u32[]{:S(2)}) collective-permute-start(bf16[1,384]{1,0:T(2,128)(2,1)S(1)} %slice_bitcast_fusion), channel_id=1, source_target_pairs={{0,9},{1,10},{2,11},{3,12},{4,13},{5,14},{6,15},{7,8},{8,17},{9,18... | collective-permute-start | bytes 2312 | tf_op jit(solution)/shard_map/ppermute | solution.py:615
  105.8 0.0 copy-done.1
  105.8 2.7 %down_expand.1 = (bf16[16,2,32,1536]{3,2,1,0:T(8,128)(2,1)S(1)}, bf16[8,32,384]{2,1,0:T(8,128)(2,1)S(1)}) custom-call(bf16[16,64,384]{2,1,0:T(8,128)(2,1)S(1)} %bitcast.28, bf16[384,1536]{1,0:T(8,128)(2,1)S(1)} %copy-done.1), custom_call_target="tpu_custom_call" | custom-call | flops 2415919104 | bytes 1048576 | tf_op jit(solution)/shard_map/down_expand/pallas_call | solution.py:35
  108.5 1.9 %collective-permute-done.6.corner_ref = bf16[1,384]{1,0:T(2,128)(2,1)S(1)} collective-permute-done((bf16[1,384]{1,0:T(2,128)(2,1)S(1)}, bf16[1,384]{1,0:T(2,128)(2,1)S(1)}, u32[]{:S(2)}, u32[]{:S(2)}) %collective-permute-start.6) | collective-permute-done | bytes 800 | tf_op jit(solution)/shard_map/ppermute | solution.py:615
  110.5 0.0 collective-permute-done.5.left_ref
  110.5 0.0 collective-permute-done.4.upper_ref
  110.5 0.0 copy-done.3
  110.5 0.0 copy-done.5
  110.5 0.0 copy-start
  110.5 0.0 copy-start.2
  110.5 0.0 copy-start.4
  110.5 3.1 %down_conv.1 = (bf16[8,32,1536]{2,1,0:T(8,128)(2,1)S(1)}, f32[128,96]{1,0:T(8,128)S(1)}, bf16[16,64,384]{2,1,0:T(8,128)(2,1)}) custom-call(bf16[16,2,32,1536]{3,2,1,0:T(8,128)(2,1)S(1)} %get-tuple-element.33.hid_ref, bf16[16,64,384]{2,1,0:T(8,128)(2,1)S(1)} %bitcast.29, bf16[64,384]{1,0:T(8,128)(2,1)S(1)} %collective-permute-done.4.upper_ref, ...), custom_call_target="tpu_custom_call" | custom-call | tf_op jit(solution)/shard_map/down_conv/pallas_call | solution.py:555
  113.6 15.9 %all_to_all.23 = f32[128,1,96]{2,1,0:T(1,128)S(1)} all-to-all(f32[128,1,96]{2,1,0:T(1,128)S(1)} %bitcast.36), channel_id=1, replica_groups=mesh['row_pair'=8,'core'=2,'depth'=4,'col_pair'=2] {'core','row_pair','c..., dimensions={0} | all-to-all | bytes 98304 | tf_op jit(solution)/shard_map/all_to_all | solution.py:629
  129.5 0.0 copy-done
  129.5 0.0 copy-done.2
  129.5 0.0 copy-done.4
  129.5 1.9 %down_out.1 = bf16[8,32,768]{2,1,0:T(8,128)(2,1)} custom-call(bf16[8,32,1536]{2,1,0:T(8,128)(2,1)S(1)} %get-tuple-element.35.act_ref, bf16[8,32,384]{2,1,0:T(8,128)(2,1)S(1)} %get-tuple-element.36.pool_ref, f32[128,96]{1,0:T(8,128)S(1)} %bitcast.34, bf16[96,1536]{1,0:T(8,128)(2,1)S(1)} %copy-done.4, bf16[1536,768]{1,0:T(8,128)(2,1)S(1)} %copy-done, ...), custom_call_target="tpu_custom_call" | custom-call | tf_op jit(solution)/shard_map/down_out/pallas_call | solution.py:593
  (10 shorter events, 0.1 us)
Async XLA Ops:
  1.6 10.6 %collective-permute-start = (bf16[16,384]{1,0:T(8,128)(2,1)S(1)}, bf16[16,384]{1,0:T(8,128)(2,1)S(1)}, u32[]{:S(2)}, u32[]{:S(2)}) collective-permute-start(bf16[16,384]{1,0:T(8,128)(2,1)S(1)} %bitcast.40), channel_id=1, source_target_pairs={{0,1},{1,2},{2,3},{3,4},{4,5},{5,6},{6,7},{7,0},{8,9},{9,10},{10,1... | collective-permute-start | bytes 36872 | tf_op jit(solution)/shard_map/ppermute | solution.py:605
  5.4 9.9 %copy-start.7 = (bf16[384,1536]{1,0:T(8,128)(2,1)S(1)}, bf16[384,1536]{1,0:T(8,128)(2,1)}, u32[]{:S(2)}) copy-start(bf16[384,1536]{1,0:T(8,128)(2,1)} %w_ref.5) | copy-start | bytes 3538948
  5.5 9.9 %copy-start.19 = (bf16[9,1536]{1,0:T(8,128)(2,1)S(1)}, bf16[9,1536]{1,0:T(8,128)(2,1)}, u32[]{:S(2)}) copy-start(bf16[9,1536]{1,0:T(8,128)(2,1)} %taps_ref.4) | copy-start | bytes 82948
  5.5 6.8 %collective-permute-start.1 = (bf16[16,384]{1,0:T(8,128)(2,1)S(1)}, bf16[16,384]{1,0:T(8,128)(2,1)S(1)}, u32[]{:S(2)}, u32[]{:S(2)}) collective-permute-start(bf16[16,384]{1,0:T(8,128)(2,1)S(1)} %bitcast.41), channel_id=1, source_target_pairs={{0,7},{1,0},{2,1},{3,2},{4,3},{5,4},{6,5},{7,6},{8,15},{9,8},{10,9... | collective-permute-start | bytes 36872 | tf_op jit(solution)/shard_map/ppermute | solution.py:605
  12.3 10.5 %collective-permute-start.2 = (bf16[80,384]{1,0:T(8,128)(2,1)S(1)}, bf16[80,384]{1,0:T(8,128)(2,1)S(1)}, u32[]{:S(2)}, u32[]{:S(2)}) collective-permute-start(bf16[80,384]{1,0:T(8,128)(2,1)S(1)} %get-tuple-element.28), channel_id=1, source_target_pairs={{0,120},{8,16},{16,8},{24,32},{32,24},{40,48},{48,40},{56,64},{64,... | collective-permute-start | bytes 184328 | tf_op jit(solution)/shard_map/ppermute | solution.py:656
  14.4 8.4 %collective-permute-start.3 = (bf16[80,384]{1,0:T(8,128)(2,1)S(1)}, bf16[80,384]{1,0:T(8,128)(2,1)S(1)}, u32[]{:S(2)}, u32[]{:S(2)}) collective-permute-start(bf16[80,384]{1,0:T(8,128)(2,1)S(1)} %get-tuple-element.29), channel_id=1, source_target_pairs={{0,8},{8,0},{1,9},{9,1},{2,10},{10,2},{3,11},{11,3},{4,12},{12,4},... | collective-permute-start | bytes 184328 | tf_op jit(solution)/shard_map/ppermute | solution.py:657
  15.4 7.4 %copy-start.15 = (bf16[1536,96]{0,1:T(8,128)(2,1)S(1)}, bf16[1536,96]{0,1:T(8,128)(2,1)}, u32[]{:S(2)}) copy-start(bf16[1536,96]{0,1:T(8,128)(2,1)} %param.23) | copy-start | bytes 884740
  22.8 19.5 %copy-start.6 = (bf16[16,64,384]{2,1,0:T(8,128)(2,1)S(1)}, bf16[16,64,384]{2,1,0:T(8,128)(2,1)}, u32[]{:S(2)}) copy-start(bf16[16,64,384]{2,1,0:T(8,128)(2,1)} %img_ref.1) | copy-start | bytes 2359300
  22.9 19.5 %copy-start.8 = (bf16[1536,384]{1,0:T(8,128)(2,1)S(1)}, bf16[1536,384]{1,0:T(8,128)(2,1)}, u32[]{:S(2)}) copy-start(bf16[1536,384]{1,0:T(8,128)(2,1)} %project_ref.2) | copy-start | bytes 3538948
  22.9 19.5 %copy-start.9 = (bf16[384,1536]{1,0:T(8,128)(2,1)S(1)}, bf16[384,1536]{1,0:T(8,128)(2,1)}, u32[]{:S(2)}) copy-start(bf16[384,1536]{1,0:T(8,128)(2,1)} %up_ref.2) | copy-start | bytes 3538948
  22.9 19.5 %copy-start.10 = (bf16[1536,384]{1,0:T(8,128)(2,1)S(1)}, bf16[1536,384]{1,0:T(8,128)(2,1)}, u32[]{:S(2)}) copy-start(bf16[1536,384]{1,0:T(8,128)(2,1)} %down_ref.2) | copy-start | bytes 3538948
  22.9 19.5 %copy-start.13 = (bf16[384,1152]{1,0:T(8,128)(2,1)S(1)}, bf16[384,1152]{1,0:T(8,128)(2,1)}, u32[]{:S(2)}) copy-start(bf16[384,1152]{1,0:T(8,128)(2,1)} %qkv_ref.2) | copy-start | bytes 2654212
  22.9 19.5 %copy-start.16 = (bf16[96,1536]{1,0:T(8,128)(2,1)S(1)}, bf16[96,1536]{1,0:T(8,128)(2,1)}, u32[]{:S(2)}) copy-start(bf16[96,1536]{1,0:T(8,128)(2,1)} %restore_ref.2) | copy-start | bytes 884740
  22.9 19.5 %copy-start.17 = (bf16[384,384]{1,0:T(8,128)(2,1)S(1)}, bf16[384,384]{1,0:T(8,128)(2,1)}, u32[]{:S(2)}) copy-start(bf16[384,384]{1,0:T(8,128)(2,1)} %out_ref.2) | copy-start | bytes 884740
  42.4 28.7 %copy-start.12 = (bf16[1536,384]{1,0:T(8,128)(2,1)S(1)}, bf16[1536,384]{1,0:T(8,128)(2,1)}, u32[]{:S(2)}) copy-start(bf16[1536,384]{1,0:T(8,128)(2,1)} %down_ref.3) | copy-start | bytes 3538948
  42.4 28.7 %copy-start.14 = (bf16[384,1152]{1,0:T(8,128)(2,1)S(1)}, bf16[384,1152]{1,0:T(8,128)(2,1)}, u32[]{:S(2)}) copy-start(bf16[384,1152]{1,0:T(8,128)(2,1)} %qkv_ref.3) | copy-start | bytes 2654212
  53.0 18.1 %copy-start.11 = (bf16[384,1536]{1,0:T(8,128)(2,1)S(1)}, bf16[384,1536]{1,0:T(8,128)(2,1)}, u32[]{:S(2)}) copy-start(bf16[384,1536]{1,0:T(8,128)(2,1)} %up_ref.3) | copy-start | bytes 3538948
  53.0 18.1 %copy-start.18 = (bf16[384,384]{1,0:T(8,128)(2,1)S(1)}, bf16[384,384]{1,0:T(8,128)(2,1)}, u32[]{:S(2)}) copy-start(bf16[384,384]{1,0:T(8,128)(2,1)} %out_ref.3) | copy-start | bytes 884740
  80.3 25.5 %copy-start.1 = (bf16[384,1536]{1,0:T(8,128)(2,1)S(1)}, bf16[384,1536]{1,0:T(8,128)(2,1)}, u32[]{:S(2)}) copy-start(bf16[384,1536]{1,0:T(8,128)(2,1)} %w_ref.7) | copy-start | bytes 3538948
  98.9 11.5 %collective-permute-start.4 = (bf16[64,384]{1,0:T(8,128)(2,1)S(1)}, bf16[64,384]{1,0:T(8,128)(2,1)S(1)}, u32[]{:S(2)}, u32[]{:S(2)}) collective-permute-start(bf16[64,384]{1,0:T(8,128)(2,1)S(1)} %bitcast.39), channel_id=1, source_target_pairs={{0,8},{8,16},{16,24},{24,32},{32,40},{40,48},{48,56},{56,64},{64,7... | collective-permute-start | bytes 147464 | tf_op jit(solution)/shard_map/ppermute | solution.py:605
  102.6 7.9 %copy-start.3 = (bf16[1536,96]{0,1:T(8,128)(2,1)S(1)}, bf16[1536,96]{0,1:T(8,128)(2,1)}, u32[]{:S(2)}) copy-start(bf16[1536,96]{0,1:T(8,128)(2,1)} %param.36) | copy-start | bytes 884740
  102.6 7.9 %copy-start.5 = (bf16[9,1536]{1,0:T(8,128)(2,1)S(1)}, bf16[9,1536]{1,0:T(8,128)(2,1)}, u32[]{:S(2)}) copy-start(bf16[9,1536]{1,0:T(8,128)(2,1)} %taps_ref.5) | copy-start | bytes 82948
  102.6 7.8 %collective-permute-start.5 = (bf16[16,384]{1,0:T(8,128)(2,1)S(1)}, bf16[16,384]{1,0:T(8,128)(2,1)S(1)}, u32[]{:S(2)}, u32[]{:S(2)}) collective-permute-start(bf16[16,384]{1,0:T(8,128)(2,1)S(1)} %bitcast.42), channel_id=1, source_target_pairs={{0,1},{1,2},{2,3},{3,4},{4,5},{5,6},{6,7},{7,0},{8,9},{9,10},{10,1... | collective-permute-start | bytes 36872 | tf_op jit(solution)/shard_map/ppermute | solution.py:605
  103.8 6.6 %collective-permute-start.6 = (bf16[1,384]{1,0:T(2,128)(2,1)S(1)}, bf16[1,384]{1,0:T(2,128)(2,1)S(1)}, u32[]{:S(2)}, u32[]{:S(2)}) collective-permute-start(bf16[1,384]{1,0:T(2,128)(2,1)S(1)} %slice_bitcast_fusion), channel_id=1, source_target_pairs={{0,9},{1,10},{2,11},{3,12},{4,13},{5,14},{6,15},{7,8},{8,17},{9,18... | collective-permute-start | bytes 2312 | tf_op jit(solution)/shard_map/ppermute | solution.py:615
  110.5 19.0 %copy-start = (bf16[1536,768]{1,0:T(8,128)(2,1)S(1)}, bf16[1536,768]{1,0:T(8,128)(2,1)}, u32[]{:S(2)}) copy-start(bf16[1536,768]{1,0:T(8,128)(2,1)} %project_ref.3) | copy-start | bytes 7077892
  110.5 19.0 %copy-start.2 = (bf16[384,768]{1,0:T(8,128)(2,1)S(1)}, bf16[384,768]{1,0:T(8,128)(2,1)}, u32[]{:S(2)}) copy-start(bf16[384,768]{1,0:T(8,128)(2,1)} %short_ref.1) | copy-start | bytes 1769476
  110.5 19.0 %copy-start.4 = (bf16[96,1536]{1,0:T(8,128)(2,1)S(1)}, bf16[96,1536]{1,0:T(8,128)(2,1)}, u32[]{:S(2)}) copy-start(bf16[96,1536]{1,0:T(8,128)(2,1)} %restore_ref.3) | copy-start | bytes 884740

commit v8 on v7

--- a/solution.py
+++ b/solution.py
@@ -505,7 +505,7 @@
     normed[0:32, :] = take_strided(cells, 0, 32, 2).astype(BF16)
     normed[32:64, :] = take_strided(cells, 1, 32, 2).astype(BF16)
     normed[64:80, :] = (half_norm(left_ref[...].astype(F32)) * has_left).astype(BF16)
-    corner = half_norm(corner_ref[...].astype(F32)) * (has_upper * has_left)
+    corner = half_norm(corner_ref[corner_ref.shape[0] - 16 :].astype(F32)[15:16]) * (has_upper * has_left)
     normed[80:96, :] = jnp.broadcast_to(corner, (16, corner.shape[1])).astype(BF16)
     rim_of(normed, w_ref[:, :chunk], rim, 0)
     place = lax.broadcasted_iota(jnp.int32, (8, 128), 0)
@@ -702,7 +702,7 @@
 
     upper = shift(section[rows - 1], ROWS, 1)
     left = shift(section[:, cols - 1], COLS, 1)
-    corner = shift_both(section[rows - 1, cols - 1 :])
+    corner = shift_both(section[rows - 2 :].reshape(2 * cols, channels))
     hidden, pooled = down_expand_part(section, down_expand)
     act, part, whole = down_conv(
         hidden, section, upper, left, corner, down_expand, down_taps, down_reduce.T,

time: 132 us -> 132 us (level)
    ppermute x4, starting transfers between devices: 12.3 us -> 9.68 us  [shift(): return lax.ppermute(x, axes, [(i, (i + by) % size) for i in range(size)])]
    ppermute x1, starting transfers between devices: 1.99 us -> 4.52 us  [shift_both(): return lax.ppermute(x, AXES, pairs)]
    ppermute x1, waiting for transfers between devices: 1.9 us -> 0.01 us  [shift_both(): return lax.ppermute(x, AXES, pairs)]
    ppermute x4, waiting for transfers between devices: 0.01 us -> 1.44 us  [shift(): return lax.ppermute(x, axes, [(i, (i + by) % size) for i in range(size)])]
where the time goes in v8:
time: 132 us
  blocking collectives  70.2 us (53%)
  Pallas kernels  40.5 us (31%)
  starting transfers between devices  17.3 us (13%)
  waiting for transfers between devices  1.45 us (1%)
    all_to_all x2, blocking collectives, exchange(): lax.all_to_all(pieces, CLASS, split_axis=0, concat_axis=0, tiled=True)  36.6 us
    all_to_all x2, blocking collectives, sum_parts(): arrived = lax.all_to_all(part, ALL, split_axis=0, concat_axis=0, tiled=True)  33.6 us
    pallas_call x6, Pallas kernels, resident(): pl.pallas_call(kernel, in_specs=[here] * len(args), out_specs=[here] * le...  32.4 us
    ppermute x4, starting transfers between devices, shift(): return lax.ppermute(x, axes, [(i, (i + by) % size) for i in range(size)])  9.68 us
    ppermute x1, starting transfers between devices, shift_both(): return lax.ppermute(x, AXES, pairs)  4.52 us
    pallas_call x1, Pallas kernels, expand_upper(): pl.pallas_call(kernel, in_specs=[away, away], out_specs=[here] * 6, out_s...  3.21 us
    pallas_call x1, Pallas kernels, down_conv(): pl.pallas_call(functools.partial(down_conv_kernel, chunk=chunk), in_specs...  3.06 us
  transfers between devices with their start and end apart: 7, of which 1 were waited for; matrix products, arithmetic and copies ran while one was open for 0% of the time, Pallas kernels for 10%

profile of v8, /device:TPU:1, one launch (start us, length us, event | category | flops | bytes accessed | tf_op | source)
XLA Modules:
  0.0 131.5 jit_solution(1492186513820033528)
XLA Ops:
  0.6 1.0 fusion
  1.6 3.8 %collective-permute-start = (bf16[16,384]{1,0:T(8,128)(2,1)S(1)}, bf16[16,384]{1,0:T(8,128)(2,1)S(1)}, u32[]{:S(2)}, u32[]{:S(2)}) collective-permute-start(bf16[16,384]{1,0:T(8,128)(2,1)S(1)} %bitcast.39), channel_id=1, source_target_pairs={{0,1},{1,2},{2,3},{3,4},{4,5},{5,6},{6,7},{7,0},{8,9},{9,10},{10,1... | collective-permute-start | bytes 36872 | tf_op jit(solution)/shard_map/ppermute | solution.py:605
  5.5 3.6 %collective-permute-start.1 = (bf16[16,384]{1,0:T(8,128)(2,1)S(1)}, bf16[16,384]{1,0:T(8,128)(2,1)S(1)}, u32[]{:S(2)}, u32[]{:S(2)}) collective-permute-start(bf16[16,384]{1,0:T(8,128)(2,1)S(1)} %bitcast.40), channel_id=1, source_target_pairs={{0,7},{1,0},{2,1},{3,2},{4,3},{5,4},{6,5},{7,6},{8,15},{9,8},{10,9... | collective-permute-start | bytes 36872 | tf_op jit(solution)/shard_map/ppermute | solution.py:605
  9.0 3.2 %expand_upper.1 = (bf16[8,64,1536]{2,1,0:T(8,128)(2,1)S(1)}, bf16[2,64,1536]{2,1,0:T(8,128)(2,1)S(1)}, bf16[64,384]{1,0:T(8,128)(2,1)S(1)}, bf16[64,384]{1,0:T(8...) custom-call(bf16[16,64,384]{2,1,0:T(8,128)(2,1)} %img_ref.1, bf16[384,1536]{1,0:T(8,128)(2,1)} %w_ref.5), custom_call_target="tpu_custom_call" | custom-call | flops 2000000000 | bytes 1048576 | tf_op jit(solution)/shard_map/expand_upper/pallas_call | solution.py:143
  12.3 0.0 collective-permute-done.left_ref
  12.3 0.0 collective-permute-done.1.right_ref
  12.3 2.1 %collective-permute-start.2 = (bf16[80,384]{1,0:T(8,128)(2,1)S(1)}, bf16[80,384]{1,0:T(8,128)(2,1)S(1)}, u32[]{:S(2)}, u32[]{:S(2)}) collective-permute-start(bf16[80,384]{1,0:T(8,128)(2,1)S(1)} %get-tuple-element.28), channel_id=1, source_target_pairs={{0,120},{8,16},{16,8},{24,32},{32,24},{40,48},{48,40},{56,64},{64,... | collective-permute-start | bytes 184328 | tf_op jit(solution)/shard_map/ppermute | solution.py:656
  14.4 0.9 collective-permute-start.3
  15.4 0.0 copy-done.7
  15.4 0.0 copy-done.19
  15.4 7.4 %conv_inner.1 = (bf16[16,64,1536]{2,1,0:T(8,128)(2,1)S(1)}, f32[8,1536]{1,0:T(8,128)S(1)}, bf16[2,64,1536]{2,1,0:T(8,128)(2,1)S(1)}) custom-call(bf16[8,64,1536]{2,1,0:T(8,128)(2,1)S(1)} %get-tuple-element.20.up_ref, bf16[512,384]{1,0:T(8,128)(2,1)S(1)} %get-tuple-element.21.x_ref, bf16[8,64,256]{2,1,0:T(8,128)(2,1)S(1)} %get-tuple-element.22.start_ref, ...), custom_call_target="tpu_custom_call" | custom-call | flops 8000000000 | bytes 1048576 | tf_op jit(solution)/shard_map/conv_inner/pallas_call | solution.py:35
  22.8 0.0 collective-permute-done.2.over_ref
  22.8 0.0 collective-permute-done.3.pair_ref
  22.8 0.0 copy-done.15
  22.8 0.0 copy-start.6
  22.9 0.0 copy-start.8
  22.9 0.0 copy-start.9
  22.9 0.0 copy-start.10
  22.9 0.0 copy-start.13
  22.9 0.0 copy-start.16
  22.9 0.0 copy-start.17
  22.9 2.3 %conv_outer.1 = (bf16[2,64,1536]{2,1,0:T(8,128)(2,1)S(1)}, f32[128,96]{1,0:T(8,128)S(1)}) custom-call(bf16[2,64,1536]{2,1,0:T(8,128)(2,1)S(1)} %get-tuple-element.24.near0_ref, bf16[2,64,1536]{2,1,0:T(8,128)(2,1)S(1)} %get-tuple-element.25.near1_ref, bf16[80,384]{1,0:T(8,128)(2,1)S(1)} %collective-permute-done.2.over_ref, ...), custom_call_target="tpu_custom_call" | custom-call | flops 2000000000 | bytes 1048576 | tf_op jit(solution)/shard_map/conv_outer/pallas_call | solution.py:35
  25.3 17.1 %all_to_all.20 = f32[128,1,96]{2,1,0:T(1,128)S(1)} all-to-all(f32[128,1,96]{2,1,0:T(1,128)S(1)} %bitcast.33), channel_id=1, replica_groups=mesh['row_pair'=8,'core'=2,'depth'=4,'col_pair'=2] {'core','row_pair','c..., dimensions={0} | all-to-all | bytes 98304 | tf_op jit(solution)/shard_map/all_to_all | solution.py:629
  42.4 0.0 copy-done.6
  42.4 0.0 copy-done.8
  42.4 0.0 copy-done.9
  42.4 0.0 copy-done.10
  42.4 0.0 copy-done.13
  42.4 0.0 copy-done.16
  42.4 0.0 copy-done.17
  42.4 0.0 copy-start.12
  42.4 0.0 copy-start.14
  42.4 10.6 %block_part.1 = bf16[1024,384]{1,0:T(8,128)(2,1)S(1)} custom-call(bf16[16,64,384]{2,1,0:T(8,128)(2,1)S(1)} %copy-done.6, bf16[16,64,1536]{2,1,0:T(8,128)(2,1)S(1)} %get-tuple-element.23.act_ref, bf16[2,64,1536]{2,1,0:T(8,128)(2,1)S(1)} %get-tuple-element.31.edge_ref, f32[128,96]{1,0:T(8,128)S(1)} %bitcast.35, bf16[96,1536]{1,0:T(8,128)(2,1)S(1)} %copy-done.16, ...), custom_call_target="tpu_custom_call" | custom-call | flops 12000000000 | bytes 1048576 | tf_op jit(solution)/shard_map/block_part/pallas_call | solution.py:35
  53.0 0.0 copy-start.11
  53.0 0.0 copy-start.18
  53.0 18.0 %all_to_all.21 = bf16[64,16,384]{2,1,0:T(8,128)(2,1)S(1)} all-to-all(bf16[64,16,384]{2,1,0:T(8,128)(2,1)S(1)} %bitcast.28), channel_id=1, replica_groups=mesh['row_pair'=8,'core'=2,'depth'=4,'col_pair'=2] {'row_pair','col_pair..., dimensions={0} | all-to-all | bytes 1572864 | tf_op jit(solution)/shard_map/all_to_all | solution.py:622
  71.1 0.0 copy-done.12
  71.1 0.0 copy-done.14
  71.1 0.0 copy-done.11
  71.1 0.0 copy-done.18
  71.1 9.2 %grid_part.1 = bf16[1024,384]{1,0:T(8,128)(2,1)S(1)} custom-call(bf16[1024,384]{1,0:T(8,128)(2,1)S(1)} %bitcast.29, bf16[384,1152]{1,0:T(8,128)(2,1)S(1)} %copy-done.14, bf16[384,384]{1,0:T(8,128)(2,1)S(1)} %copy-done.18, bf16[384,1536]{1,0:T(8,128)(2,1)S(1)} %copy-done.11, bf16[1536,384]{1,0:T(8,128)(2,1)S(1)} %copy-done.12), custom_call_target="tpu_custom_call" | custom-call | flops 10000000000 | bytes 1048576 | tf_op jit(solution)/shard_map/grid_part/pallas_call | solution.py:35
  80.3 0.0 copy-start.1
  80.4 18.5 %all_to_all.22 = bf16[64,16,384]{2,1,0:T(8,128)(2,1)S(1)} all-to-all(bf16[64,16,384]{2,1,0:T(8,128)(2,1)S(1)} %bitcast.30), channel_id=1, replica_groups=mesh['row_pair'=8,'core'=2,'depth'=4,'col_pair'=2] {'row_pair','col_pair..., dimensions={0} | all-to-all | bytes 1572864 | tf_op jit(solution)/shard_map/all_to_all | solution.py:622
  98.9 4.5 %collective-permute-start.6 = (bf16[128,384]{1,0:T(8,128)(2,1)S(1)}, bf16[128,384]{1,0:T(8,128)(2,1)S(1)}, u32[]{:S(2)}, u32[]{:S(2)}) collective-permute-start(bf16[128,384]{1,0:T(8,128)(2,1)S(1)} %bitcast.37), channel_id=1, source_target_pairs={{0,9},{1,10},{2,11},{3,12},{4,13},{5,14},{6,15},{7,8},{8,17},{9,18... | collective-permute-start | bytes 294920 | tf_op jit(solution)/shard_map/ppermute | solution.py:615
  103.4 0.0 collective-permute-start.4
  103.5 0.0 copy-start.3
  103.5 0.0 copy-start.5
  103.5 2.3 %collective-permute-start.5 = (bf16[16,384]{1,0:T(8,128)(2,1)S(1)}, bf16[16,384]{1,0:T(8,128)(2,1)S(1)}, u32[]{:S(2)}, u32[]{:S(2)}) collective-permute-start(bf16[16,384]{1,0:T(8,128)(2,1)S(1)} %bitcast.41), channel_id=1, source_target_pairs={{0,1},{1,2},{2,3},{3,4},{4,5},{5,6},{6,7},{7,0},{8,9},{9,10},{10,1... | collective-permute-start | bytes 36872 | tf_op jit(solution)/shard_map/ppermute | solution.py:605
  105.8 0.0 copy-done.1
  105.8 2.8 %down_expand.1 = (bf16[16,2,32,1536]{3,2,1,0:T(8,128)(2,1)S(1)}, bf16[8,32,384]{2,1,0:T(8,128)(2,1)S(1)}) custom-call(bf16[16,64,384]{2,1,0:T(8,128)(2,1)S(1)} %bitcast.26, bf16[384,1536]{1,0:T(8,128)(2,1)S(1)} %copy-done.1), custom_call_target="tpu_custom_call" | custom-call | flops 2415919104 | bytes 1048576 | tf_op jit(solution)/shard_map/down_expand/pallas_call | solution.py:35
  108.6 1.4 %collective-permute-done.5.left_ref = bf16[16,384]{1,0:T(8,128)(2,1)S(1)} collective-permute-done((bf16[16,384]{1,0:T(8,128)(2,1)S(1)}, bf16[16,384]{1,0:T(8,128)(2,1)S(1)}, u32[]{:S(2)}, u32[]{:S(2)}) %collective-permute-start.5) | collective-permute-done | bytes 12320 | tf_op jit(solution)/shard_map/ppermute | solution.py:605
  110.0 0.0 collective-permute-done.4.upper_ref
  110.0 0.0 collective-permute-done.6.corner_ref
  110.0 0.0 copy-done.3
  110.0 0.0 copy-done.5
  110.0 0.0 copy-start
  110.0 0.0 copy-start.2
  110.0 0.0 copy-start.4
  110.1 3.1 %down_conv.1 = (bf16[8,32,1536]{2,1,0:T(8,128)(2,1)S(1)}, f32[128,96]{1,0:T(8,128)S(1)}, bf16[16,64,384]{2,1,0:T(8,128)(2,1)}) custom-call(bf16[16,2,32,1536]{3,2,1,0:T(8,128)(2,1)S(1)} %get-tuple-element.33.hid_ref, bf16[16,64,384]{2,1,0:T(8,128)(2,1)S(1)} %bitcast.27, bf16[64,384]{1,0:T(8,128)(2,1)S(1)} %collective-permute-done.4.upper_ref, ...), custom_call_target="tpu_custom_call" | custom-call | tf_op jit(solution)/shard_map/down_conv/pallas_call | solution.py:555
  113.1 16.5 %all_to_all.23 = f32[128,1,96]{2,1,0:T(1,128)S(1)} all-to-all(f32[128,1,96]{2,1,0:T(1,128)S(1)} %bitcast.34), channel_id=1, replica_groups=mesh['row_pair'=8,'core'=2,'depth'=4,'col_pair'=2] {'core','row_pair','c..., dimensions={0} | all-to-all | bytes 98304 | tf_op jit(solution)/shard_map/all_to_all | solution.py:629
  129.6 0.0 copy-done
  129.6 0.0 copy-done.2
  129.6 0.0 copy-done.4
  129.6 1.9 %down_out.1 = bf16[8,32,768]{2,1,0:T(8,128)(2,1)} custom-call(bf16[8,32,1536]{2,1,0:T(8,128)(2,1)S(1)} %get-tuple-element.35.act_ref, bf16[8,32,384]{2,1,0:T(8,128)(2,1)S(1)} %get-tuple-element.36.pool_ref, f32[128,96]{1,0:T(8,128)S(1)} %bitcast.32, bf16[96,1536]{1,0:T(8,128)(2,1)S(1)} %copy-done.4, bf16[1536,768]{1,0:T(8,128)(2,1)S(1)} %copy-done, ...), custom_call_target="tpu_custom_call" | custom-call | tf_op jit(solution)/shard_map/down_out/pallas_call | solution.py:593
  (10 shorter events, 0.1 us)
Async XLA Ops:
  1.6 10.6 %collective-permute-start = (bf16[16,384]{1,0:T(8,128)(2,1)S(1)}, bf16[16,384]{1,0:T(8,128)(2,1)S(1)}, u32[]{:S(2)}, u32[]{:S(2)}) collective-permute-start(bf16[16,384]{1,0:T(8,128)(2,1)S(1)} %bitcast.39), channel_id=1, source_target_pairs={{0,1},{1,2},{2,3},{3,4},{4,5},{5,6},{6,7},{7,0},{8,9},{9,10},{10,1... | collective-permute-start | bytes 36872 | tf_op jit(solution)/shard_map/ppermute | solution.py:605
  5.4 9.9 %copy-start.7 = (bf16[384,1536]{1,0:T(8,128)(2,1)S(1)}, bf16[384,1536]{1,0:T(8,128)(2,1)}, u32[]{:S(2)}) copy-start(bf16[384,1536]{1,0:T(8,128)(2,1)} %w_ref.5) | copy-start | bytes 3538948
  5.5 9.9 %copy-start.19 = (bf16[9,1536]{1,0:T(8,128)(2,1)S(1)}, bf16[9,1536]{1,0:T(8,128)(2,1)}, u32[]{:S(2)}) copy-start(bf16[9,1536]{1,0:T(8,128)(2,1)} %taps_ref.4) | copy-start | bytes 82948
  5.5 6.8 %collective-permute-start.1 = (bf16[16,384]{1,0:T(8,128)(2,1)S(1)}, bf16[16,384]{1,0:T(8,128)(2,1)S(1)}, u32[]{:S(2)}, u32[]{:S(2)}) collective-permute-start(bf16[16,384]{1,0:T(8,128)(2,1)S(1)} %bitcast.40), channel_id=1, source_target_pairs={{0,7},{1,0},{2,1},{3,2},{4,3},{5,4},{6,5},{7,6},{8,15},{9,8},{10,9... | collective-permute-start | bytes 36872 | tf_op jit(solution)/shard_map/ppermute | solution.py:605
  12.3 10.5 %collective-permute-start.2 = (bf16[80,384]{1,0:T(8,128)(2,1)S(1)}, bf16[80,384]{1,0:T(8,128)(2,1)S(1)}, u32[]{:S(2)}, u32[]{:S(2)}) collective-permute-start(bf16[80,384]{1,0:T(8,128)(2,1)S(1)} %get-tuple-element.28), channel_id=1, source_target_pairs={{0,120},{8,16},{16,8},{24,32},{32,24},{40,48},{48,40},{56,64},{64,... | collective-permute-start | bytes 184328 | tf_op jit(solution)/shard_map/ppermute | solution.py:656
  14.4 8.4 %collective-permute-start.3 = (bf16[80,384]{1,0:T(8,128)(2,1)S(1)}, bf16[80,384]{1,0:T(8,128)(2,1)S(1)}, u32[]{:S(2)}, u32[]{:S(2)}) collective-permute-start(bf16[80,384]{1,0:T(8,128)(2,1)S(1)} %get-tuple-element.29), channel_id=1, source_target_pairs={{0,8},{8,0},{1,9},{9,1},{2,10},{10,2},{3,11},{11,3},{4,12},{12,4},... | collective-permute-start | bytes 184328 | tf_op jit(solution)/shard_map/ppermute | solution.py:657
  15.4 7.4 %copy-start.15 = (bf16[1536,96]{0,1:T(8,128)(2,1)S(1)}, bf16[1536,96]{0,1:T(8,128)(2,1)}, u32[]{:S(2)}) copy-start(bf16[1536,96]{0,1:T(8,128)(2,1)} %param.23) | copy-start | bytes 884740
  22.8 19.5 %copy-start.6 = (bf16[16,64,384]{2,1,0:T(8,128)(2,1)S(1)}, bf16[16,64,384]{2,1,0:T(8,128)(2,1)}, u32[]{:S(2)}) copy-start(bf16[16,64,384]{2,1,0:T(8,128)(2,1)} %img_ref.1) | copy-start | bytes 2359300
  22.9 19.5 %copy-start.8 = (bf16[1536,384]{1,0:T(8,128)(2,1)S(1)}, bf16[1536,384]{1,0:T(8,128)(2,1)}, u32[]{:S(2)}) copy-start(bf16[1536,384]{1,0:T(8,128)(2,1)} %project_ref.2) | copy-start | bytes 3538948
  22.9 19.5 %copy-start.9 = (bf16[384,1536]{1,0:T(8,128)(2,1)S(1)}, bf16[384,1536]{1,0:T(8,128)(2,1)}, u32[]{:S(2)}) copy-start(bf16[384,1536]{1,0:T(8,128)(2,1)} %up_ref.2) | copy-start | bytes 3538948
  22.9 19.5 %copy-start.10 = (bf16[1536,384]{1,0:T(8,128)(2,1)S(1)}, bf16[1536,384]{1,0:T(8,128)(2,1)}, u32[]{:S(2)}) copy-start(bf16[1536,384]{1,0:T(8,128)(2,1)} %down_ref.2) | copy-start | bytes 3538948
  22.9 19.5 %copy-start.13 = (bf16[384,1152]{1,0:T(8,128)(2,1)S(1)}, bf16[384,1152]{1,0:T(8,128)(2,1)}, u32[]{:S(2)}) copy-start(bf16[384,1152]{1,0:T(8,128)(2,1)} %qkv_ref.2) | copy-start | bytes 2654212
  22.9 19.5 %copy-start.16 = (bf16[96,1536]{1,0:T(8,128)(2,1)S(1)}, bf16[96,1536]{1,0:T(8,128)(2,1)}, u32[]{:S(2)}) copy-start(bf16[96,1536]{1,0:T(8,128)(2,1)} %restore_ref.2) | copy-start | bytes 884740
  22.9 19.5 %copy-start.17 = (bf16[384,384]{1,0:T(8,128)(2,1)S(1)}, bf16[384,384]{1,0:T(8,128)(2,1)}, u32[]{:S(2)}) copy-start(bf16[384,384]{1,0:T(8,128)(2,1)} %out_ref.2) | copy-start | bytes 884740
  42.4 28.7 %copy-start.12 = (bf16[1536,384]{1,0:T(8,128)(2,1)S(1)}, bf16[1536,384]{1,0:T(8,128)(2,1)}, u32[]{:S(2)}) copy-start(bf16[1536,384]{1,0:T(8,128)(2,1)} %down_ref.3) | copy-start | bytes 3538948
  42.4 28.7 %copy-start.14 = (bf16[384,1152]{1,0:T(8,128)(2,1)S(1)}, bf16[384,1152]{1,0:T(8,128)(2,1)}, u32[]{:S(2)}) copy-start(bf16[384,1152]{1,0:T(8,128)(2,1)} %qkv_ref.3) | copy-start | bytes 2654212
  53.0 18.1 %copy-start.11 = (bf16[384,1536]{1,0:T(8,128)(2,1)S(1)}, bf16[384,1536]{1,0:T(8,128)(2,1)}, u32[]{:S(2)}) copy-start(bf16[384,1536]{1,0:T(8,128)(2,1)} %up_ref.3) | copy-start | bytes 3538948
  53.0 18.1 %copy-start.18 = (bf16[384,384]{1,0:T(8,128)(2,1)S(1)}, bf16[384,384]{1,0:T(8,128)(2,1)}, u32[]{:S(2)}) copy-start(bf16[384,384]{1,0:T(8,128)(2,1)} %out_ref.3) | copy-start | bytes 884740
  80.3 25.4 %copy-start.1 = (bf16[384,1536]{1,0:T(8,128)(2,1)S(1)}, bf16[384,1536]{1,0:T(8,128)(2,1)}, u32[]{:S(2)}) copy-start(bf16[384,1536]{1,0:T(8,128)(2,1)} %w_ref.7) | copy-start | bytes 3538948
  98.9 11.1 %collective-permute-start.6 = (bf16[128,384]{1,0:T(8,128)(2,1)S(1)}, bf16[128,384]{1,0:T(8,128)(2,1)S(1)}, u32[]{:S(2)}, u32[]{:S(2)}) collective-permute-start(bf16[128,384]{1,0:T(8,128)(2,1)S(1)} %bitcast.37), channel_id=1, source_target_pairs={{0,9},{1,10},{2,11},{3,12},{4,13},{5,14},{6,15},{7,8},{8,17},{9,18... | collective-permute-start | bytes 294920 | tf_op jit(solution)/shard_map/ppermute | solution.py:615
  103.4 6.6 %collective-permute-start.4 = (bf16[64,384]{1,0:T(8,128)(2,1)S(1)}, bf16[64,384]{1,0:T(8,128)(2,1)S(1)}, u32[]{:S(2)}, u32[]{:S(2)}) collective-permute-start(bf16[64,384]{1,0:T(8,128)(2,1)S(1)} %bitcast.38), channel_id=1, source_target_pairs={{0,8},{8,16},{16,24},{24,32},{32,40},{40,48},{48,56},{56,64},{64,7... | collective-permute-start | bytes 147464 | tf_op jit(solution)/shard_map/ppermute | solution.py:605
  103.5 6.5 %copy-start.3 = (bf16[1536,96]{0,1:T(8,128)(2,1)S(1)}, bf16[1536,96]{0,1:T(8,128)(2,1)}, u32[]{:S(2)}) copy-start(bf16[1536,96]{0,1:T(8,128)(2,1)} %param.36) | copy-start | bytes 884740
  103.5 6.5 %copy-start.5 = (bf16[9,1536]{1,0:T(8,128)(2,1)S(1)}, bf16[9,1536]{1,0:T(8,128)(2,1)}, u32[]{:S(2)}) copy-start(bf16[9,1536]{1,0:T(8,128)(2,1)} %taps_ref.5) | copy-start | bytes 82948
  103.5 6.5 %collective-permute-start.5 = (bf16[16,384]{1,0:T(8,128)(2,1)S(1)}, bf16[16,384]{1,0:T(8,128)(2,1)S(1)}, u32[]{:S(2)}, u32[]{:S(2)}) collective-permute-start(bf16[16,384]{1,0:T(8,128)(2,1)S(1)} %bitcast.41), channel_id=1, source_target_pairs={{0,1},{1,2},{2,3},{3,4},{4,5},{5,6},{6,7},{7,0},{8,9},{9,10},{10,1... | collective-permute-start | bytes 36872 | tf_op jit(solution)/shard_map/ppermute | solution.py:605
  110.0 19.6 %copy-start = (bf16[1536,768]{1,0:T(8,128)(2,1)S(1)}, bf16[1536,768]{1,0:T(8,128)(2,1)}, u32[]{:S(2)}) copy-start(bf16[1536,768]{1,0:T(8,128)(2,1)} %project_ref.3) | copy-start | bytes 7077892
  110.0 19.6 %copy-start.2 = (bf16[384,768]{1,0:T(8,128)(2,1)S(1)}, bf16[384,768]{1,0:T(8,128)(2,1)}, u32[]{:S(2)}) copy-start(bf16[384,768]{1,0:T(8,128)(2,1)} %short_ref.1) | copy-start | bytes 1769476
  110.0 19.6 %copy-start.4 = (bf16[96,1536]{1,0:T(8,128)(2,1)S(1)}, bf16[96,1536]{1,0:T(8,128)(2,1)}, u32[]{:S(2)}) copy-start(bf16[96,1536]{1,0:T(8,128)(2,1)} %restore_ref.3) | copy-start | bytes 884740
